TPU v7x, 32 devices: a whole 2x2x4 slice. The times are simulated.
32 devices in a mesh: dp: 8 (over z, core), expert: 4 (over y, x).
Axes of the slice: x: 2, y: 2, z: 4, core: 2. Of those that a mesh axis runs over, the one named last changes fastest.
Arguments:
- ssm_state: bfloat16 [256, 16, 4096], P('expert', None, 'dp'), may hold values from -6 to 6
- conv_state: bfloat16 [256, 3, 4096], P('expert', None, 'dp'), may hold values from -6 to 6
- new_slot: int32 [256], replicated, may hold values from 0 to 255, as said below
- conv_input: bfloat16 [256, 4096], P('expert', 'dp'), may hold values from -6 to 6
- gate_input: bfloat16 [256, 4096], P('expert', 'dp'), may hold values from -6 to 6
- conv_weight: float32 [4, 4096], P(None, 'dp'), may hold values from -3 to 3
- conv_bias: float32 [4096], P('dp'), may hold values from -3 to 3
- x_proj_weight: bfloat16 [4096, 288], P('dp'), may hold values from -0.09375 to 0.09375
- step_weight: bfloat16 [256, 4096], P(None, 'dp'), may hold values from -0.375 to 0.375
- step_bias: float32 [4096], P('dp'), may hold values from -3 to -0.5
- decay_log: float32 [16, 4096], P(None, 'dp'), may hold values from 0 to 2
- skip_gain: float32 [4096], P('dp'), may hold values from 0.5 to 1.5
- out_proj_weight: bfloat16 [4096, 4096], P('dp', 'expert'), may hold values from -0.09375 to 0.09375
- residual: bfloat16 [256, 4096], P(None, 'expert'), may hold values from -6 to 6
- norm_gain: float32 [4096], replicated, may hold values from 0.1 to 1.9
- routes: int32 [256, 2], replicated, may hold values from 0 to 3, all different within a row; in each aligned block of 64 rows (0 to 63, 64 to 127, ...) at most 64 rows name the same one
- gate_weight: float32 [256, 2], replicated, may hold values from 0.1 to 0.9
- expert_gate: bfloat16 [4, 4096, 7168], P('expert', None, 'dp'), may hold values from -0.09375 to 0.09375
- expert_up: bfloat16 [4, 4096, 7168], P('expert', None, 'dp'), may hold values from -0.09375 to 0.09375
- expert_down: bfloat16 [4, 7168, 4096], P('expert', 'dp'), may hold values from -0.0625 to 0.0625
Outputs:
- ssm_new: bfloat16 [256, 16, 4096], P('expert', None, 'dp')
- conv_new: bfloat16 [256, 3, 4096], P('expert', None, 'dp')
- layer_out: bfloat16 [256, 4096], P(None, 'expert')
Inputs may be any that keep to these rules, and one draw needn't show every extreme that they name: new_slot is a permutation of the 256 slots; slot s belongs to expert index s // 64. Of the 64 old slots of one expert index, at most 32 get new slots of any one expert index, and exactly 32 those of some expert index; every expert index sends the same multiset of such counts. `routes`: each row names 2 different experts; within each aligned block of 64 rows (the rows of one expert index) no expert is named by more than 64 rows, a bound that some block reaches.
All inputs are finite; a program needn't handle non-finite values.
Results may differ from a plain program's by a relative error of at most 0.012.
Values may be sent and summed in bfloat16 or wider, within the bound.
No kernel may reach another device: no remote copies, remote signals or barrier semaphores. Data moves between devices by JAX's collectives and lax.ppermute only.
A program may use at most 128 MiB of HBM per device.

v0:
```python
import jax
import jax.numpy as jnp
from jax import lax
from jax.sharding import PartitionSpec as P


def dp_total(values):
    return lax.psum(values, "dp")


def body(
    ssm_state,
    conv_state,
    new_slot,
    conv_input,
    gate_input,
    conv_weight,
    conv_bias,
    x_proj_weight,
    step_weight,
    step_bias,
    decay_log,
    skip_gain,
    out_proj_weight,
    residual,
    norm_gain,
    routes,
    gate_weight,
    expert_gate,
    expert_up,
    expert_down,
):
    row_count, state_dim, channels = ssm_state.shape
    owners = lax.axis_size("expert")
    own_index = lax.axis_index("expert")
    move_cap = 2 * row_count // owners
    slot_count = owners * move_cap
    my_slots = lax.dynamic_slice_in_dim(new_slot, own_index * row_count, row_count)
    target = my_slots // row_count
    target_hot = (target[:, None] == jnp.arange(owners)[None, :]).astype(jnp.int32)
    earlier = jnp.sum((jnp.cumsum(target_hot, axis=0) - target_hot) * target_hot, axis=1)
    send_slot = target * move_cap + earlier
    send_hot = (jnp.arange(slot_count)[:, None] == send_slot[None, :]).astype(jnp.bfloat16)
    packed_ssm = (
        jnp.dot(send_hot, ssm_state.reshape(row_count, -1), preferred_element_type=jnp.float32)
        .astype(jnp.bfloat16)
        .reshape(owners, move_cap, -1)
    )
    packed_conv = (
        jnp.dot(send_hot, conv_state.reshape(row_count, -1), preferred_element_type=jnp.float32)
        .astype(jnp.bfloat16)
        .reshape(owners, move_cap, -1)
    )
    recv_ssm, recv_conv = (
        lax.all_to_all(packed_ssm, "expert", split_axis=0, concat_axis=0, tiled=True),
        lax.all_to_all(packed_conv, "expert", split_axis=0, concat_axis=0, tiled=True),
    )
    arriving = (new_slot // row_count == own_index).astype(jnp.int32).reshape(owners, row_count)
    arrive_rank = (jnp.cumsum(arriving, axis=1) - arriving).reshape(-1)
    source_ids = jnp.arange(owners * row_count) // row_count
    recv_slot = source_ids * move_cap + arrive_rank
    new_place = new_slot % row_count
    place_rows = (
        (new_place[None, :] == jnp.arange(row_count)[:, None])
        & (arriving.reshape(-1)[None, :] == 1)
    ).astype(jnp.bfloat16)
    place_slots = (recv_slot[:, None] == jnp.arange(slot_count)[None, :]).astype(jnp.bfloat16)
    place_hot = jnp.dot(place_rows, place_slots, preferred_element_type=jnp.float32).astype(
        jnp.bfloat16
    )
    moved_ssm = (
        jnp.dot(place_hot, recv_ssm.reshape(slot_count, -1), preferred_element_type=jnp.float32)
        .astype(jnp.bfloat16)
        .reshape(row_count, state_dim, channels)
    )
    moved_conv = (
        jnp.dot(place_hot, recv_conv.reshape(slot_count, -1), preferred_element_type=jnp.float32)
        .astype(jnp.bfloat16)
        .reshape(row_count, -1, channels)
    )
    window = jnp.concatenate([moved_conv, conv_input[:, None, :]], axis=1)
    conv_new = window[:, 1:, :]
    conv_sum = (
        jnp.sum(window.astype(jnp.float32) * conv_weight[None, :, :], axis=1) + conv_bias[None, :]
    )
    activated = jax.nn.silu(conv_sum).astype(jnp.bfloat16)
    projected = dp_total(jnp.dot(activated, x_proj_weight, preferred_element_type=jnp.float32))
    rank_dim = step_weight.shape[0]
    step_low = projected[:, :rank_dim]
    b_coef = projected[:, rank_dim : rank_dim + state_dim]
    c_coef = projected[:, rank_dim + state_dim :]
    step_norm = (
        step_low * lax.rsqrt(jnp.mean(step_low * step_low, axis=1, keepdims=True) + 1e-06)
    ).astype(jnp.bfloat16)
    step_size = jax.nn.softplus(
        jnp.dot(step_norm, step_weight, preferred_element_type=jnp.float32) + step_bias[None, :]
    )
    act_float = activated.astype(jnp.float32)
    decays = jnp.exp(step_size[:, None, :] * (-jnp.exp(decay_log))[None, :, :])
    states = (
        decays * moved_ssm.astype(jnp.float32)
        + (step_size * act_float)[:, None, :] * b_coef[:, :, None]
    )
    ssm_new = states.astype(jnp.bfloat16)
    gated_out = (
        (jnp.sum(c_coef[:, :, None] * states, axis=1) + skip_gain[None, :] * act_float)
        * jax.nn.silu(gate_input.astype(jnp.float32))
    ).astype(jnp.bfloat16)
    mamba_mix = dp_total(
        jnp.dot(
            lax.all_gather(gated_out, "expert", axis=0, tiled=True),
            out_proj_weight,
            preferred_element_type=jnp.float32,
        )
    )
    stream = (residual.astype(jnp.float32) + mamba_mix).astype(jnp.bfloat16)
    top_count = routes.shape[1]
    width = stream.shape[1]
    capacity = min(row_count, 5 * row_count * top_count // (2 * owners))
    expert_hot = (
        (routes[:, :, None] == jnp.arange(owners)[None, None, :])
        .astype(jnp.int32)
        .reshape(owners, row_count * top_count, owners)
    )
    prior = jnp.sum((jnp.cumsum(expert_hot, axis=1) - expert_hot) * expert_hot, axis=2)
    slot_of = (routes.reshape(owners, row_count * top_count) * capacity + prior).reshape(
        owners, row_count, top_count
    )
    matches = slot_of[:, :, :, None] == jnp.arange(owners * capacity)[None, None, None, :]
    dispatch_hot = (
        jnp.any(matches, axis=2).astype(jnp.bfloat16).reshape(owners, row_count, owners, capacity)
    )
    combine_w = jnp.sum(
        jnp.where(matches, gate_weight.reshape(owners, row_count, top_count)[:, :, :, None], 0.0),
        axis=2,
    ).reshape(owners, row_count, owners, capacity)
    outgoing = jnp.einsum(
        "orec,ord->eocd",
        dispatch_hot,
        stream.reshape(owners, row_count, width),
        preferred_element_type=jnp.float32,
    ).astype(jnp.bfloat16)
    arrived = lax.all_to_all(outgoing, "expert", split_axis=0, concat_axis=3, tiled=True)
    tokens = arrived.reshape(owners * capacity, -1).astype(jnp.float32)
    normed = (
        tokens
        * lax.rsqrt(jnp.mean(tokens * tokens, axis=1, keepdims=True) + 1e-05)
        * norm_gain[None, :]
    ).astype(jnp.bfloat16)
    gate_val = jnp.dot(normed, expert_gate[0], preferred_element_type=jnp.float32)
    up_val = jnp.dot(normed, expert_up[0], preferred_element_type=jnp.float32)
    hidden = (jax.nn.silu(gate_val) * up_val).astype(jnp.bfloat16)
    partial_out = jnp.dot(hidden, expert_down[0], preferred_element_type=jnp.float32).reshape(
        owners, capacity, -1
    )
    summed = dp_total(partial_out)
    returned = lax.all_to_all(
        summed.astype(jnp.bfloat16), "expert", split_axis=2, concat_axis=0, tiled=True
    ).astype(summed.dtype)
    expert_mix = jnp.einsum(
        "orec,eocd->ord",
        combine_w,
        returned.reshape(owners, owners, capacity, width),
        precision=lax.Precision.HIGHEST,
        preferred_element_type=jnp.float32,
    )
    layer_out = (stream.astype(jnp.float32) + expert_mix.reshape(-1, width)).astype(jnp.bfloat16)
    return (ssm_new, conv_new, layer_out)


def solution(mesh):
    in_specs = (
        P("expert", None, "dp"),
        P("expert", None, "dp"),
        P(),
        P("expert", "dp"),
        P("expert", "dp"),
        P(None, "dp"),
        P("dp"),
        P("dp", None),
        P(None, "dp"),
        P("dp"),
        P(None, "dp"),
        P("dp"),
        P("dp", "expert"),
        P(None, "expert"),
        P(),
        P(),
        P(),
        P("expert", None, "dp"),
        P("expert", None, "dp"),
        P("expert", "dp", None),
    )
    out_specs = (P("expert", None, "dp"), P("expert", None, "dp"), P(None, "expert"))
    return jax.shard_map(body, mesh=mesh, in_specs=in_specs, out_specs=out_specs, check_vma=False)
```

profile of v0, /device:TPU:0, one launch (start us, length us, event | category | flops | bytes accessed | tf_op | source)
XLA Modules:
  0.0 355.5 jit_solution(2429530057049202176)
XLA Ops:
  7.2 0.9 and_select_fusion
  8.5 0.8 multiply_add_fusion
  9.2 0.9 copy.90
  10.2 1.0 convolution_convert_fusion.2
  11.2 5.2 %all-to-all-start = ((bf16[4,32,1536]{2,1,0:T(8,128)(2,1)}), bf16[4,32,1536]{2,1,0:T(8,128)(2,1)S(1)}, u32[]{:S(2)}, u32[]{:S(2)}) async-start(bf16[4,32,1536]{2,1,0:T(8,128)(2,1)} %bitcast), calls=%async_computation | async-start | bytes 786432 | tf_op jit(solution)/shard_map/all_to_all | solution.py:56
  16.3 0.7 broadcast_compare_fusion
  17.4 0.7 and_select_fusion.3
  18.8 0.8 copy.72
  19.7 2.0 convolution_convert_fusion
  21.8 1.2 all-to-all-done
  23.0 3.6 %all-to-all-start.1 = ((bf16[4,32,8192]{2,1,0:T(8,128)(2,1)}), bf16[4,32,8192]{2,1,0:T(8,128)(2,1)S(1)}, u32[]{:S(2)}, u32[]{:S(2)}) async-start(bf16[4,32,8192]{2,1,0:T(8,128)(2,1)} %bitcast.3), calls=%async_computation.1 | async-start | bytes 4194304 | tf_op jit(solution)/shard_map/all_to_all | solution.py:55
  26.6 0.9 convolution_convert_fusion.3
  27.5 1.1 reshape.137
  28.6 1.5 multiply_reduce_fusion.1
  30.0 1.8 fusion.43
  31.9 1.4 exponential_negate_fusion
  33.3 52.1 %all-reduce.4.cloned.1.call-done = f32[64,288]{1,0:T(8,128)} async-done(((f32[64,288]{1,0:T(8,128)}), f32[64,288]{1,0:T(8,128)}) %all-reduce.4.cloned.1.call-update) | async-done | bytes 73744 | tf_op jit(solution)/shard_map/psum | solution.py:8
  85.4 0.9 multiply_reduce_fusion.2
  86.3 1.5 fusion.44
  87.9 1.9 convert_multiply_fusion.4
  90.3 1.2 copy.92
  91.6 1.9 multiply_reduce_fusion
  93.6 9.0 %all_gather.3 = bf16[256,512]{1,0:T(8,128)(2,1)S(1)} all-gather(bf16[64,512]{1,0:T(8,128)(2,1)S(1)} %fusion.28), channel_id=1, replica_groups=mesh['dp'=8,'expert'=4] {'expert'}, dimensions={0}, use_global_device_ids=true | all-gather | bytes 327680 | tf_op jit(solution)/shard_map/all_gather | solution.py:111
  102.6 1.5 fusion.45
  105.5 58.5 %all-reduce.6.cloned.1.call-done = f32[256,1024]{1,0:T(8,128)} async-done(((f32[256,1024]{1,0:T(8,128)}), f32[256,1024]{1,0:T(8,128)}) %all-reduce.6.cloned.1.call-update) | async-done | bytes 1048592 | tf_op jit(solution)/shard_map/psum | solution.py:8
  164.0 1.4 add_convert_fusion
  165.4 0.7 fusion.46
  166.5 1.6 copy.79
  168.1 3.9 %all-to-all-start.2 = ((bf16[4,4,64,1024]{3,2,1,0:T(8,128)(2,1)}), bf16[4,4,64,1024]{3,2,1,0:T(8,128)(2,1)S(1)}, u32[]{:S(2)}, u32[]{:S(2)}) async-start(bf16[4,4,64,1024]{3,2,1,0:T(8,128)(2,1)} %copy.79), calls=%async_computation.2 | async-start | bytes 4194304 | tf_op jit(solution)/shard_map/all_to_all | solution.py:143
  172.1 23.1 %all-to-all-done.2 = bf16[4,4,64,1024]{3,2,1,0:T(8,128)(2,1)S(1)} async-done(((bf16[4,4,64,1024]{3,2,1,0:T(8,128)(2,1)}), bf16[4,4,64,1024]{3,2,1,0:T(8,128)(2,1)S(1)}, u32[]{:S(2)}, u32[]{:S(2)}) %all-to-all-start.2) | async-done | bytes 2097184 | tf_op jit(solution)/shard_map/all_to_all | solution.py:143
  195.7 0.7 fusion.10
  196.4 1.6 copy.80
  198.1 0.9 copy.93
  199.0 2.3 fusion.5
  201.4 1.2 slice-done.5
  202.5 2.3 fusion.18
  204.9 4.4 %fusion.1 = f32[4,64,4096]{2,1,0:T(8,128)} fusion(bf16[4,64,896]{2,1,0:T(8,128)(2,1)S(1)} %bitcast.97, bf16[1,896,4096]{2,1,0:T(8,128)(2,1)S(1)} %bitcast.86), kind=kOutput, calls=%fused_computation.3 | convolution fusion | flops 1879048192 | bytes 11993088 | tf_op jit(solution)/shard_map/dot_general | solution.py:153
  209.3 88.6 %all-reduce.7 = bf16[4,64,4096]{2,1,0:T(8,128)(2,1)S(1)} all-reduce(f32[4,64,4096]{2,1,0:T(8,128)} %fusion.1), channel_id=1, replica_groups=mesh['dp'=8,'expert'=4] {'dp'}, use_global_device_ids=true, to_apply=%region_13.14 | all-reduce | flops 1048576 | bytes 6291456 | tf_op jit(solution)/shard_map/psum | solution.py:8
  297.9 4.7 %copy.81 = bf16[4,64,4096]{1,0,2:T(4,128)(2,1)} copy(bf16[4,64,4096]{2,1,0:T(8,128)(2,1)S(1)} %all-reduce.7) | data formatting | bytes 4194304 | tf_op jit(solution)/shard_map/convert_element_type | solution.py:158
  302.6 5.9 %reshape.151 = bf16[4,2,131072]{2,1,0:T(2,128)(2,1)} reshape(bf16[4096,4,64]{2,1,0:T(4,128)(2,1)} %bitcast.83) | data formatting | bytes 4194304
  308.5 4.0 %all-to-all-start.3 = ((bf16[4,2,131072]{2,1,0:T(2,128)(2,1)}), bf16[4,2,131072]{2,1,0:T(2,128)(2,1)S(1)}, u32[]{:S(2)}, u32[]{:S(2)}) async-start(bf16[4,2,131072]{2,1,0:T(2,128)(2,1)} %reshape.151), calls=%async_computation.3 | async-start | bytes 4194304 | tf_op jit(solution)/shard_map/all_to_all | solution.py:157
  312.8 1.0 reshape.141
  314.2 0.7 copy.85
  314.9 20.8 %all-to-all-done.3 = bf16[4,2,131072]{2,1,0:T(2,128)(2,1)S(1)} async-done(((bf16[4,2,131072]{2,1,0:T(2,128)(2,1)}), bf16[4,2,131072]{2,1,0:T(2,128)(2,1)S(1)}, u32[]{:S(2)}, u32[]{:S(2)}) %all-to-all-start.3) | async-done | bytes 2097184 | tf_op jit(solution)/shard_map/all_to_all | solution.py:157
  335.6 4.0 %reshape.152 = bf16[4096,4,64]{2,1,0:T(4,128)(2,1)} reshape(bf16[4,2,131072]{2,1,0:T(2,128)(2,1)S(1)} %all-to-all-done.3) | data formatting | bytes 4194304
  339.6 5.6 %copy.83 = bf16[4,64,4,1024]{3,1,2,0:T(8,128)(2,1)S(1)} copy(bf16[4,64,4,1024]{1,0,3,2:T(4,128)(2,1)} %bitcast.84) | data formatting | bytes 4194304 | tf_op jit(solution)/shard_map/all_to_all | solution.py:157
  345.3 2.4 fusion.12
  347.7 0.9 fusion.21
  (88 shorter events, 5.3 us)
Async XLA Ops:
  7.2 95.4 %copy-start = (bf16[512,1024]{1,0:T(8,128)(2,1)S(1)}, bf16[512,1024]{1,0:T(8,128)(2,1)}, u32[]{:S(2)}) copy-start(bf16[512,1024]{1,0:T(8,128)(2,1)} %param.32) | copy-start | bytes 3145732
  7.2 11.0 %copy-start.5 = (bf16[64,16,512]{2,1,0:T(8,128)(2,1)S(1)}, bf16[64,16,512]{2,1,0:T(8,128)(2,1)}, u32[]{:S(2)}) copy-start(bf16[64,16,512]{2,1,0:T(8,128)(2,1)} %param.20) | copy-start | bytes 3145732
  7.2 11.6 %copy-start.12 = (bf16[64,512]{1,0:T(8,128)(2,1)S(1)}, bf16[64,512]{1,0:T(8,128)(2,1)}, u32[]{:S(2)}) copy-start(bf16[64,512]{1,0:T(8,128)(2,1)} %param.23) | copy-start | bytes 196612
  11.2 11.8 %all-to-all-start = ((bf16[4,32,1536]{2,1,0:T(8,128)(2,1)}), bf16[4,32,1536]{2,1,0:T(8,128)(2,1)S(1)}, u32[]{:S(2)}, u32[]{:S(2)}) async-start(bf16[4,32,1536]{2,1,0:T(8,128)(2,1)} %bitcast), calls=%async_computation | async-start | bytes 786432 | tf_op jit(solution)/shard_map/all_to_all | solution.py:56
  23.0 66.9 %all-to-all-start.1 = ((bf16[4,32,8192]{2,1,0:T(8,128)(2,1)}), bf16[4,32,8192]{2,1,0:T(8,128)(2,1)S(1)}, u32[]{:S(2)}, u32[]{:S(2)}) async-start(bf16[4,32,8192]{2,1,0:T(8,128)(2,1)} %bitcast.3), calls=%async_computation.1 | async-start | bytes 4194304 | tf_op jit(solution)/shard_map/all_to_all | solution.py:55
  26.6 58.8 %all-reduce.4.cloned.1.call-start = ((), (), s32[]{:S(2)}) async-start(), calls=%async_computation.4 | async-start | bytes 196608 | tf_op jit(solution)/shard_map/psum | solution.py:8
  31.9 132.1 %all-reduce.6.cloned.1.call-start = ((), (), s32[]{:S(2)}) async-start(), calls=%async_computation.5 | async-start | bytes 2097152 | tf_op jit(solution)/shard_map/psum | solution.py:8
  90.2 1.3 copy-start.7
  90.3 1.3 copy-start.8
  90.3 1.3 copy-start.9
  90.3 1.3 copy-start.10
  90.3 1.3 copy-start.11
  91.5 2.0 copy-start.13
  91.5 2.0 copy-start.16
  91.5 2.0 copy-start.17
  93.5 10.6 %copy-start.15 = (s32[256,2]{0,1:T(2,128)S(1)}, s32[256,2]{0,1:T(2,128)}, u32[]{:S(2)}) copy-start(s32[256,2]{0,1:T(2,128)} %param.35) | copy-start | bytes 6148
  102.6 61.4 %copy-start.6 = (bf16[256,1024]{1,0:T(8,128)(2,1)S(1)}, bf16[256,1024]{1,0:T(8,128)(2,1)}, u32[]{:S(2)}) copy-start(bf16[256,1024]{1,0:T(8,128)(2,1)} %param.33) | copy-start | bytes 1572868
  165.4 0.8 copy-start.2
  168.1 3.9 %copy-start.14 = (f32[4096]{0:T(1024)S(1)}, f32[4096]{0:T(1024)}, u32[]{:S(2)}) copy-start(f32[4096]{0:T(1024)} %param.34) | copy-start | bytes 49156
  168.1 27.0 %all-to-all-start.2 = ((bf16[4,4,64,1024]{3,2,1,0:T(8,128)(2,1)}), bf16[4,4,64,1024]{3,2,1,0:T(8,128)(2,1)S(1)}, u32[]{:S(2)}, u32[]{:S(2)}) async-start(bf16[4,4,64,1024]{3,2,1,0:T(8,128)(2,1)} %copy.79), calls=%async_computation.2 | async-start | bytes 4194304 | tf_op jit(solution)/shard_map/all_to_all | solution.py:143
  195.1 3.8 %slice-start.2 = ((s8[7340032]{0:T(1024)(128)(4,1)}), s8[4194304]{0:T(1024)(128)(4,1)S(1)}, s32[]{:S(2)}) async-start(s8[7340032]{0:T(1024)(128)(4,1)} %bitcast.101), calls=%async_computation.8 | async-start | bytes 8388608
  196.4 2.6 slice-start.3
  198.0 3.3 slice-start.4
  198.1 6.8 %slice-start = ((s8[7340032]{0:T(1024)(128)(4,1)}), s8[4194304]{0:T(1024)(128)(4,1)S(1)}, s32[]{:S(2)}) async-start(s8[7340032]{0:T(1024)(128)(4,1)} %bitcast.85), calls=%async_computation.6 | async-start | bytes 8388608
  199.0 3.5 slice-start.5
  199.0 5.9 %slice-start.1 = ((s8[7340032]{0:T(1024)(128)(4,1)}), s8[3145728]{0:T(1024)(128)(4,1)S(1)}, s32[]{:S(2)}) async-start(s8[7340032]{0:T(1024)(128)(4,1)} %bitcast.85), calls=%async_computation.7 | async-start | bytes 6291456
  308.5 4.0 %copy-start.18 = (f32[256,2]{0,1:T(2,128)S(1)}, f32[256,2]{0,1:T(2,128)}, u32[]{:S(2)}) copy-start(f32[256,2]{0,1:T(2,128)} %param.36) | copy-start | bytes 6148
  308.5 5.3 %copy-start.4 = (bf16[64,1,512]{2,1,0:T(2,128)(2,1)S(1)}, bf16[64,1,512]{2,1,0:T(2,128)(2,1)}, u32[]{:S(2)}) copy-start(bf16[64,1,512]{2,1,0:T(2,128)(2,1)} %copy.72) | copy-start | bytes 196612
  308.5 27.1 %all-to-all-start.3 = ((bf16[4,2,131072]{2,1,0:T(2,128)(2,1)}), bf16[4,2,131072]{2,1,0:T(2,128)(2,1)S(1)}, u32[]{:S(2)}, u32[]{:S(2)}) async-start(bf16[4,2,131072]{2,1,0:T(2,128)(2,1)} %reshape.151), calls=%async_computation.3 | async-start | bytes 4194304 | tf_op jit(solution)/shard_map/all_to_all | solution.py:157
  345.2 2.5 copy-start.3
  345.2 3.4 copy-start.1
Sparse Core Ops, SparseCore 0:
  32.0 53.3 all-reduce.3
  104.2 59.7 all-reduce.5
where the time goes:
time: 357 us; the launch traced here: 355 us
  waiting for transfers between devices  156 us (44%)
  blocking collectives  97.6 us (27%)
  local copies, waits for them, and re-layouts  34.3 us (10%)
  matrix products  22 us (6%)
  starting transfers between devices  16.7 us (5%)
  other arithmetic  14.7 us (4%)
  between operations  14.6 us (4%)
    psum x2, waiting for transfers between devices, dp_total(): return lax.psum(values, 'dp')  111 us
    psum x1, blocking collectives, dp_total(): return lax.psum(values, 'dp')  88.6 us
    all_to_all x1, waiting for transfers between devices, body(): lax.all_to_all(outgoing, 'expert', split_axis=0, concat_axis=3, tiled=True)  23.1 us
    all_to_all x1, waiting for transfers between devices, body(): lax.all_to_all(summed.astype(jnp.bfloat16), 'expert', split_axis=2, conca...  20.8 us
    unnamed x57, local copies, waits for them, and re-layouts  14.8 us
    all_gather x1, blocking collectives, body(): lax.all_gather(gated_out, 'expert', axis=0, tiled=True)  8.96 us
  transfers between devices with their start and end apart: 6, of which 5 were waited for; matrix products, arithmetic and copies ran while one was open for 6% of the time, Pallas kernels for 0%

commit v1 on v0

v1 whole, which is shorter than its diff:
```python
import jax
import jax.numpy as jnp
from jax import lax
from jax.sharding import PartitionSpec as P

F32 = jnp.float32
BF16 = jnp.bfloat16


def swap(values, axis, flip):
    size = lax.axis_size(axis)
    return lax.ppermute(values, axis, [(i, i ^ flip) for i in range(size)])


def gather_pairs(values, axis, stride=1):
    count = lax.axis_size(axis) // stride
    return [values] + [swap(values, axis, flip * stride) for flip in range(1, count)]


def scatter_pairs(parts, axis, stride=1):
    total = parts[0].astype(F32)
    for flip in range(1, len(parts)):
        total = total + swap(parts[flip].astype(BF16), axis, flip * stride).astype(F32)
    return total


def dispatch_experts(stream, norm_gain, routes, gate_weight, expert_gate, expert_up, expert_down, row_count, capacity):
    owners = lax.axis_size("expert")
    top_count = routes.shape[1]
    width = stream.shape[1]
    expert_hot = (
        (routes[:, :, None] == jnp.arange(owners)[None, None, :])
        .astype(jnp.int32)
        .reshape(owners, row_count * top_count, owners)
    )
    prior = jnp.sum((jnp.cumsum(expert_hot, axis=1) - expert_hot) * expert_hot, axis=2)
    slot_of = (routes.reshape(owners, row_count * top_count) * capacity + prior).reshape(owners, row_count, top_count)
    matches = slot_of[:, :, :, None] == jnp.arange(owners * capacity)[None, None, None, :]
    dispatch_hot = jnp.any(matches, axis=2).astype(BF16).reshape(owners, row_count, owners, capacity)
    combine_w = jnp.sum(
        jnp.where(matches, gate_weight.reshape(owners, row_count, top_count)[:, :, :, None], 0.0), axis=2
    ).reshape(owners, row_count, owners, capacity)
    outgoing = jnp.einsum(
        "orec,ord->eocd", dispatch_hot, stream.reshape(owners, row_count, width), preferred_element_type=F32
    ).astype(BF16)
    arrived = lax.all_to_all(outgoing, "expert", split_axis=0, concat_axis=3, tiled=True)
    tokens = arrived.reshape(owners * capacity, -1).astype(F32)
    normed = (
        tokens * lax.rsqrt(jnp.mean(tokens * tokens, axis=1, keepdims=True) + 1e-05) * norm_gain[None, :]
    ).astype(BF16)
    gate_val = jnp.dot(normed, expert_gate, preferred_element_type=F32)
    up_val = jnp.dot(normed, expert_up, preferred_element_type=F32)
    hidden = (jax.nn.silu(gate_val) * up_val).astype(BF16)
    partial_out = jnp.dot(hidden, expert_down, preferred_element_type=F32).reshape(owners, capacity, -1)
    summed = lax.psum(partial_out, "dp")
    returned = lax.all_to_all(summed.astype(BF16), "expert", split_axis=2, concat_axis=0, tiled=True).astype(F32)
    expert_mix = jnp.einsum(
        "orec,eocd->ord",
        combine_w,
        returned.reshape(owners, owners, capacity, width),
        precision=lax.Precision.HIGHEST,
        preferred_element_type=F32,
    )
    return (stream.astype(F32) + expert_mix.reshape(-1, width)).astype(BF16)


def body(
    ssm_state,
    conv_state,
    new_slot,
    conv_input,
    gate_input,
    conv_weight,
    conv_bias,
    x_proj_weight,
    step_weight,
    step_bias,
    decay_log,
    skip_gain,
    out_proj_weight,
    residual,
    norm_gain,
    routes,
    gate_weight,
    expert_gate,
    expert_up,
    expert_down,
):
    row_count, state_dim, channels = ssm_state.shape
    owners = lax.axis_size("expert")
    own = lax.axis_index("expert")
    dp_index = lax.axis_index("dp")
    core = dp_index % 2
    plane = dp_index // 2
    planes = lax.axis_size("dp") // 2
    rows = owners * row_count
    half = rows // 2
    chunk = half // planes
    tap_count = conv_weight.shape[0]

    conv_all = jnp.concatenate(gather_pairs(conv_input, "expert"), axis=0)
    tied_gate, conv_all = lax.optimization_barrier((gate_input, conv_all))
    gate_all = jnp.concatenate(gather_pairs(tied_gate, "expert"), axis=0)
    my_slots = lax.dynamic_slice_in_dim(new_slot, own * row_count, row_count)
    near_ids = (
        (jnp.arange(owners) ^ own)[:, None] * row_count + jnp.arange(row_count)[None, :]
    ).reshape(-1)
    pick = (my_slots[:, None] == near_ids[None, :]).astype(BF16)
    conv_in = jnp.dot(pick, conv_all, preferred_element_type=F32)

    conv_sum = (
        jnp.sum(conv_state.astype(F32) * conv_weight[None, : tap_count - 1, :], axis=1)
        + conv_in * conv_weight[tap_count - 1][None, :]
        + conv_bias[None, :]
    )
    activated = jax.nn.silu(conv_sum).astype(BF16)
    projected = jnp.dot(activated, x_proj_weight, preferred_element_type=F32)
    projected = projected + swap(projected, "dp", 1)
    projected = scatter_pairs([projected] * planes, "dp", 2)
    rank_dim = step_weight.shape[0]
    step_low = projected[:, :rank_dim]
    b_coef = projected[:, rank_dim : rank_dim + state_dim]
    c_coef = projected[:, rank_dim + state_dim :]
    step_norm = (
        step_low * lax.rsqrt(jnp.mean(step_low * step_low, axis=1, keepdims=True) + 1e-06)
    ).astype(BF16)
    step_size = jax.nn.softplus(
        jnp.dot(step_norm, step_weight, preferred_element_type=F32) + step_bias[None, :]
    )
    act_float = activated.astype(F32)
    decays = jnp.exp(step_size[:, None, :] * (-jnp.exp(decay_log))[None, :, :])
    states = decays * ssm_state.astype(F32) + (step_size * act_float)[:, None, :] * b_coef[:, :, None]
    gate_in = jnp.dot(pick, gate_all, preferred_element_type=F32)
    gated_out = (
        (jnp.sum(c_coef[:, :, None] * states, axis=1) + skip_gain[None, :] * act_float) * jax.nn.silu(gate_in)
    ).astype(BF16)
    ssm_old = states.astype(BF16)

    gated_all = jnp.concatenate(gather_pairs(gated_out, "expert"), axis=0)
    old_slots = new_slot.reshape(owners, row_count)
    near_slots = jnp.concatenate(
        [lax.dynamic_slice_in_dim(old_slots, own ^ flip, 1, axis=0) for flip in range(owners)], axis=0
    ).reshape(-1)
    order_hot = (jnp.arange(rows)[:, None] == near_slots[None, :]).astype(BF16)
    gated_new = jnp.dot(order_hot, gated_all, preferred_element_type=F32).astype(BF16)
    mix = jnp.dot(gated_new, out_proj_weight, preferred_element_type=F32)

    width = mix.shape[1]
    mix = mix.reshape(2, planes, chunk, width)
    kept = lax.dynamic_index_in_dim(mix, core, 0, keepdims=False)
    sent = lax.dynamic_index_in_dim(mix, 1 - core, 0, keepdims=False)
    mix_half = kept + swap(sent.astype(BF16), "dp", 1).astype(F32)
    mix_chunk = scatter_pairs(
        [lax.dynamic_index_in_dim(mix_half, plane ^ flip, 0, keepdims=False) for flip in range(planes)], "dp", 2
    )
    residual_chunk = lax.dynamic_slice_in_dim(residual, core * half + plane * chunk, chunk, axis=0)
    stream_chunk = (residual_chunk.astype(F32) + mix_chunk).astype(BF16)
    stream_half = jnp.concatenate(gather_pairs(stream_chunk, "dp", 2), axis=0)

    def in_order(near_half):
        stacked = near_half.reshape(planes, chunk, width)
        own_half = jnp.concatenate(
            [lax.dynamic_index_in_dim(stacked, plane ^ p, 0, keepdims=False) for p in range(planes)], axis=0
        )
        other = swap(own_half, "dp", 1)
        lower = jnp.where(core == 0, own_half, other)
        upper = jnp.where(core == 0, other, own_half)
        return jnp.concatenate([lower, upper], axis=0)

    move_cap = 2 * row_count // owners
    target = my_slots // row_count
    target_hot = (target[:, None] == jnp.arange(owners)[None, :]).astype(jnp.int32)
    earlier = jnp.sum((jnp.cumsum(target_hot, axis=0) - target_hot) * target_hot, axis=1)
    send_slot = (target ^ own) * move_cap + earlier
    slot_count = owners * move_cap
    send_hot = (jnp.arange(slot_count)[:, None] == send_slot[None, :]).astype(BF16)
    moving = jnp.concatenate([ssm_old, conv_state[:, 1:, :]], axis=1).reshape(row_count, -1)
    packed = (
        jnp.dot(send_hot, moving, preferred_element_type=F32).astype(BF16).reshape(owners, move_cap, -1)
    )
    arrived = jnp.concatenate(
        [packed[0]] + [swap(packed[flip], "expert", flip) for flip in range(1, owners)], axis=0
    )
    arriving = (new_slot // row_count == own).astype(jnp.int32).reshape(owners, row_count)
    arrive_rank = (jnp.cumsum(arriving, axis=1) - arriving).reshape(-1)
    source_ids = jnp.arange(rows) // row_count
    recv_slot = (source_ids ^ own) * move_cap + arrive_rank
    place_rows = (
        (new_slot[None, :] == (own * row_count + jnp.arange(row_count))[:, None])
    ).astype(BF16)
    place_slots = (recv_slot[:, None] == jnp.arange(slot_count)[None, :]).astype(BF16)
    place_hot = jnp.dot(place_rows, place_slots, preferred_element_type=F32).astype(BF16)
    moved = (
        jnp.dot(place_hot, arrived, preferred_element_type=F32)
        .astype(BF16)
        .reshape(row_count, state_dim + tap_count - 2, channels)
    )
    ssm_new = moved[:, :state_dim]
    conv_new = jnp.concatenate([moved[:, state_dim:], conv_input[:, None, :]], axis=1)

    capacity = min(row_count, 5 * row_count * routes.shape[1] // (2 * owners))
    if capacity < row_count:
        layer_out = dispatch_experts(
            in_order(stream_half),
            norm_gain,
            routes,
            gate_weight,
            expert_gate[0],
            expert_up[0],
            expert_down[0],
            row_count,
            capacity,
        )
        return (ssm_new, conv_new, layer_out)

    blocks = gather_pairs(stream_half, "expert")
    blocks = [jnp.concatenate([block, swap(block, "dp", 1)], axis=0).astype(F32) for block in blocks]
    square = sum(jnp.sum(block * block, axis=1, keepdims=True) for block in blocks)
    scale = lax.rsqrt(square / (owners * width) + 1e-05)
    gains = norm_gain.reshape(owners, 1, width)
    near_normed = jnp.stack(
        [
            (block * scale * lax.dynamic_index_in_dim(gains, own ^ flip, 0, keepdims=False)).astype(BF16)
            for flip, block in enumerate(blocks)
        ]
    )
    normed = jnp.concatenate(
        [lax.dynamic_index_in_dim(near_normed, own ^ e, 0, keepdims=False) for e in range(owners)], axis=1
    )
    gate_val = jnp.dot(normed, expert_gate[0], preferred_element_type=F32)
    up_val = jnp.dot(normed, expert_up[0], preferred_element_type=F32)
    hidden = (jax.nn.silu(gate_val) * up_val).astype(BF16)
    near_rows = (
        (jnp.arange(2) ^ core)[:, None, None] * half
        + (jnp.arange(planes) ^ plane)[None, :, None] * chunk
        + jnp.arange(chunk)[None, None, :]
    ).reshape(-1)
    row_weight = jnp.sum(jnp.where(routes == own, gate_weight, 0.0), axis=1)
    near_weight = jnp.sum(
        jnp.where(near_rows[:, None] == jnp.arange(rows)[None, :], row_weight[None, :], 0.0), axis=1, keepdims=True
    )
    expert_out = (jnp.dot(hidden, expert_down[0], preferred_element_type=F32) * near_weight).astype(BF16)

    out_half = expert_out[:half].astype(F32) + swap(expert_out[half:], "dp", 1).astype(F32)
    own_columns = scatter_pairs(
        [lax.dynamic_slice_in_dim(out_half, (own ^ flip) * width, width, axis=1) for flip in range(owners)], "expert"
    ).reshape(planes, chunk, width)
    mix_rows = scatter_pairs([own_columns[flip] for flip in range(planes)], "dp", 2)
    layer_chunk = (stream_chunk.astype(F32) + mix_rows).astype(BF16)
    layer_out = in_order(jnp.concatenate(gather_pairs(layer_chunk, "dp", 2), axis=0))
    return (ssm_new, conv_new, layer_out)


def solution(mesh):
    in_specs = (
        P("expert", None, "dp"),
        P("expert", None, "dp"),
        P(),
        P("expert", "dp"),
        P("expert", "dp"),
        P(None, "dp"),
        P("dp"),
        P("dp", None),
        P(None, "dp"),
        P("dp"),
        P(None, "dp"),
        P("dp"),
        P("dp", "expert"),
        P(None, "expert"),
        P(),
        P(),
        P(),
        P("expert", None, "dp"),
        P("expert", None, "dp"),
        P("expert", "dp", None),
    )
    out_specs = (P("expert", None, "dp"), P("expert", None, "dp"), P(None, "expert"))
    return jax.shard_map(body, mesh=mesh, in_specs=in_specs, out_specs=out_specs, check_vma=False)
```

time: 357 us -> 153 us (0.43)
  blocking collectives: 97.6 us -> 0 us
  waiting for transfers between devices: 156 us -> 62.3 us
  starting transfers between devices: 16.7 us -> 45.7 us
  local copies, waits for them, and re-layouts: 34.3 us -> 10.1 us
  between operations: 14.6 us -> 1.27 us
  other arithmetic: 14.7 us -> 11.1 us
    psum x2 -> x0, waiting for transfers between devices: 111 us -> none  [dp_total(): return lax.psum(values, 'dp')]
    psum x1 -> x0, blocking collectives: 88.6 us -> none  [dp_total(): return lax.psum(values, 'dp')]
    ppermute x0 -> x41, waiting for transfers between devices: none -> 62.3 us  [swap(): return lax.ppermute(values, axis, [(i, i ^ flip) for i in range(size)])]
    ppermute x0 -> x41, starting transfers between devices: none -> 45.7 us  [swap(): return lax.ppermute(values, axis, [(i, i ^ flip) for i in range(size)])]
    all_to_all x4 -> x0, waiting for transfers between devices: 45 us -> none  [the longest x1 23.1 us: body(): lax.all_to_all(outgoing, 'expert', split_axis=0, concat_axis=3, tiled=True)]
    all_to_all x4 -> x0, starting transfers between devices: 16.7 us -> none  [the longest x1 5.17 us: body(): lax.all_to_all(packed_conv, 'expert', split_axis=0, concat_axis=0, tiled=...]
    unnamed x57 -> x39, local copies, waits for them, and re-layouts: 14.8 us -> 2.9 us
    all_gather x1 -> x0, blocking collectives: 8.96 us -> none  [body(): lax.all_gather(gated_out, 'expert', axis=0, tiled=True)]
  transfers between devices with their start and end apart: 6 -> 41, of which waited for: 5 -> 23; matrix products, arithmetic and copies ran while one was open for 6% -> 11% of each run, Pallas kernels for 0% -> 0%
where the time goes in v1:
time: 153 us; the launch traced here: 152 us
  waiting for transfers between devices  62.3 us (41%)
  starting transfers between devices  45.7 us (30%)
  matrix products  21.9 us (14%)
  other arithmetic  11.1 us (7%)
  local copies, waits for them, and re-layouts  10.1 us (7%)
    ppermute x41, waiting for transfers between devices, swap(): return lax.ppermute(values, axis, [(i, i ^ flip) for i in range(size)])  62.3 us
    ppermute x41, starting transfers between devices, swap(): return lax.ppermute(values, axis, [(i, i ^ flip) for i in range(size)])  45.7 us
    dot_general x1, matrix products, body(): jnp.dot(hidden, expert_down[0], preferred_element_type=F32) * near_weight  11.6 us
    dot_general x1, matrix products, body(): gate_val = jnp.dot(normed, expert_gate[0], preferred_element_type=F32)  3.26 us
    dot_general x1, matrix products, body(): jnp.dot(place_hot, arrived, preferred_element_type=F32).astype(BF16)  3.14 us
  transfers between devices with their start and end apart: 41, of which 23 were waited for; matrix products, arithmetic and copies ran while one was open for 11% of the time, Pallas kernels for 0%

profile of v1, /device:TPU:0, one launch (start us, length us, event | category | flops | bytes accessed | tf_op | source)
XLA Modules:
  0.0 152.4 jit_solution(14617528707173445792)
XLA Ops:
  0.7 3.0 %collective-permute-start = (bf16[64,512]{1,0:T(8,128)(2,1)}, bf16[64,512]{1,0:T(8,128)(2,1)S(1)}, u32[]{:S(2)}, u32[]{:S(2)}) collective-permute-start(bf16[64,512]{1,0:T(8,128)(2,1)} %param.23), channel_id=1, source_target_pairs={{0,1},{1,0},{2,3},{3,2},{4,5},{5,4},{6,7},{7,6},{8,9},{9,8},{10,11... | collective-permute-start | bytes 196616 | tf_op jit(solution)/shard_map/ppermute | solution.py:12
  3.7 1.5 collective-permute-start.1
  8.7 1.9 %collective-permute-done.2 = bf16[64,512]{1,0:T(8,128)(2,1)S(1)} collective-permute-done((bf16[64,512]{1,0:T(8,128)(2,1)}, bf16[64,512]{1,0:T(8,128)(2,1)S(1)}, u32[]{:S(2)}, u32[]{:S(2)}) %collective-permute-start.2) | collective-permute-done | bytes 65568 | tf_op jit(solution)/shard_map/ppermute | solution.py:12
  12.4 1.2 fusion.108
  13.8 1.1 collective-permute-done.3
  15.0 1.6 %collective-permute-start.4 = (bf16[64,288]{1,0:T(8,128)(2,1)S(1)}, bf16[64,288]{1,0:T(8,128)(2,1)S(1)}, u32[]{:S(2)}, u32[]{:S(2)}) collective-permute-start(bf16[64,288]{1,0:T(8,128)(2,1)S(1)} %get-tuple-element.22), channel_id=1, source_target_pairs={{0,8},{4,12},{8,0},{12,4},{16,24},{20,28},{24,16},{28,20},{1,9},{5... | collective-permute-start | bytes 110600 | tf_op jit(solution)/shard_map/ppermute | solution.py:12
  16.6 2.6 %collective-permute-start.5 = (bf16[64,288]{1,0:T(8,128)(2,1)S(1)}, bf16[64,288]{1,0:T(8,128)(2,1)S(1)}, u32[]{:S(2)}, u32[]{:S(2)}) collective-permute-start(bf16[64,288]{1,0:T(8,128)(2,1)S(1)} %get-tuple-element.22), channel_id=1, source_target_pairs={{0,16},{4,20},{8,24},{12,28},{16,0},{20,4},{24,8},{28,12},{1,17},{... | collective-permute-start | bytes 110600 | tf_op jit(solution)/shard_map/ppermute | solution.py:12
  20.0 1.1 collective-permute-start.11
  21.1 1.9 %collective-permute-start.12 = (bf16[64,512]{1,0:T(8,128)(2,1)S(1)}, bf16[64,512]{1,0:T(8,128)(2,1)S(1)}, u32[]{:S(2)}, u32[]{:S(2)}) collective-permute-start(bf16[64,512]{1,0:T(8,128)(2,1)S(1)} %copy-done.11), channel_id=1, source_target_pairs={{0,3},{1,2},{2,1},{3,0},{4,7},{5,6},{6,5},{7,4},{8,11},{9,10},{10,... | collective-permute-start | bytes 196616 | tf_op jit(solution)/shard_map/ppermute | solution.py:12
  23.0 2.1 %collective-permute-done.6 = bf16[64,288]{1,0:T(8,128)(2,1)S(1)} collective-permute-done((bf16[64,288]{1,0:T(8,128)(2,1)S(1)}, bf16[64,288]{1,0:T(8,128)(2,1)S(1)}, u32[]{:S(2)}, u32[]{:S(2)}) %collective-permute-start.6) | collective-permute-done | bytes 36896 | tf_op jit(solution)/shard_map/ppermute | solution.py:12
  27.6 1.5 collective-permute-start.14
  29.1 1.5 collective-permute-start.15
  31.8 2.4 %collective-permute-done.15 = bf16[64,512]{1,0:T(8,128)(2,1)S(1)} collective-permute-done((bf16[64,512]{1,0:T(8,128)(2,1)S(1)}, bf16[64,512]{1,0:T(8,128)(2,1)S(1)}, u32[]{:S(2)}, u32[]{:S(2)}) %collective-permute-start.15) | collective-permute-done | bytes 65568 | tf_op jit(solution)/shard_map/ppermute | solution.py:12
  35.3 1.2 collective-permute-done.16
  37.3 3.5 %collective-permute-start.18 = (bf16[32,1024]{1,0:T(8,128)(2,1)S(1)}, bf16[32,1024]{1,0:T(8,128)(2,1)S(1)}, u32[]{:S(2)}, u32[]{:S(2)}) collective-permute-start(bf16[32,1024]{1,0:T(8,128)(2,1)S(1)} %get-tuple-element.41), channel_id=1, source_target_pairs={{0,16},{4,20},{8,24},{12,28},{16,0},{20,4},{24,8},{28,12},{1,17},{... | collective-permute-start | bytes 196616 | tf_op jit(solution)/shard_map/ppermute | solution.py:12
  41.0 3.8 %collective-permute-done.18 = bf16[32,1024]{1,0:T(8,128)(2,1)S(1)} collective-permute-done((bf16[32,1024]{1,0:T(8,128)(2,1)S(1)}, bf16[32,1024]{1,0:T(8,128)(2,1)S(1)}, u32[]{:S(2)}, u32[]{:S(2)}) %collective-permute-start.18) | collective-permute-done | bytes 65568 | tf_op jit(solution)/shard_map/ppermute | solution.py:12
  44.8 2.1 %collective-permute-done.19 = bf16[32,1024]{1,0:T(8,128)(2,1)S(1)} collective-permute-done((bf16[32,1024]{1,0:T(8,128)(2,1)S(1)}, bf16[32,1024]{1,0:T(8,128)(2,1)S(1)}, u32[]{:S(2)}, u32[]{:S(2)}) %collective-permute-start.19) | collective-permute-done | bytes 65568 | tf_op jit(solution)/shard_map/ppermute | solution.py:12
  48.6 1.7 %collective-permute-start.21 = (bf16[32,1024]{1,0:T(8,128)(2,1)S(1)}, bf16[32,1024]{1,0:T(8,128)(2,1)S(1)}, u32[]{:S(2)}, u32[]{:S(2)}) collective-permute-start(bf16[32,1024]{1,0:T(8,128)(2,1)S(1)} %get-tuple-element.19), channel_id=1, source_target_pairs={{0,16},{4,20},{8,24},{12,28},{16,0},{20,4},{24,8},{28,12},{1,17},{... | collective-permute-start | bytes 196616 | tf_op jit(solution)/shard_map/ppermute | solution.py:12
  50.4 1.9 %collective-permute-start.22 = (bf16[32,1024]{1,0:T(8,128)(2,1)S(1)}, bf16[32,1024]{1,0:T(8,128)(2,1)S(1)}, u32[]{:S(2)}, u32[]{:S(2)}) collective-permute-start(bf16[32,1024]{1,0:T(8,128)(2,1)S(1)} %get-tuple-element.19), channel_id=1, source_target_pairs={{0,24},{4,28},{8,16},{12,20},{16,8},{20,12},{24,0},{28,4},{1,25},{... | collective-permute-start | bytes 196616 | tf_op jit(solution)/shard_map/ppermute | solution.py:12
  52.3 2.8 %collective-permute-done.21 = bf16[32,1024]{1,0:T(8,128)(2,1)S(1)} collective-permute-done((bf16[32,1024]{1,0:T(8,128)(2,1)S(1)}, bf16[32,1024]{1,0:T(8,128)(2,1)S(1)}, u32[]{:S(2)}, u32[]{:S(2)}) %collective-permute-start.21) | collective-permute-done | bytes 65568 | tf_op jit(solution)/shard_map/ppermute | solution.py:12
  55.1 1.4 collective-permute-done.22
  57.1 1.1 collective-permute-start.26
  58.1 1.9 %collective-permute-start.28 = (bf16[128,1024]{1,0:T(8,128)(2,1)S(1)}, bf16[128,1024]{1,0:T(8,128)(2,1)S(1)}, u32[]{:S(2)}, u32[]{:S(2)}) collective-permute-start(bf16[128,1024]{1,0:T(8,128)(2,1)S(1)} %pad_maximum_fusion.9), channel_id=1, source_target_pairs={{0,3},{1,2},{2,1},{3,0},{4,7},{5,6},{6,5},{7,4},{8,11},{9,10},{10,... | collective-permute-start | bytes 786440 | tf_op jit(solution)/shard_map/ppermute | solution.py:12
  60.1 4.3 %collective-permute-done.24 = bf16[128,1024]{1,0:T(8,128)(2,1)S(1)} collective-permute-done((bf16[128,1024]{1,0:T(8,128)(2,1)S(1)}, bf16[128,1024]{1,0:T(8,128)(2,1)S(1)}, u32[]{:S(2)}, u32[]{:S(2)}) %collective-permute-start.24) | collective-permute-done | bytes 262176 | tf_op jit(solution)/shard_map/ppermute | solution.py:12
  64.6 6.8 %collective-permute-done.26 = bf16[128,1024]{1,0:T(8,128)(2,1)S(1)} collective-permute-done((bf16[128,1024]{1,0:T(8,128)(2,1)S(1)}, bf16[128,1024]{1,0:T(8,128)(2,1)S(1)}, u32[]{:S(2)}, u32[]{:S(2)}) %collective-permute-start.26) | collective-permute-done | bytes 262176 | tf_op jit(solution)/shard_map/ppermute | solution.py:12
  75.1 1.2 slice-done.2
  76.4 3.3 %fusion.4 = f32[256,896]{1,0:T(8,128)} fusion(bf16[1,4096,896]{2,1,0:T(8,128)(2,1)S(1)} %bitcast.110, bf16[256,1024]{1,0:T(8,128)(2,1)S(1)} %get-tuple-element.32, bf16[256,1024]{1,0:T(8,128)(2,1)S(1)} %get-tuple-element.33, bf16[256,1024]{1,0:T(8,128)(2,1)S(1)} %get-tuple-element.34, bf16[256,1024]{1,0:T(8,128)(2,1)S(1)} %get-tuple-element.31), kind=kOutput, calls=%fused_computation.6 | convolution fusion | flops 1887436800 | bytes 10354688 | tf_op jit(solution)/shard_map/dot_general | solution.py:230
  79.6 11.6 %fusion.9 = bf16[256,4096]{1,0:T(8,128)(2,1)} fusion(bf16[1,896,4096]{2,1,0:T(8,128)(2,1)} %param.39, f32[256]{0:T(256)S(1)} %select_reduce_fusion, bf16[1,4096,896]{2,1,0:T(8,128)(2,1)} %param.38, f32[256,896]{1,0:T(8,128)} %fusion.4, bf16[256,1024]{1,0:T(8,128)(2,1)S(1)} %get-tuple-element.32, bf16[256,1024]{1,0:T(8,128)(2,1)S(1)} %get-tuple-element.33, ...), kind=kOutput, calls=%fused_computation.9 | convolution fusion | flops 3769958400 | bytes 19792896 | tf_op jit(solution)/shard_map/dot_general | solution.py:242
  91.2 1.3 slice.93
  95.7 1.6 %collective-permute-start.31 = (bf16[128,1024]{1,0:T(8,128)(2,1)S(1)}, bf16[128,1024]{1,0:T(8,128)(2,1)S(1)}, u32[]{:S(2)}, u32[]{:S(2)}) collective-permute-start(bf16[128,1024]{1,0:T(8,128)(2,1)S(1)} %get-tuple-element.28), channel_id=1, source_target_pairs={{0,1},{1,0},{2,3},{3,2},{4,5},{5,4},{6,7},{7,6},{8,9},{9,8},{10,11... | collective-permute-start | bytes 786440 | tf_op jit(solution)/shard_map/ppermute | solution.py:12
  97.7 1.5 collective-permute-start.33
  100.0 4.9 %collective-permute-done.31 = bf16[128,1024]{1,0:T(8,128)(2,1)S(1)} collective-permute-done((bf16[128,1024]{1,0:T(8,128)(2,1)S(1)}, bf16[128,1024]{1,0:T(8,128)(2,1)S(1)}, u32[]{:S(2)}, u32[]{:S(2)}) %collective-permute-start.31) | collective-permute-done | bytes 262176 | tf_op jit(solution)/shard_map/ppermute | solution.py:12
  104.9 6.3 %collective-permute-done.32 = bf16[128,1024]{1,0:T(8,128)(2,1)S(1)} collective-permute-done((bf16[128,1024]{1,0:T(8,128)(2,1)S(1)}, bf16[128,1024]{1,0:T(8,128)(2,1)S(1)}, u32[]{:S(2)}, u32[]{:S(2)}) %collective-permute-start.32) | collective-permute-done | bytes 262176 | tf_op jit(solution)/shard_map/ppermute | solution.py:12
  111.4 2.5 %collective-permute-start.35 = (bf16[32,1024]{1,0:T(8,128)(2,1)S(1)}, bf16[32,1024]{1,0:T(8,128)(2,1)S(1)}, u32[]{:S(2)}, u32[]{:S(2)}) collective-permute-start(bf16[32,1024]{1,0:T(8,128)(2,1)S(1)} %get-tuple-element.48), channel_id=1, source_target_pairs={{0,16},{4,20},{8,24},{12,28},{16,0},{20,4},{24,8},{28,12},{1,17},{... | collective-permute-start | bytes 196616 | tf_op jit(solution)/shard_map/ppermute | solution.py:12
  113.9 1.8 %collective-permute-start.36 = (bf16[32,1024]{1,0:T(8,128)(2,1)S(1)}, bf16[32,1024]{1,0:T(8,128)(2,1)S(1)}, u32[]{:S(2)}, u32[]{:S(2)}) collective-permute-start(bf16[32,1024]{1,0:T(8,128)(2,1)S(1)} %get-tuple-element.47), channel_id=1, source_target_pairs={{0,24},{4,28},{8,16},{12,20},{16,8},{20,12},{24,0},{28,4},{1,25},{... | collective-permute-start | bytes 196616 | tf_op jit(solution)/shard_map/ppermute | solution.py:12
  117.3 1.2 collective-permute-start.8
  118.5 1.8 %collective-permute-start.9 = (bf16[32,9216]{1,0:T(8,128)(2,1)S(1)}, bf16[32,9216]{1,0:T(8,128)(2,1)}, u32[]{:S(2)}, u32[]{:S(2)}) collective-permute-start(bf16[32,9216]{1,0:T(8,128)(2,1)S(1)} %get-tuple-element.25), channel_id=1, source_target_pairs={{0,3},{1,2},{2,1},{3,0},{4,7},{5,6},{6,5},{7,4},{8,11},{9,10},{10,... | collective-permute-start | bytes 1769480 | tf_op jit(solution)/shard_map/ppermute | solution.py:12
  120.5 2.6 %collective-permute-start.38 = (bf16[32,1024]{1,0:T(8,128)(2,1)S(1)}, bf16[32,1024]{1,0:T(8,128)(2,1)S(1)}, u32[]{:S(2)}, u32[]{:S(2)}) collective-permute-start(bf16[32,1024]{1,0:T(8,128)(2,1)S(1)} %fusion.61), channel_id=1, source_target_pairs={{0,16},{4,20},{8,24},{12,28},{16,0},{20,4},{24,8},{28,12},{1,17},{... | collective-permute-start | bytes 196616 | tf_op jit(solution)/shard_map/ppermute | solution.py:12
  123.1 1.5 collective-permute-done.37
  124.6 2.0 %collective-permute-start.39 = (bf16[32,1024]{1,0:T(8,128)(2,1)S(1)}, bf16[32,1024]{1,0:T(8,128)(2,1)S(1)}, u32[]{:S(2)}, u32[]{:S(2)}) collective-permute-start(bf16[32,1024]{1,0:T(8,128)(2,1)S(1)} %fusion.61), channel_id=1, source_target_pairs={{0,24},{4,28},{8,16},{12,20},{16,8},{20,12},{24,0},{28,4},{1,25},{... | collective-permute-start | bytes 196616 | tf_op jit(solution)/shard_map/ppermute | solution.py:12
  126.6 4.1 %collective-permute-done.39 = bf16[32,1024]{1,0:T(8,128)(2,1)S(1)} collective-permute-done((bf16[32,1024]{1,0:T(8,128)(2,1)S(1)}, bf16[32,1024]{1,0:T(8,128)(2,1)S(1)}, u32[]{:S(2)}, u32[]{:S(2)}) %collective-permute-start.39) | collective-permute-done | bytes 65568 | tf_op jit(solution)/shard_map/ppermute | solution.py:12
  130.9 2.5 %collective-permute-done.7 = bf16[32,9216]{1,0:T(8,128)(2,1)} collective-permute-done((bf16[32,9216]{1,0:T(8,128)(2,1)}, bf16[32,9216]{1,0:T(8,128)(2,1)}, u32[]{:S(2)}, u32[]{:S(2)}) %collective-permute-start.7) | collective-permute-done | bytes 589856 | tf_op jit(solution)/shard_map/ppermute | solution.py:12
  133.3 9.0 %collective-permute-done.8 = bf16[32,9216]{1,0:T(8,128)(2,1)} collective-permute-done((bf16[32,9216]{1,0:T(8,128)(2,1)S(1)}, bf16[32,9216]{1,0:T(8,128)(2,1)}, u32[]{:S(2)}, u32[]{:S(2)}) %collective-permute-start.8) | collective-permute-done | bytes 589856 | tf_op jit(solution)/shard_map/ppermute | solution.py:12
  142.3 1.1 collective-permute-done.9
  143.4 3.1 %convolution_convert_fusion.1 = bf16[64,9216]{1,0:T(8,128)(2,1)} fusion(bf16[32,9216]{1,0:T(8,128)(2,1)} %collective-permute-done.9, bf16[32,9216]{1,0:T(8,128)(2,1)} %collective-permute-done.8, bf16[32,9216]{1,0:T(8,128)(2,1)} %collective-permute-done.7, bf16[32,9216]{1,0:T(8,128)(2,1)S(1)} %get-tuple-element.24, s32[256]{0:T(256)S(1)} %fusion.93, ...), kind=kOutput, calls=%fused_computation.1 | convolution fusion | flops 165273600 | bytes 3541248 | tf_op jit(solution)/shard_map/dot_general | solution.py:194
  146.6 1.7 %reshape.547 = bf16[64,18,512]{2,1,0:T(8,128)(2,1)S(1)} reshape(bf16[64,9216]{1,0:T(8,128)(2,1)} %convolution_convert_fusion.1) | data formatting | bytes 2359296 | tf_op jit(solution)/shard_map/reshape | solution.py:196
  148.3 1.1 slice.89
  150.5 1.1 broadcast_select_fusion.1
  (155 shorter events, 26.7 us)
Async XLA Ops:
  0.6 33.6 %copy-start = (bf16[512,1024]{1,0:T(8,128)(2,1)S(1)}, bf16[512,1024]{1,0:T(8,128)(2,1)}, u32[]{:S(2)}) copy-start(bf16[512,1024]{1,0:T(8,128)(2,1)} %param.32) | copy-start | bytes 3145732
  0.6 13.1 %copy-start.7 = (s32[256]{0:T(256)S(1)}, s32[256]{0:T(256)}, u32[]{:S(2)}) copy-start(s32[256]{0:T(256)} %param.22) | copy-start | bytes 3076
  0.7 18.8 %copy-start.11 = (bf16[64,512]{1,0:T(8,128)(2,1)S(1)}, bf16[64,512]{1,0:T(8,128)(2,1)}, u32[]{:S(2)}) copy-start(bf16[64,512]{1,0:T(8,128)(2,1)} %param.24) | copy-start | bytes 196612
  0.7 24.6 %copy-start.4 = (bf16[256,512]{1,0:T(8,128)(2,1)S(1)}, bf16[256,512]{1,0:T(8,128)(2,1)}, u32[]{:S(2)}) copy-start(bf16[256,512]{1,0:T(8,128)(2,1)} %param.28) | copy-start | bytes 786436
  0.7 24.6 %copy-start.8 = (f32[512]{0:T(512)S(1)}, f32[512]{0:T(512)}, u32[]{:S(2)}) copy-start(f32[512]{0:T(512)} %param.29) | copy-start | bytes 6148
  0.7 24.9 %copy-start.3 = (bf16[64,16,512]{2,1,0:T(8,128)(2,1)S(1)}, bf16[64,16,512]{2,1,0:T(8,128)(2,1)}, u32[]{:S(2)}) copy-start(bf16[64,16,512]{2,1,0:T(8,128)(2,1)} %param.20) | copy-start | bytes 3145732
  0.7 8.0 %collective-permute-start = (bf16[64,512]{1,0:T(8,128)(2,1)}, bf16[64,512]{1,0:T(8,128)(2,1)S(1)}, u32[]{:S(2)}, u32[]{:S(2)}) collective-permute-start(bf16[64,512]{1,0:T(8,128)(2,1)} %param.23), channel_id=1, source_target_pairs={{0,1},{1,0},{2,3},{3,2},{4,5},{5,4},{6,7},{7,6},{8,9},{9,8},{10,11... | collective-permute-start | bytes 196616 | tf_op jit(solution)/shard_map/ppermute | solution.py:12
  3.7 5.0 %collective-permute-start.1 = (bf16[64,512]{1,0:T(8,128)(2,1)}, bf16[64,512]{1,0:T(8,128)(2,1)S(1)}, u32[]{:S(2)}, u32[]{:S(2)}) collective-permute-start(bf16[64,512]{1,0:T(8,128)(2,1)} %param.23), channel_id=1, source_target_pairs={{0,2},{1,3},{2,0},{3,1},{4,6},{5,7},{6,4},{7,5},{8,10},{9,11},{10,... | collective-permute-start | bytes 196616 | tf_op jit(solution)/shard_map/ppermute | solution.py:12
  5.2 5.4 %collective-permute-start.2 = (bf16[64,512]{1,0:T(8,128)(2,1)}, bf16[64,512]{1,0:T(8,128)(2,1)S(1)}, u32[]{:S(2)}, u32[]{:S(2)}) collective-permute-start(bf16[64,512]{1,0:T(8,128)(2,1)} %param.23), channel_id=1, source_target_pairs={{0,3},{1,2},{2,1},{3,0},{4,7},{5,6},{6,5},{7,4},{8,11},{9,10},{10,... | collective-permute-start | bytes 196616 | tf_op jit(solution)/shard_map/ppermute | solution.py:12
  13.6 13.1 %copy-start.12 = (f32[512]{0:T(512)S(1)}, f32[512]{0:T(512)}, u32[]{:S(2)}) copy-start(f32[512]{0:T(512)} %param.31) | copy-start | bytes 6148
  13.6 1.4 collective-permute-start.3
  15.0 6.1 %collective-permute-start.4 = (bf16[64,288]{1,0:T(8,128)(2,1)S(1)}, bf16[64,288]{1,0:T(8,128)(2,1)S(1)}, u32[]{:S(2)}, u32[]{:S(2)}) collective-permute-start(bf16[64,288]{1,0:T(8,128)(2,1)S(1)} %get-tuple-element.22), channel_id=1, source_target_pairs={{0,8},{4,12},{8,0},{12,4},{16,24},{20,28},{24,16},{28,20},{1,9},{5... | collective-permute-start | bytes 110600 | tf_op jit(solution)/shard_map/ppermute | solution.py:12
  16.6 6.4 %collective-permute-start.5 = (bf16[64,288]{1,0:T(8,128)(2,1)S(1)}, bf16[64,288]{1,0:T(8,128)(2,1)S(1)}, u32[]{:S(2)}, u32[]{:S(2)}) collective-permute-start(bf16[64,288]{1,0:T(8,128)(2,1)S(1)} %get-tuple-element.22), channel_id=1, source_target_pairs={{0,16},{4,20},{8,24},{12,28},{16,0},{20,4},{24,8},{28,12},{1,17},{... | collective-permute-start | bytes 110600 | tf_op jit(solution)/shard_map/ppermute | solution.py:12
  19.2 5.9 %collective-permute-start.6 = (bf16[64,288]{1,0:T(8,128)(2,1)S(1)}, bf16[64,288]{1,0:T(8,128)(2,1)S(1)}, u32[]{:S(2)}, u32[]{:S(2)}) collective-permute-start(bf16[64,288]{1,0:T(8,128)(2,1)S(1)} %get-tuple-element.22), channel_id=1, source_target_pairs={{0,24},{4,28},{8,16},{12,20},{16,8},{20,12},{24,0},{28,4},{1,25},{... | collective-permute-start | bytes 110600 | tf_op jit(solution)/shard_map/ppermute | solution.py:12
  19.5 7.2 %collective-permute-start.10 = (bf16[64,512]{1,0:T(8,128)(2,1)S(1)}, bf16[64,512]{1,0:T(8,128)(2,1)S(1)}, u32[]{:S(2)}, u32[]{:S(2)}) collective-permute-start(bf16[64,512]{1,0:T(8,128)(2,1)S(1)} %copy-done.11), channel_id=1, source_target_pairs={{0,1},{1,0},{2,3},{3,2},{4,5},{5,4},{6,7},{7,6},{8,9},{9,8},{10,11... | collective-permute-start | bytes 196616 | tf_op jit(solution)/shard_map/ppermute | solution.py:12
  20.0 6.6 %collective-permute-start.11 = (bf16[64,512]{1,0:T(8,128)(2,1)S(1)}, bf16[64,512]{1,0:T(8,128)(2,1)S(1)}, u32[]{:S(2)}, u32[]{:S(2)}) collective-permute-start(bf16[64,512]{1,0:T(8,128)(2,1)S(1)} %copy-done.11), channel_id=1, source_target_pairs={{0,2},{1,3},{2,0},{3,1},{4,6},{5,7},{6,4},{7,5},{8,10},{9,11},{10,... | collective-permute-start | bytes 196616 | tf_op jit(solution)/shard_map/ppermute | solution.py:12
  21.1 5.6 %collective-permute-start.12 = (bf16[64,512]{1,0:T(8,128)(2,1)S(1)}, bf16[64,512]{1,0:T(8,128)(2,1)S(1)}, u32[]{:S(2)}, u32[]{:S(2)}) collective-permute-start(bf16[64,512]{1,0:T(8,128)(2,1)S(1)} %copy-done.11), channel_id=1, source_target_pairs={{0,3},{1,2},{2,1},{3,0},{4,7},{5,6},{6,5},{7,4},{8,11},{9,10},{10,... | collective-permute-start | bytes 196616 | tf_op jit(solution)/shard_map/ppermute | solution.py:12
  27.0 4.3 %collective-permute-start.13 = (bf16[64,512]{1,0:T(8,128)(2,1)S(1)}, bf16[64,512]{1,0:T(8,128)(2,1)S(1)}, u32[]{:S(2)}, u32[]{:S(2)}) collective-permute-start(bf16[64,512]{1,0:T(8,128)(2,1)S(1)} %fusion.57), channel_id=1, source_target_pairs={{0,1},{1,0},{2,3},{3,2},{4,5},{5,4},{6,7},{7,6},{8,9},{9,8},{10,11... | collective-permute-start | bytes 196616 | tf_op jit(solution)/shard_map/ppermute | solution.py:12
  27.6 4.3 %collective-permute-start.14 = (bf16[64,512]{1,0:T(8,128)(2,1)S(1)}, bf16[64,512]{1,0:T(8,128)(2,1)S(1)}, u32[]{:S(2)}, u32[]{:S(2)}) collective-permute-start(bf16[64,512]{1,0:T(8,128)(2,1)S(1)} %fusion.57), channel_id=1, source_target_pairs={{0,2},{1,3},{2,0},{3,1},{4,6},{5,7},{6,4},{7,5},{8,10},{9,11},{10,... | collective-permute-start | bytes 196616 | tf_op jit(solution)/shard_map/ppermute | solution.py:12
  29.1 5.2 %collective-permute-start.15 = (bf16[64,512]{1,0:T(8,128)(2,1)S(1)}, bf16[64,512]{1,0:T(8,128)(2,1)S(1)}, u32[]{:S(2)}, u32[]{:S(2)}) collective-permute-start(bf16[64,512]{1,0:T(8,128)(2,1)S(1)} %fusion.57), channel_id=1, source_target_pairs={{0,3},{1,2},{2,1},{3,0},{4,7},{5,6},{6,5},{7,4},{8,11},{9,10},{10,... | collective-permute-start | bytes 196616 | tf_op jit(solution)/shard_map/ppermute | solution.py:12
  34.8 1.6 %collective-permute-start.16 = (bf16[4,32,1024]{2,1,0:T(8,128)(2,1)S(1)}, bf16[4,32,1024]{2,1,0:T(8,128)(2,1)S(1)}, u32[]{:S(2)}, u32[]{:S(2)}) collective-permute-start(bf16[4,32,1024]{2,1,0:T(8,128)(2,1)S(1)} %fusion.32), channel_id=1, source_target_pairs={{0,4},{4,0},{8,12},{12,8},{16,20},{20,16},{24,28},{28,24},{1,5},{5... | collective-permute-start | bytes 786440 | tf_op jit(solution)/shard_map/ppermute | solution.py:12
  36.6 4.5 %collective-permute-start.17 = (bf16[32,1024]{1,0:T(8,128)(2,1)S(1)}, bf16[32,1024]{1,0:T(8,128)(2,1)S(1)}, u32[]{:S(2)}, u32[]{:S(2)}) collective-permute-start(bf16[32,1024]{1,0:T(8,128)(2,1)S(1)} %get-tuple-element.39), channel_id=1, source_target_pairs={{0,8},{4,12},{8,0},{12,4},{16,24},{20,28},{24,16},{28,20},{1,9},{5... | collective-permute-start | bytes 196616 | tf_op jit(solution)/shard_map/ppermute | solution.py:12
  37.3 7.5 %collective-permute-start.18 = (bf16[32,1024]{1,0:T(8,128)(2,1)S(1)}, bf16[32,1024]{1,0:T(8,128)(2,1)S(1)}, u32[]{:S(2)}, u32[]{:S(2)}) collective-permute-start(bf16[32,1024]{1,0:T(8,128)(2,1)S(1)} %get-tuple-element.41), channel_id=1, source_target_pairs={{0,16},{4,20},{8,24},{12,28},{16,0},{20,4},{24,8},{28,12},{1,17},{... | collective-permute-start | bytes 196616 | tf_op jit(solution)/shard_map/ppermute | solution.py:12
  40.8 6.2 %collective-permute-start.19 = (bf16[32,1024]{1,0:T(8,128)(2,1)S(1)}, bf16[32,1024]{1,0:T(8,128)(2,1)S(1)}, u32[]{:S(2)}, u32[]{:S(2)}) collective-permute-start(bf16[32,1024]{1,0:T(8,128)(2,1)S(1)} %get-tuple-element.40), channel_id=1, source_target_pairs={{0,24},{4,28},{8,16},{12,20},{16,8},{20,12},{24,0},{28,4},{1,25},{... | collective-permute-start | bytes 196616 | tf_op jit(solution)/shard_map/ppermute | solution.py:12
  47.8 4.5 %collective-permute-start.20 = (bf16[32,1024]{1,0:T(8,128)(2,1)S(1)}, bf16[32,1024]{1,0:T(8,128)(2,1)S(1)}, u32[]{:S(2)}, u32[]{:S(2)}) collective-permute-start(bf16[32,1024]{1,0:T(8,128)(2,1)S(1)} %get-tuple-element.19), channel_id=1, source_target_pairs={{0,8},{4,12},{8,0},{12,4},{16,24},{20,28},{24,16},{28,20},{1,9},{5... | collective-permute-start | bytes 196616 | tf_op jit(solution)/shard_map/ppermute | solution.py:12
  48.6 6.4 %collective-permute-start.21 = (bf16[32,1024]{1,0:T(8,128)(2,1)S(1)}, bf16[32,1024]{1,0:T(8,128)(2,1)S(1)}, u32[]{:S(2)}, u32[]{:S(2)}) collective-permute-start(bf16[32,1024]{1,0:T(8,128)(2,1)S(1)} %get-tuple-element.19), channel_id=1, source_target_pairs={{0,16},{4,20},{8,24},{12,28},{16,0},{20,4},{24,8},{28,12},{1,17},{... | collective-permute-start | bytes 196616 | tf_op jit(solution)/shard_map/ppermute | solution.py:12
  50.4 6.1 %collective-permute-start.22 = (bf16[32,1024]{1,0:T(8,128)(2,1)S(1)}, bf16[32,1024]{1,0:T(8,128)(2,1)S(1)}, u32[]{:S(2)}, u32[]{:S(2)}) collective-permute-start(bf16[32,1024]{1,0:T(8,128)(2,1)S(1)} %get-tuple-element.19), channel_id=1, source_target_pairs={{0,24},{4,28},{8,16},{12,20},{16,8},{20,12},{24,0},{28,4},{1,25},{... | collective-permute-start | bytes 196616 | tf_op jit(solution)/shard_map/ppermute | solution.py:12
  56.5 8.0 %collective-permute-start.24 = (bf16[128,1024]{1,0:T(8,128)(2,1)S(1)}, bf16[128,1024]{1,0:T(8,128)(2,1)S(1)}, u32[]{:S(2)}, u32[]{:S(2)}) collective-permute-start(bf16[128,1024]{1,0:T(8,128)(2,1)S(1)} %pad_maximum_fusion.9), channel_id=1, source_target_pairs={{0,1},{1,0},{2,3},{3,2},{4,5},{5,4},{6,7},{7,6},{8,9},{9,8},{10,11... | collective-permute-start | bytes 786440 | tf_op jit(solution)/shard_map/ppermute | solution.py:12
  57.1 7.4 %collective-permute-start.23 = (bf16[128,1024]{1,0:T(8,128)(2,1)S(1)}, bf16[128,1024]{1,0:T(8,128)(2,1)S(1)}, u32[]{:S(2)}, u32[]{:S(2)}) collective-permute-start(bf16[128,1024]{1,0:T(8,128)(2,1)S(1)} %pad_maximum_fusion.9), channel_id=1, source_target_pairs={{0,4},{4,0},{8,12},{12,8},{16,20},{20,16},{24,28},{28,24},{1,5},{5... | collective-permute-start | bytes 786440 | tf_op jit(solution)/shard_map/ppermute | solution.py:12
  57.1 14.3 %collective-permute-start.26 = (bf16[128,1024]{1,0:T(8,128)(2,1)S(1)}, bf16[128,1024]{1,0:T(8,128)(2,1)S(1)}, u32[]{:S(2)}, u32[]{:S(2)}) collective-permute-start(bf16[128,1024]{1,0:T(8,128)(2,1)S(1)} %pad_maximum_fusion.9), channel_id=1, source_target_pairs={{0,2},{1,3},{2,0},{3,1},{4,6},{5,7},{6,4},{7,5},{8,10},{9,11},{10,... | collective-permute-start | bytes 786440 | tf_op jit(solution)/shard_map/ppermute | solution.py:12
  58.1 13.3 %collective-permute-start.28 = (bf16[128,1024]{1,0:T(8,128)(2,1)S(1)}, bf16[128,1024]{1,0:T(8,128)(2,1)S(1)}, u32[]{:S(2)}, u32[]{:S(2)}) collective-permute-start(bf16[128,1024]{1,0:T(8,128)(2,1)S(1)} %pad_maximum_fusion.9), channel_id=1, source_target_pairs={{0,3},{1,2},{2,1},{3,0},{4,7},{5,6},{6,5},{7,4},{8,11},{9,10},{10,... | collective-permute-start | bytes 786440 | tf_op jit(solution)/shard_map/ppermute | solution.py:12
  64.4 7.5 %collective-permute-start.25 = (bf16[128,1024]{1,0:T(8,128)(2,1)S(1)}, bf16[128,1024]{1,0:T(8,128)(2,1)S(1)}, u32[]{:S(2)}, u32[]{:S(2)}) collective-permute-start(bf16[128,1024]{1,0:T(8,128)(2,1)S(1)} %collective-permute-done.24), channel_id=1, source_target_pairs={{0,4},{4,0},{8,12},{12,8},{16,20},{20,16},{24,28},{28,24},{1,5},{5... | collective-permute-start | bytes 786440 | tf_op jit(solution)/shard_map/ppermute | solution.py:12
  71.4 1.5 %collective-permute-start.27 = (bf16[128,1024]{1,0:T(8,128)(2,1)S(1)}, bf16[128,1024]{1,0:T(8,128)(2,1)S(1)}, u32[]{:S(2)}, u32[]{:S(2)}) collective-permute-start(bf16[128,1024]{1,0:T(8,128)(2,1)S(1)} %collective-permute-done.26), channel_id=1, source_target_pairs={{0,4},{4,0},{8,12},{12,8},{16,20},{20,16},{24,28},{28,24},{1,5},{5... | collective-permute-start | bytes 786440 | tf_op jit(solution)/shard_map/ppermute | solution.py:12
  71.4 1.9 %collective-permute-start.29 = (bf16[128,1024]{1,0:T(8,128)(2,1)S(1)}, bf16[128,1024]{1,0:T(8,128)(2,1)S(1)}, u32[]{:S(2)}, u32[]{:S(2)}) collective-permute-start(bf16[128,1024]{1,0:T(8,128)(2,1)S(1)} %collective-permute-done.28), channel_id=1, source_target_pairs={{0,4},{4,0},{8,12},{12,8},{16,20},{20,16},{24,28},{28,24},{1,5},{5... | collective-permute-start | bytes 786440 | tf_op jit(solution)/shard_map/ppermute | solution.py:12
  92.5 2.7 %collective-permute-start.30 = (bf16[128,4096]{1,0:T(8,128)(2,1)S(1)}, bf16[128,4096]{1,0:T(8,128)(2,1)S(1)}, u32[]{:S(2)}, u32[]{:S(2)}) collective-permute-start(bf16[128,4096]{1,0:T(8,128)(2,1)S(1)} %slice.93), channel_id=1, source_target_pairs={{0,4},{4,0},{8,12},{12,8},{16,20},{20,16},{24,28},{28,24},{1,5},{5... | collective-permute-start | bytes 3145736 | tf_op jit(solution)/shard_map/ppermute | solution.py:12
  95.7 9.2 %collective-permute-start.31 = (bf16[128,1024]{1,0:T(8,128)(2,1)S(1)}, bf16[128,1024]{1,0:T(8,128)(2,1)S(1)}, u32[]{:S(2)}, u32[]{:S(2)}) collective-permute-start(bf16[128,1024]{1,0:T(8,128)(2,1)S(1)} %get-tuple-element.28), channel_id=1, source_target_pairs={{0,1},{1,0},{2,3},{3,2},{4,5},{5,4},{6,7},{7,6},{8,9},{9,8},{10,11... | collective-permute-start | bytes 786440 | tf_op jit(solution)/shard_map/ppermute | solution.py:12
  97.2 13.9 %collective-permute-start.32 = (bf16[128,1024]{1,0:T(8,128)(2,1)S(1)}, bf16[128,1024]{1,0:T(8,128)(2,1)S(1)}, u32[]{:S(2)}, u32[]{:S(2)}) collective-permute-start(bf16[128,1024]{1,0:T(8,128)(2,1)S(1)} %get-tuple-element.30), channel_id=1, source_target_pairs={{0,2},{1,3},{2,0},{3,1},{4,6},{5,7},{6,4},{7,5},{8,10},{9,11},{10,... | collective-permute-start | bytes 786440 | tf_op jit(solution)/shard_map/ppermute | solution.py:12
  97.7 13.4 %collective-permute-start.33 = (bf16[128,1024]{1,0:T(8,128)(2,1)S(1)}, bf16[128,1024]{1,0:T(8,128)(2,1)S(1)}, u32[]{:S(2)}, u32[]{:S(2)}) collective-permute-start(bf16[128,1024]{1,0:T(8,128)(2,1)S(1)} %get-tuple-element.29), channel_id=1, source_target_pairs={{0,3},{1,2},{2,1},{3,0},{4,7},{5,6},{6,5},{7,4},{8,11},{9,10},{10,... | collective-permute-start | bytes 786440 | tf_op jit(solution)/shard_map/ppermute | solution.py:12
  111.3 7.2 %collective-permute-start.34 = (bf16[32,1024]{1,0:T(8,128)(2,1)S(1)}, bf16[32,1024]{1,0:T(8,128)(2,1)S(1)}, u32[]{:S(2)}, u32[]{:S(2)}) collective-permute-start(bf16[32,1024]{1,0:T(8,128)(2,1)S(1)} %get-tuple-element.46), channel_id=1, source_target_pairs={{0,8},{4,12},{8,0},{12,4},{16,24},{20,28},{24,16},{28,20},{1,9},{5... | collective-permute-start | bytes 196616 | tf_op jit(solution)/shard_map/ppermute | solution.py:12
  111.4 8.8 %collective-permute-start.35 = (bf16[32,1024]{1,0:T(8,128)(2,1)S(1)}, bf16[32,1024]{1,0:T(8,128)(2,1)S(1)}, u32[]{:S(2)}, u32[]{:S(2)}) collective-permute-start(bf16[32,1024]{1,0:T(8,128)(2,1)S(1)} %get-tuple-element.48), channel_id=1, source_target_pairs={{0,16},{4,20},{8,24},{12,28},{16,0},{20,4},{24,8},{28,12},{1,17},{... | collective-permute-start | bytes 196616 | tf_op jit(solution)/shard_map/ppermute | solution.py:12
  113.9 6.3 %collective-permute-start.36 = (bf16[32,1024]{1,0:T(8,128)(2,1)S(1)}, bf16[32,1024]{1,0:T(8,128)(2,1)S(1)}, u32[]{:S(2)}, u32[]{:S(2)}) collective-permute-start(bf16[32,1024]{1,0:T(8,128)(2,1)S(1)} %get-tuple-element.47), channel_id=1, source_target_pairs={{0,24},{4,28},{8,16},{12,20},{16,8},{20,12},{24,0},{28,4},{1,25},{... | collective-permute-start | bytes 196616 | tf_op jit(solution)/shard_map/ppermute | solution.py:12
  116.8 16.6 %collective-permute-start.7 = (bf16[32,9216]{1,0:T(8,128)(2,1)}, bf16[32,9216]{1,0:T(8,128)(2,1)}, u32[]{:S(2)}, u32[]{:S(2)}) collective-permute-start(bf16[32,9216]{1,0:T(8,128)(2,1)} %get-tuple-element.27), channel_id=1, source_target_pairs={{0,1},{1,0},{2,3},{3,2},{4,5},{5,4},{6,7},{7,6},{8,9},{9,8},{10,11... | collective-permute-start | bytes 1769480 | tf_op jit(solution)/shard_map/ppermute | solution.py:12
  117.3 25.1 %collective-permute-start.8 = (bf16[32,9216]{1,0:T(8,128)(2,1)S(1)}, bf16[32,9216]{1,0:T(8,128)(2,1)}, u32[]{:S(2)}, u32[]{:S(2)}) collective-permute-start(bf16[32,9216]{1,0:T(8,128)(2,1)S(1)} %get-tuple-element.26), channel_id=1, source_target_pairs={{0,2},{1,3},{2,0},{3,1},{4,6},{5,7},{6,4},{7,5},{8,10},{9,11},{10,... | collective-permute-start | bytes 1769480 | tf_op jit(solution)/shard_map/ppermute | solution.py:12
  118.5 24.9 %collective-permute-start.9 = (bf16[32,9216]{1,0:T(8,128)(2,1)S(1)}, bf16[32,9216]{1,0:T(8,128)(2,1)}, u32[]{:S(2)}, u32[]{:S(2)}) collective-permute-start(bf16[32,9216]{1,0:T(8,128)(2,1)S(1)} %get-tuple-element.25), channel_id=1, source_target_pairs={{0,3},{1,2},{2,1},{3,0},{4,7},{5,6},{6,5},{7,4},{8,11},{9,10},{10,... | collective-permute-start | bytes 1769480 | tf_op jit(solution)/shard_map/ppermute | solution.py:12
  120.3 4.3 %collective-permute-start.37 = (bf16[32,1024]{1,0:T(8,128)(2,1)S(1)}, bf16[32,1024]{1,0:T(8,128)(2,1)S(1)}, u32[]{:S(2)}, u32[]{:S(2)}) collective-permute-start(bf16[32,1024]{1,0:T(8,128)(2,1)S(1)} %fusion.61), channel_id=1, source_target_pairs={{0,8},{4,12},{8,0},{12,4},{16,24},{20,28},{24,16},{28,20},{1,9},{5... | collective-permute-start | bytes 196616 | tf_op jit(solution)/shard_map/ppermute | solution.py:12
  120.5 6.1 %collective-permute-start.38 = (bf16[32,1024]{1,0:T(8,128)(2,1)S(1)}, bf16[32,1024]{1,0:T(8,128)(2,1)S(1)}, u32[]{:S(2)}, u32[]{:S(2)}) collective-permute-start(bf16[32,1024]{1,0:T(8,128)(2,1)S(1)} %fusion.61), channel_id=1, source_target_pairs={{0,16},{4,20},{8,24},{12,28},{16,0},{20,4},{24,8},{28,12},{1,17},{... | collective-permute-start | bytes 196616 | tf_op jit(solution)/shard_map/ppermute | solution.py:12
  124.6 6.1 %collective-permute-start.39 = (bf16[32,1024]{1,0:T(8,128)(2,1)S(1)}, bf16[32,1024]{1,0:T(8,128)(2,1)S(1)}, u32[]{:S(2)}, u32[]{:S(2)}) collective-permute-start(bf16[32,1024]{1,0:T(8,128)(2,1)S(1)} %fusion.61), channel_id=1, source_target_pairs={{0,24},{4,28},{8,16},{12,20},{16,8},{20,12},{24,0},{28,4},{1,25},{... | collective-permute-start | bytes 196616 | tf_op jit(solution)/shard_map/ppermute | solution.py:12
  130.8 19.7 %collective-permute-start.40 = (bf16[128,1024]{1,0:T(8,128)(2,1)S(1)}, bf16[128,1024]{1,0:T(8,128)(2,1)}, u32[]{:S(2)}, u32[]{:S(2)}) collective-permute-start(bf16[128,1024]{1,0:T(8,128)(2,1)S(1)} %pad_maximum_fusion.11), channel_id=1, source_target_pairs={{0,4},{4,0},{8,12},{12,8},{16,20},{20,16},{24,28},{28,24},{1,5},{5... | collective-permute-start | bytes 786440 | tf_op jit(solution)/shard_map/ppermute | solution.py:12
  (9 other events, 45.2 us)

commit v2 on v1

v2 whole, which is shorter than its diff:
```python
import jax
import jax.numpy as jnp
from jax import lax
from jax.experimental import pallas as pl
from jax.experimental.pallas import tpu as pltpu
from jax.sharding import PartitionSpec as P

F32 = jnp.float32
BF16 = jnp.bfloat16


def swap(values, axis, flip):
    size = lax.axis_size(axis)
    return lax.ppermute(values, axis, [(i, i ^ flip) for i in range(size)])


def gather_pairs(values, axis, stride=1):
    count = lax.axis_size(axis) // stride
    return [values] + [swap(values, axis, flip * stride) for flip in range(1, count)]


def scatter_pairs(parts, axis, stride=1):
    total = parts[0].astype(F32)
    for flip in range(1, len(parts)):
        total = total + swap(parts[flip].astype(BF16), axis, flip * stride).astype(F32)
    return total


def dispatch_experts(stream, norm_gain, routes, gate_weight, expert_gate, expert_up, expert_down, row_count, capacity):
    owners = lax.axis_size("expert")
    top_count = routes.shape[1]
    width = stream.shape[1]
    expert_hot = (
        (routes[:, :, None] == jnp.arange(owners)[None, None, :])
        .astype(jnp.int32)
        .reshape(owners, row_count * top_count, owners)
    )
    prior = jnp.sum((jnp.cumsum(expert_hot, axis=1) - expert_hot) * expert_hot, axis=2)
    slot_of = (routes.reshape(owners, row_count * top_count) * capacity + prior).reshape(owners, row_count, top_count)
    matches = slot_of[:, :, :, None] == jnp.arange(owners * capacity)[None, None, None, :]
    dispatch_hot = jnp.any(matches, axis=2).astype(BF16).reshape(owners, row_count, owners, capacity)
    combine_w = jnp.sum(
        jnp.where(matches, gate_weight.reshape(owners, row_count, top_count)[:, :, :, None], 0.0), axis=2
    ).reshape(owners, row_count, owners, capacity)
    outgoing = jnp.einsum(
        "orec,ord->eocd", dispatch_hot, stream.reshape(owners, row_count, width), preferred_element_type=F32
    ).astype(BF16)
    arrived = lax.all_to_all(outgoing, "expert", split_axis=0, concat_axis=3, tiled=True)
    tokens = arrived.reshape(owners * capacity, -1).astype(F32)
    normed = (
        tokens * lax.rsqrt(jnp.mean(tokens * tokens, axis=1, keepdims=True) + 1e-05) * norm_gain[None, :]
    ).astype(BF16)
    gate_val = jnp.dot(normed, expert_gate, preferred_element_type=F32)
    up_val = jnp.dot(normed, expert_up, preferred_element_type=F32)
    hidden = (jax.nn.silu(gate_val) * up_val).astype(BF16)
    partial_out = jnp.dot(hidden, expert_down, preferred_element_type=F32).reshape(owners, capacity, -1)
    summed = lax.psum(partial_out, "dp")
    returned = lax.all_to_all(summed.astype(BF16), "expert", split_axis=2, concat_axis=0, tiled=True).astype(F32)
    expert_mix = jnp.einsum(
        "orec,eocd->ord",
        combine_w,
        returned.reshape(owners, owners, capacity, width),
        precision=lax.Precision.HIGHEST,
        preferred_element_type=F32,
    )
    return (stream.astype(F32) + expert_mix.reshape(-1, width)).astype(BF16)


def pack_rows(source_rows, states, segments):
    tails = [tail for _, _, tail in segments if tail is not None]
    extra = tails[0].shape[0]

    def kernel(rows_ref, states_ref, *refs):
        tail_refs, out_refs = list(refs[: len(tails)]), refs[len(tails) :]
        for (start, count, tail), out_ref in zip(segments, out_refs):

            def step(i, carry, start=start, out_ref=out_ref):
                out_ref[i] = states_ref[rows_ref[start + i]]
                return carry

            lax.fori_loop(0, count, step, 0, unroll=8)
            if tail is not None:
                out_ref[count:] = tail_refs.pop(0)[...]

    here = pl.BlockSpec(memory_space=pltpu.VMEM)
    return pl.pallas_call(
        kernel,
        out_shape=[
            jax.ShapeDtypeStruct((count + (0 if tail is None else extra),) + states.shape[1:], states.dtype)
            for _, count, tail in segments
        ],
        in_specs=[pl.BlockSpec(memory_space=pltpu.SMEM)] + [here] * (1 + len(tails)),
        out_specs=[here] * len(segments),
        name="pack_rows",
    )(source_rows, states, *tails)


def place_rows(source_rows, parts):
    counts = [part.shape[0] for part in parts]
    starts = [sum(counts[:k]) for k in range(len(parts))]
    row_shape = parts[0].shape[1:]
    row_count = source_rows.shape[0]

    def kernel(rows_ref, *refs):
        part_refs, (out_ref, held, sems) = refs[: len(parts)], refs[len(parts) :]
        copies = [
            pltpu.make_async_copy(part_ref, held.at[pl.ds(start, count)], sems.at[k])
            for k, (part_ref, start, count) in enumerate(zip(part_refs, starts, counts))
        ]
        for copy in copies:
            copy.start()
        for copy in copies:
            copy.wait()

        def step(i, carry):
            out_ref[i] = held[rows_ref[i]]
            return carry

        lax.fori_loop(0, row_count, step, 0, unroll=8)

    return pl.pallas_call(
        kernel,
        out_shape=jax.ShapeDtypeStruct((row_count,) + row_shape, parts[0].dtype),
        in_specs=[pl.BlockSpec(memory_space=pltpu.SMEM)] + [pl.BlockSpec(memory_space=pl.ANY)] * len(parts),
        out_specs=pl.BlockSpec(memory_space=pltpu.VMEM),
        scratch_shapes=[
            pltpu.VMEM((sum(counts),) + row_shape, parts[0].dtype),
            pltpu.SemaphoreType.DMA((len(parts),)),
        ],
        name="place_rows",
    )(source_rows, *parts)


def expert_kernel(owner_ids, blocks, gains, gate_w, up_w, carry=None, down=None):
    half, width = blocks[0][0].shape
    rows = 2 * half
    depth, hidden_dim = gate_w.shape
    count = len(blocks)
    tile = 256
    last = down is not None
    out_count = down[2] if last else 0

    def kernel(ids_ref, *refs):
        block_refs, refs = refs[: 2 * count], refs[2 * count :]
        gains_ref, gate_ref, up_ref = refs[:3]
        refs = list(refs[3:])
        if carry is not None:
            gate_in, up_in, square_in = (refs.pop(0) for _ in range(3))
            gate_carry, up_carry, carry_sems = (refs.pop() for _ in range(3))
        if last:
            down_ref, weight_ref = (refs.pop(0) for _ in range(2))
            out_refs = [refs.pop(0) for _ in range(2 * out_count)]
            hidden, down_buf, outs, tail_sems = (refs.pop() for _ in range(4))
        gate_sum, up_sum, square, mixed, gate_buf, up_buf, sems = refs

        def fetch(b, w):
            source, buf = ((gate_ref, gate_buf), (up_ref, up_buf))[w]
            at = pl.multiple_of(ids_ref[b] * width, width)
            return pltpu.make_async_copy(source.at[pl.ds(at, width)], buf.at[b], sems.at[b, w])

        def fetch_down(k):
            at = pl.multiple_of(ids_ref[count + k] * width, width)
            return pltpu.make_async_copy(down_ref.at[:, pl.ds(at, width)], down_buf.at[k], tail_sems.at[0, k])

        def fetch_carry(w):
            source, buf = ((gate_in, gate_carry), (up_in, up_carry))[w]
            return pltpu.make_async_copy(source, buf, carry_sems.at[w])

        def give(k, h):
            return pltpu.make_async_copy(outs.at[k, h], out_refs[2 * k + h], tail_sems.at[1 + h, k])

        queue = [[fetch(b, 0), fetch(b, 1)] for b in range(count)]
        if carry is not None:
            queue.append([fetch_carry(0), fetch_carry(1)])
        queue += [[fetch_down(k)] for k in range(out_count)]

        def start_next():
            if queue:
                for copy in queue.pop(0):
                    copy.start()

        start_next()
        start_next()
        square[...] = jnp.zeros_like(square) if carry is None else square_in[...]
        for b in range(count):
            gain = gains_ref[ids_ref[b]]
            for h in range(2):
                values = block_refs[2 * b + h][...].astype(F32)
                square[h * half : (h + 1) * half] += jnp.sum(values * values, axis=1, keepdims=True)
                mixed[b, h * half : (h + 1) * half] = (values * gain).astype(BF16)
        for b in range(count):
            fetch(b, 0).wait()
            fetch(b, 1).wait()
            start_next()
            if carry is not None and b == count - 1:
                fetch_carry(0).wait()
                fetch_carry(1).wait()
                start_next()
            if last and b == count - 1:
                scale = lax.rsqrt(square[...] / depth + 1e-05)
            left = mixed[b]
            for at in range(0, hidden_dim, tile):
                to = min(at + tile, hidden_dim)
                gate_val = jnp.dot(left, gate_buf[b, :, at:to], preferred_element_type=F32)
                up_val = jnp.dot(left, up_buf[b, :, at:to], preferred_element_type=F32)
                if b > 0:
                    gate_val, up_val = gate_val + gate_sum[:, at:to], up_val + up_sum[:, at:to]
                if carry is not None and b == count - 1:
                    gate_val, up_val = gate_val + gate_carry[:, at:to], up_val + up_carry[:, at:to]
                if last and b == count - 1:
                    hidden[:, at:to] = (jax.nn.silu(gate_val * scale) * (up_val * scale)).astype(BF16)
                else:
                    gate_sum[:, at:to] = gate_val
                    up_sum[:, at:to] = up_val
        for k in range(out_count):
            fetch_down(k).wait()
            start_next()
            for at in range(0, width, tile):
                out = jnp.dot(hidden[...], down_buf[k, :, at : at + tile], preferred_element_type=F32)
                out = out * weight_ref[...]
                outs[k, 0, :, at : at + tile] = out[:half].astype(BF16)
                outs[k, 1, :, at : at + tile] = out[half:].astype(BF16)
            give(k, 0).start()
            give(k, 1).start()
        for k in range(out_count):
            give(k, 0).wait()
            give(k, 1).wait()

    here = pl.BlockSpec(memory_space=pltpu.VMEM)
    anywhere = pl.BlockSpec(memory_space=pl.ANY)
    operands = [owner_ids] + [part for block in blocks for part in block] + [gains, gate_w, up_w]
    in_specs = [pl.BlockSpec(memory_space=pltpu.SMEM)] + [here] * (2 * count + 1) + [anywhere] * 2
    sums = [(rows, hidden_dim), (rows, hidden_dim), (rows, 1)]
    scratch = [
        pltpu.VMEM((count, rows, width), BF16),
        pltpu.VMEM((count, width, hidden_dim), BF16),
        pltpu.VMEM((count, width, hidden_dim), BF16),
        pltpu.SemaphoreType.DMA((count, 2)),
    ]
    if carry is not None:
        operands += list(carry)
        in_specs += [anywhere, anywhere, here]
    if last:
        operands += [down[0], down[1]]
        in_specs += [anywhere, here]
        out_shape = [jax.ShapeDtypeStruct((half, width), BF16)] * (2 * out_count)
        out_specs = [anywhere] * (2 * out_count)
        scratch = [pltpu.VMEM(shape, F32) for shape in sums] + scratch
        scratch += [
            pltpu.SemaphoreType.DMA((3, out_count)),
            pltpu.VMEM((out_count, 2, half, width), BF16),
            pltpu.VMEM((out_count, hidden_dim, width), BF16),
            pltpu.VMEM((rows, hidden_dim), BF16),
        ]
    else:
        out_shape = [jax.ShapeDtypeStruct(shape, F32) for shape in sums]
        out_specs = [here] * 3
    if carry is not None:
        scratch += [
            pltpu.SemaphoreType.DMA((2,)),
            pltpu.VMEM((rows, hidden_dim), F32),
            pltpu.VMEM((rows, hidden_dim), F32),
        ]
    return pl.pallas_call(
        kernel,
        out_shape=out_shape,
        in_specs=in_specs,
        out_specs=out_specs,
        scratch_shapes=scratch,
        compiler_params=pltpu.CompilerParams(vmem_limit_bytes=56 * 1024 * 1024),
        name="expert_outputs" if last else "expert_sums",
    )(*operands)


def body(
    ssm_state,
    conv_state,
    new_slot,
    conv_input,
    gate_input,
    conv_weight,
    conv_bias,
    x_proj_weight,
    step_weight,
    step_bias,
    decay_log,
    skip_gain,
    out_proj_weight,
    residual,
    norm_gain,
    routes,
    gate_weight,
    expert_gate,
    expert_up,
    expert_down,
):
    row_count, state_dim, channels = ssm_state.shape
    owners = lax.axis_size("expert")
    own = lax.axis_index("expert")
    dp_index = lax.axis_index("dp")
    core = dp_index % 2
    plane = dp_index // 2
    planes = lax.axis_size("dp") // 2
    rows = owners * row_count
    half = rows // 2
    chunk = half // planes
    tap_count = conv_weight.shape[0]

    conv_all = jnp.concatenate(gather_pairs(conv_input, "expert"), axis=0)
    my_slots = lax.dynamic_slice_in_dim(new_slot, own * row_count, row_count)
    near_ids = (
        (jnp.arange(owners) ^ own)[:, None] * row_count + jnp.arange(row_count)[None, :]
    ).reshape(-1)
    pick = (my_slots[:, None] == near_ids[None, :]).astype(BF16)
    conv_in = jnp.dot(pick, conv_all, preferred_element_type=F32)

    conv_sum = (
        jnp.sum(conv_state.astype(F32) * conv_weight[None, : tap_count - 1, :], axis=1)
        + conv_in * conv_weight[tap_count - 1][None, :]
        + conv_bias[None, :]
    )
    activated = jax.nn.silu(conv_sum).astype(BF16)
    projected = jnp.dot(activated, x_proj_weight, preferred_element_type=F32)
    projected = projected + swap(projected, "dp", 1)
    new_slot, my_slots, gate_input, projected = lax.optimization_barrier(
        (new_slot, my_slots, gate_input, projected)
    )
    gate_all = jnp.concatenate(gather_pairs(gate_input, "expert"), axis=0)
    projected = scatter_pairs([projected] * planes, "dp", 2)

    move_cap = 2 * row_count // owners
    slot_count = owners * move_cap
    target = my_slots // row_count
    target_hot = (target[:, None] == jnp.arange(owners)[None, :]).astype(jnp.int32)
    earlier = jnp.sum((jnp.cumsum(target_hot, axis=0) - target_hot) * target_hot, axis=1)
    send_slot = (target ^ own) * move_cap + earlier
    send_match = jnp.arange(slot_count)[:, None] == send_slot[None, :]
    send_rows = jnp.sum(jnp.where(send_match, jnp.arange(row_count)[None, :], 0), axis=1)
    conv_keep = conv_state[:, 1:, :]
    conv_moving = jnp.dot(
        send_match.astype(BF16), conv_keep.reshape(row_count, -1), preferred_element_type=F32
    ).astype(BF16)
    tails = conv_moving.reshape(owners, -1, state_dim, channels)
    tail_rows = tails.shape[1]
    arriving = (new_slot // row_count == own).astype(jnp.int32).reshape(owners, row_count)
    arrive_rank = (jnp.cumsum(arriving, axis=1) - arriving).reshape(-1)
    source_flip = (jnp.arange(rows) // row_count) ^ own
    from_here = source_flip == 0
    here_row = jnp.arange(rows) % row_count
    is_source = new_slot[None, :] == (own * row_count + jnp.arange(row_count))[:, None]

    early = owners // 2

    def source_of(extra):
        at = row_count + (source_flip - 1) * (move_cap + extra) + arrive_rank
        return jnp.sum(jnp.where(is_source, jnp.where(from_here, here_row, at)[None, :], 0), axis=1)

    ssm_source = source_of(tail_rows)
    conv_source = source_of(0)

    rank_dim = step_weight.shape[0]
    step_low = projected[:, :rank_dim]
    b_coef = projected[:, rank_dim : rank_dim + state_dim]
    c_coef = projected[:, rank_dim + state_dim :]
    step_norm = (
        step_low * lax.rsqrt(jnp.mean(step_low * step_low, axis=1, keepdims=True) + 1e-06)
    ).astype(BF16)
    step_size = jax.nn.softplus(
        jnp.dot(step_norm, step_weight, preferred_element_type=F32) + step_bias[None, :]
    )
    act_float = activated.astype(F32)

    def update(state, step, rate, b_in):
        decays = jnp.exp(step[:, None, :] * rate[None, :, :])
        return decays * state.astype(F32) + (step * act_float)[:, None, :] * b_in[:, :, None]

    rate = -jnp.exp(decay_log)
    states = update(ssm_state, step_size, rate, b_coef)
    gate_in = jnp.dot(pick, gate_all, preferred_element_type=F32)
    gated_out = (
        (jnp.sum(c_coef[:, :, None] * states, axis=1) + skip_gain[None, :] * act_float) * jax.nn.silu(gate_in)
    ).astype(BF16)
    gated_out, *again = lax.optimization_barrier((gated_out, ssm_state, step_size, rate, b_coef))
    ssm_old = update(*again).astype(BF16)

    near_rows = (
        (jnp.arange(2) ^ core)[:, None, None] * half
        + (jnp.arange(planes) ^ plane)[None, :, None] * chunk
        + jnp.arange(chunk)[None, None, :]
    ).reshape(-1)
    gated_all = jnp.concatenate(gather_pairs(gated_out, "expert"), axis=0)
    packed = pack_rows(
        send_rows, ssm_old, [(flip * move_cap, move_cap, tails[flip]) for flip in range(1, owners)]
    )
    gated_all, *packed = lax.optimization_barrier((gated_all, *packed))
    old_slots = new_slot.reshape(owners, row_count)
    near_slots = jnp.concatenate(
        [lax.dynamic_slice_in_dim(old_slots, own ^ flip, 1, axis=0) for flip in range(owners)], axis=0
    ).reshape(-1)
    order_hot = (near_rows[:, None] == near_slots[None, :]).astype(BF16)
    gated_new = jnp.dot(order_hot, gated_all, preferred_element_type=F32).astype(BF16)
    mix = jnp.dot(gated_new, out_proj_weight, preferred_element_type=F32)
    width = mix.shape[1]

    now = [swap(part, "expert", flip) for flip, part in enumerate(packed[:early], 1)]

    mix_half = mix[:half] + swap(mix[half:].astype(BF16), "dp", 1).astype(F32)
    gate_w, up_w, down_w = expert_gate[0], expert_up[0], expert_down[0]
    capacity = min(row_count, 5 * row_count * routes.shape[1] // (2 * owners))
    dense = capacity == row_count
    mix_chunk = scatter_pairs(list(mix_half.reshape(planes, chunk, width)), "dp", 2)
    residual_chunk = lax.dynamic_slice_in_dim(residual, core * half + plane * chunk, chunk, axis=0)
    stream_chunk = (residual_chunk.astype(F32) + mix_chunk).astype(BF16)
    stream_half = jnp.concatenate(gather_pairs(stream_chunk, "dp", 2), axis=0)
    stream_half, *now = lax.optimization_barrier((stream_half, *now))

    def in_order(near_half):
        stacked = near_half.reshape(planes, chunk, width)
        own_half = jnp.concatenate(
            [lax.dynamic_index_in_dim(stacked, plane ^ p, 0, keepdims=False) for p in range(planes)], axis=0
        )
        other = swap(own_half, "dp", 1)
        return jnp.where(
            core == 0, jnp.concatenate([own_half, other], axis=0), jnp.concatenate([other, own_half], axis=0)
        )

    def finish_states(later):
        ssm_new = place_rows(ssm_source, [ssm_old] + now + later)
        conv_rows = [conv_keep.reshape(row_count, -1)] + [
            part[-tail_rows:].reshape(move_cap, -1) for part in now + later
        ]
        conv_rows = jnp.concatenate(conv_rows, axis=0)
        conv_hot = (conv_source[:, None] == jnp.arange(conv_rows.shape[0])[None, :]).astype(BF16)
        conv_moved = jnp.dot(conv_hot, conv_rows, preferred_element_type=F32).astype(BF16)
        conv_new = jnp.concatenate(
            [conv_moved.reshape(row_count, tap_count - 2, channels), conv_input[:, None, :]], axis=1
        )
        return ssm_new, conv_new

    if not dense:
        later = [swap(part, "expert", flip) for flip, part in enumerate(packed[early:], early + 1)]
        stream = in_order(stream_half)
        layer_out = dispatch_experts(
            stream,
            norm_gain,
            routes,
            gate_weight,
            gate_w,
            up_w,
            down_w,
            row_count,
            capacity,
        )
        return (*finish_states(later), layer_out)

    blocks = gather_pairs(stream_half, "expert")
    gains = norm_gain.reshape(owners, 1, width)
    near_owners = jnp.arange(owners, dtype=jnp.int32) ^ own
    row_weight = jnp.sum(jnp.where(routes == own, gate_weight, 0.0), axis=1)
    near_weight = jnp.sum(
        jnp.where(near_rows[:, None] == jnp.arange(rows)[None, :], row_weight[None, :], 0.0), axis=1, keepdims=True
    )
    near_weight, blocks[0] = lax.optimization_barrier((near_weight, blocks[0]))
    pairs = [(block, swap(block, "dp", 1)) for block in blocks[:early]]
    sums = expert_kernel(near_owners[:early], pairs, gains, gate_w, up_w)
    last_count = owners - early
    tied = lax.optimization_barrier((*blocks[early:], *packed[early:], *sums))
    pairs = [(block, swap(block, "dp", 1)) for block in tied[:last_count]]
    later = [swap(part, "expert", flip) for flip, part in enumerate(tied[last_count:-3], early + 1)]
    outs = expert_kernel(
        jnp.concatenate([near_owners[early:], near_owners]),
        pairs,
        gains,
        gate_w,
        up_w,
        tied[-3:],
        (down_w, near_weight, owners),
    )

    others = [swap(outs[2 * k + 1], "dp", 1) for k in range(owners)]
    tied = lax.optimization_barrier((*others, *later))
    others, later = tied[:owners], list(tied[owners:])
    own_columns = scatter_pairs(
        [(outs[2 * k].astype(F32) + others[k].astype(F32)).astype(BF16) for k in range(owners)], "expert"
    )
    own_columns, *done = lax.optimization_barrier((own_columns, *finish_states(later)))

    mix_rows = scatter_pairs(list(own_columns.reshape(planes, chunk, width)), "dp", 2)
    layer_chunk = (stream_chunk.astype(F32) + mix_rows).astype(BF16)
    layer_half = jnp.concatenate(gather_pairs(layer_chunk, "dp", 2), axis=0)
    return (*done, in_order(layer_half))


def solution(mesh):
    in_specs = (
        P("expert", None, "dp"),
        P("expert", None, "dp"),
        P(),
        P("expert", "dp"),
        P("expert", "dp"),
        P(None, "dp"),
        P("dp"),
        P("dp", None),
        P(None, "dp"),
        P("dp"),
        P(None, "dp"),
        P("dp"),
        P("dp", "expert"),
        P(None, "expert"),
        P(),
        P(),
        P(),
        P("expert", None, "dp"),
        P("expert", None, "dp"),
        P("expert", "dp", None),
    )
    out_specs = (P("expert", None, "dp"), P("expert", None, "dp"), P(None, "expert"))
    return jax.shard_map(body, mesh=mesh, in_specs=in_specs, out_specs=out_specs, check_vma=False)
```

time: 153 us -> 136 us (0.89)
  waiting for transfers between devices: 62.3 us -> 36.3 us
  Pallas kernels: 0 us -> 24.1 us
  matrix products: 21.9 us -> 3.02 us
  other arithmetic: 11.1 us -> 15 us
    ppermute x41 -> x44, waiting for transfers between devices: 62.3 us -> 36.3 us  [swap(): return lax.ppermute(values, axis, [(i, i ^ flip) for i in range(size)])]
    pallas_call x0 -> x4, Pallas kernels: none -> 24.1 us  [the longest x2 17.6 us: expert_kernel(): pl.pallas_call(kernel, out_shape=out_shape, in_specs=in_specs, out_specs=...]
    dot_general x4 -> x2, matrix products: 18.7 us -> 0.56 us  [the longest x1 0.33 us: body(): jnp.dot(send_match.astype(BF16), conv_keep.reshape(row_count, -1), prefer...]
    convert_element_type x1 -> x5, other arithmetic: 0.7 us -> 6.1 us  [the longest x3 3.61 us: body(): (outs[2 * k].astype(F32) + others[k].astype(F32)).astype(BF16)]
    slice x8 -> x6, local copies, waits for them, and re-layouts: 3.68 us -> 1.45 us  [the longest x3 0.86 us: finish_states(): part[-tail_rows:].reshape(move_cap, -1)]
    squeeze x2 -> x3, local copies, waits for them, and re-layouts: 0.21 us -> 1.96 us  [body(): tails[flip]]
    ppermute x41 -> x44, starting transfers between devices: 45.7 us -> 46.1 us  [swap(): return lax.ppermute(values, axis, [(i, i ^ flip) for i in range(size)])]
  transfers between devices with their start and end apart: 41 -> 44, of which waited for: 23 -> 16; matrix products, arithmetic and copies ran while one was open for 11% -> 15% of each run, Pallas kernels for 0% -> 18%
where the time goes in v2:
time: 136 us; the launch traced here: 135 us
  starting transfers between devices  46.1 us (34%)
  waiting for transfers between devices  36.3 us (27%)
  Pallas kernels  24.1 us (18%)
  other arithmetic  15 us (11%)
  local copies, waits for them, and re-layouts  9.61 us (7%)
  matrix products  3.02 us (2%)
  between operations  1.39 us (1%)
    ppermute x44, starting transfers between devices, swap(): return lax.ppermute(values, axis, [(i, i ^ flip) for i in range(size)])  46.1 us
    ppermute x44, waiting for transfers between devices, swap(): return lax.ppermute(values, axis, [(i, i ^ flip) for i in range(size)])  36.3 us
    pallas_call x2, Pallas kernels, expert_kernel(): pl.pallas_call(kernel, out_shape=out_shape, in_specs=in_specs, out_specs=...  17.6 us
    pallas_call x1, Pallas kernels, place_rows(): pl.pallas_call(kernel, out_shape=jax.ShapeDtypeStruct((row_count,) + row_...  3.63 us
    convert_element_type x3, other arithmetic, body(): (outs[2 * k].astype(F32) + others[k].astype(F32)).astype(BF16)  3.61 us
    pallas_call x1, Pallas kernels, pack_rows(): pl.pallas_call(kernel, out_shape=[jax.ShapeDtypeStruct((count + (0 if tai...  2.85 us
  transfers between devices with their start and end apart: 44, of which 16 were waited for; matrix products, arithmetic and copies ran while one was open for 15% of the time, Pallas kernels for 18%

profile of v2, /device:TPU:0, one launch (start us, length us, event | category | flops | bytes accessed | tf_op | source)
XLA Modules:
  0.0 135.5 jit_solution(6162087439791541652)
XLA Ops:
  0.7 3.0 %collective-permute-start = (bf16[64,512]{1,0:T(8,128)(2,1)}, bf16[64,512]{1,0:T(8,128)(2,1)S(1)}, u32[]{:S(2)}, u32[]{:S(2)}) collective-permute-start(bf16[64,512]{1,0:T(8,128)(2,1)} %param.23), channel_id=1, source_target_pairs={{0,1},{1,0},{2,3},{3,2},{4,5},{5,4},{6,7},{7,6},{8,9},{9,8},{10,11... | collective-permute-start | bytes 196616 | tf_op jit(solution)/shard_map/ppermute | solution.py:14
  3.7 1.5 %collective-permute-start.1 = (bf16[64,512]{1,0:T(8,128)(2,1)}, bf16[64,512]{1,0:T(8,128)(2,1)S(1)}, u32[]{:S(2)}, u32[]{:S(2)}) collective-permute-start(bf16[64,512]{1,0:T(8,128)(2,1)} %param.23), channel_id=1, source_target_pairs={{0,2},{1,3},{2,0},{3,1},{4,6},{5,7},{6,4},{7,5},{8,10},{9,11},{10,... | collective-permute-start | bytes 196616 | tf_op jit(solution)/shard_map/ppermute | solution.py:14
  6.8 0.9 slice_bitcast_fusion
  8.7 1.0 multiply_reduce_fusion.1
  10.6 1.1 multiply_convert_fusion
  12.2 1.1 collective-permute-done.3
  13.4 1.6 %collective-permute-start.4 = (bf16[64,288]{1,0:T(8,128)(2,1)S(1)}, bf16[64,288]{1,0:T(8,128)(2,1)S(1)}, u32[]{:S(2)}, u32[]{:S(2)}) collective-permute-start(bf16[64,288]{1,0:T(8,128)(2,1)S(1)} %convert_element_type.148), channel_id=1, source_target_pairs={{0,8},{4,12},{8,0},{12,4},{16,24},{20,28},{24,16},{28,20},{1,9},{5... | collective-permute-start | bytes 110600 | tf_op jit(solution)/shard_map/ppermute | solution.py:14
  15.0 2.6 %collective-permute-start.5 = (bf16[64,288]{1,0:T(8,128)(2,1)S(1)}, bf16[64,288]{1,0:T(8,128)(2,1)S(1)}, u32[]{:S(2)}, u32[]{:S(2)}) collective-permute-start(bf16[64,288]{1,0:T(8,128)(2,1)S(1)} %convert_element_type.148), channel_id=1, source_target_pairs={{0,16},{4,20},{8,24},{12,28},{16,0},{20,4},{24,8},{28,12},{1,17},{... | collective-permute-start | bytes 110600 | tf_op jit(solution)/shard_map/ppermute | solution.py:14
  17.8 1.1 collective-permute-start.7
  18.9 1.5 %collective-permute-start.8 = (bf16[64,512]{1,0:T(8,128)(2,1)S(1)}, bf16[64,512]{1,0:T(8,128)(2,1)S(1)}, u32[]{:S(2)}, u32[]{:S(2)}) collective-permute-start(bf16[64,512]{1,0:T(8,128)(2,1)S(1)} %copy-done.22), channel_id=1, source_target_pairs={{0,2},{1,3},{2,0},{3,1},{4,6},{5,7},{6,4},{7,5},{8,10},{9,11},{10,... | collective-permute-start | bytes 196616 | tf_op jit(solution)/shard_map/ppermute | solution.py:14
  25.4 1.0 multiply_reduce_fusion
  26.4 2.7 %collective-permute-done.9 = bf16[64,512]{1,0:T(8,128)(2,1)S(1)} collective-permute-done((bf16[64,512]{1,0:T(8,128)(2,1)S(1)}, bf16[64,512]{1,0:T(8,128)(2,1)S(1)}, u32[]{:S(2)}, u32[]{:S(2)}) %collective-permute-start.9) | collective-permute-done | bytes 65568 | tf_op jit(solution)/shard_map/ppermute | solution.py:14
  30.0 0.9 collective-permute-start.11
  30.9 2.0 %collective-permute-start.12 = (bf16[64,512]{1,0:T(8,128)(2,1)S(1)}, bf16[64,512]{1,0:T(8,128)(2,1)S(1)}, u32[]{:S(2)}, u32[]{:S(2)}) collective-permute-start(bf16[64,512]{1,0:T(8,128)(2,1)S(1)} %fusion.29), channel_id=1, source_target_pairs={{0,3},{1,2},{2,1},{3,0},{4,7},{5,6},{6,5},{7,4},{8,11},{9,10},{10,... | collective-permute-start | bytes 196616 | tf_op jit(solution)/shard_map/ppermute | solution.py:14
  32.9 1.6 %add_convert_fusion.states_ref.refs_0_ = bf16[64,16,512]{2,1,0:T(8,128)(2,1)} fusion(bf16[64,16,512]{2,1,0:T(8,128)(2,1)S(1)} %copy-done.1, f32[64,16]{1,0:T(8,128)S(1)} %get-tuple-element.57, f32[64,512]{1,0:T(8,128)S(1)} %convert_multiply_fusion, f32[16,512]{1,0:T(8,128)S(1)} %exponential_negate_fusion, f32[64,512]{1,0:T(8,128)S(1)} %get-tuple-element.54), kind=kLoop, calls=%fused_computation | loop fusion | flops 3145728 | bytes 2396160 | tf_op jit(solution)/shard_map/convert_element_type | solution.py:384
  34.5 2.8 %pack_rows.1 = (bf16[36,16,512]{2,1,0:T(8,128)(2,1)}, bf16[36,16,512]{2,1,0:T(8,128)(2,1)}, bf16[36,16,512]{2,1,0:T(8,128)(2,1)}) custom-call(s32[128]{0:T(128)} %select_reduce_fusion.1.rows_ref, bf16[64,16,512]{2,1,0:T(8,128)(2,1)} %add_convert_fusion.states_ref.refs_0_, bf16[4,16,512]{2,1,0:T(8,128)(2,1)} %squeeze.31.refs_0_, ...), custom_call_target="tpu_custom_call" | custom-call | tf_op jit(solution)/shard_map/pack_rows/pallas_call | solution.py:86
  38.8 0.9 collective-permute-start.21
  40.6 3.5 %collective-permute-start.15 = (bf16[32,1024]{1,0:T(8,128)(2,1)S(1)}, bf16[32,1024]{1,0:T(8,128)(2,1)S(1)}, u32[]{:S(2)}, u32[]{:S(2)}) collective-permute-start(bf16[32,1024]{1,0:T(8,128)(2,1)S(1)} %get-tuple-element.114), channel_id=1, source_target_pairs={{0,16},{4,20},{8,24},{12,28},{16,0},{20,4},{24,8},{28,12},{1,17},{... | collective-permute-start | bytes 196616 | tf_op jit(solution)/shard_map/ppermute | solution.py:14
  44.3 3.8 %collective-permute-done.15 = bf16[32,1024]{1,0:T(8,128)(2,1)S(1)} collective-permute-done((bf16[32,1024]{1,0:T(8,128)(2,1)S(1)}, bf16[32,1024]{1,0:T(8,128)(2,1)S(1)}, u32[]{:S(2)}, u32[]{:S(2)}) %collective-permute-start.15) | collective-permute-done | bytes 65568 | tf_op jit(solution)/shard_map/ppermute | solution.py:14
  48.1 2.1 %collective-permute-done.16 = bf16[32,1024]{1,0:T(8,128)(2,1)S(1)} collective-permute-done((bf16[32,1024]{1,0:T(8,128)(2,1)S(1)}, bf16[32,1024]{1,0:T(8,128)(2,1)S(1)}, u32[]{:S(2)}, u32[]{:S(2)}) %collective-permute-start.16) | collective-permute-done | bytes 65568 | tf_op jit(solution)/shard_map/ppermute | solution.py:14
  51.9 1.7 %collective-permute-start.18 = (bf16[32,1024]{1,0:T(8,128)(2,1)S(1)}, bf16[32,1024]{1,0:T(8,128)(2,1)S(1)}, u32[]{:S(2)}, u32[]{:S(2)}) collective-permute-start(bf16[32,1024]{1,0:T(8,128)(2,1)S(1)} %fusion.33), channel_id=1, source_target_pairs={{0,16},{4,20},{8,24},{12,28},{16,0},{20,4},{24,8},{28,12},{1,17},{... | collective-permute-start | bytes 196616 | tf_op jit(solution)/shard_map/ppermute | solution.py:14
  53.6 1.9 %collective-permute-start.19 = (bf16[32,1024]{1,0:T(8,128)(2,1)S(1)}, bf16[32,1024]{1,0:T(8,128)(2,1)S(1)}, u32[]{:S(2)}, u32[]{:S(2)}) collective-permute-start(bf16[32,1024]{1,0:T(8,128)(2,1)S(1)} %fusion.33), channel_id=1, source_target_pairs={{0,24},{4,28},{8,16},{12,20},{16,8},{20,12},{24,0},{28,4},{1,25},{... | collective-permute-start | bytes 196616 | tf_op jit(solution)/shard_map/ppermute | solution.py:14
  55.6 3.0 %collective-permute-done.18 = bf16[32,1024]{1,0:T(8,128)(2,1)S(1)} collective-permute-done((bf16[32,1024]{1,0:T(8,128)(2,1)S(1)}, bf16[32,1024]{1,0:T(8,128)(2,1)S(1)}, u32[]{:S(2)}, u32[]{:S(2)}) %collective-permute-start.18) | collective-permute-done | bytes 65568 | tf_op jit(solution)/shard_map/ppermute | solution.py:14
  58.6 1.2 collective-permute-done.19
  60.9 1.6 %collective-permute-start.22 = (bf16[128,1024]{1,0:T(8,128)(2,1)S(1)}, bf16[128,1024]{1,0:T(8,128)(2,1)S(1)}, u32[]{:S(2)}, u32[]{:S(2)}) collective-permute-start(bf16[128,1024]{1,0:T(8,128)(2,1)S(1)} %pad_maximum_fusion.1.refs_0_), channel_id=1, source_target_pairs={{0,2},{1,3},{2,0},{3,1},{4,6},{5,7},{6,4},{7,5},{8,10},{9,11},{10,... | collective-permute-start | bytes 786440 | tf_op jit(solution)/shard_map/ppermute | solution.py:14
  62.5 1.2 collective-permute-start.23
  63.7 4.8 %collective-permute-done.25.refs_2_ = bf16[128,1024]{1,0:T(8,128)(2,1)S(1)} collective-permute-done((bf16[128,1024]{1,0:T(8,128)(2,1)S(1)}, bf16[128,1024]{1,0:T(8,128)(2,1)S(1)}, u32[]{:S(2)}, u32[]{:S(2)}) %collective-permute-start.25) | collective-permute-done | bytes 262176 | tf_op jit(solution)/shard_map/ppermute | solution.py:14
  69.0 1.0 collective-permute-done.26.refs_3_
  70.7 6.9 %expert_sums.1 = (f32[256,896]{1,0:T(8,128)}, f32[256,896]{1,0:T(8,128)}, f32[256,1]{1,0:T(8,128)}) custom-call(s32[2]{0:T(128)} %get-tuple-element.126.ids_ref, bf16[128,1024]{1,0:T(8,128)(2,1)} %copy-done.2, bf16[128,1024]{1,0:T(8,128)(2,1)} %copy-done.10, bf16[128,1024]{1,0:T(8,128)(2,1)} %copy-done.9, bf16[128,1024]{1,0:T(8,128)(2,1)} %copy-done.11, ...), custom_call_target="tpu_custom_call" | custom-call | tf_op jit(solution)/shard_map/expert_sums/pallas_call | solution.py:264
  78.3 1.6 %collective-permute-start.33 = (bf16[36,16,512]{2,1,0:T(8,128)(2,1)}, bf16[36,16,512]{2,1,0:T(8,128)(2,1)S(1)}, u32[]{:S(2)}, u32[]{:S(2)}) collective-permute-start(bf16[36,16,512]{2,1,0:T(8,128)(2,1)} %get-tuple-element.81), channel_id=1, source_target_pairs={{0,3},{1,2},{2,1},{3,0},{4,7},{5,6},{6,5},{7,4},{8,11},{9,10},{10,... | collective-permute-start | bytes 1769480 | tf_op jit(solution)/shard_map/ppermute | solution.py:14
  82.4 10.7 %expert_outputs.1 = (bf16[128,1024]{1,0:T(8,128)(2,1)}, bf16[128,1024]{1,0:T(8,128)(2,1)}, bf16[128,1024]{1,0:T(8,128)(2,1)}, bf16[128,1024]{1,0:T(8,128)(2,1)},...) custom-call(s32[6]{0:T(128)} %pad_add_fusion.1.ids_ref, ...), custom_call_target="tpu_custom_call" | custom-call | tf_op jit(solution)/shard_map/expert_outputs/pallas_call | solution.py:264
  96.8 1.1 add_convert_fusion.3
  98.6 1.7 %add_convert_fusion.2 = bf16[128,1024]{1,0:T(8,128)(2,1)} fusion(bf16[128,1024]{1,0:T(8,128)(2,1)S(1)} %collective-permute-done.31, bf16[128,1024]{1,0:T(8,128)(2,1)} %get-tuple-element.85), kind=kLoop, calls=%fused_computation.14 | loop fusion | flops 524288 | bytes 786432 | tf_op jit(solution)/shard_map/convert_element_type | solution.py:484
  100.3 1.3 collective-permute-start.35
  102.3 1.7 %collective-permute-start.36 = (bf16[128,1024]{1,0:T(8,128)(2,1)}, bf16[128,1024]{1,0:T(8,128)(2,1)S(1)}, u32[]{:S(2)}, u32[]{:S(2)}) collective-permute-start(bf16[128,1024]{1,0:T(8,128)(2,1)} %add_convert_fusion.1), channel_id=1, source_target_pairs={{0,3},{1,2},{2,1},{3,0},{4,7},{5,6},{6,5},{7,4},{8,11},{9,10},{10,... | collective-permute-start | bytes 786440 | tf_op jit(solution)/shard_map/ppermute | solution.py:14
  104.3 3.6 %place_rows.1 = bf16[64,16,512]{2,1,0:T(8,128)(2,1)} custom-call(s32[64]{0:T(128)} %get-tuple-element.96.rows_ref, bf16[64,16,512]{2,1,0:T(8,128)(2,1)} %add_convert_fusion.states_ref.refs_0_, bf16[36,16,512]{2,1,0:T(8,128)(2,1)} %copy-done.3, bf16[36,16,512]{2,1,0:T(8,128)(2,1)} %collective-permute-done.21.refs_2_, bf16[36,16,512]{2,1,0:T(8,128)(2,1)} %copy-done.4), custom_call_target="tpu_custom_call" | custom-call | tf_op jit(solution)/shard_map/place_rows/pallas_call | solution.py:121
  108.6 5.5 %collective-permute-done.35 = bf16[128,1024]{1,0:T(8,128)(2,1)S(1)} collective-permute-done((bf16[128,1024]{1,0:T(8,128)(2,1)}, bf16[128,1024]{1,0:T(8,128)(2,1)S(1)}, u32[]{:S(2)}, u32[]{:S(2)}) %collective-permute-start.35) | collective-permute-done | bytes 262176 | tf_op jit(solution)/shard_map/ppermute | solution.py:14
  114.2 1.2 convert_add_fusion
  115.4 0.9 collective-permute-start.37
  116.4 1.3 collective-permute-start.38
  117.7 2.2 %collective-permute-start.39 = (bf16[32,1024]{1,0:T(8,128)(2,1)S(1)}, bf16[32,1024]{1,0:T(8,128)(2,1)S(1)}, u32[]{:S(2)}, u32[]{:S(2)}) collective-permute-start(bf16[32,1024]{1,0:T(8,128)(2,1)S(1)} %get-tuple-element.110), channel_id=1, source_target_pairs={{0,24},{4,28},{8,16},{12,20},{16,8},{20,12},{24,0},{28,4},{1,25},{... | collective-permute-start | bytes 196616 | tf_op jit(solution)/shard_map/ppermute | solution.py:14
  120.1 3.7 %collective-permute-done.38 = bf16[32,1024]{1,0:T(8,128)(2,1)S(1)} collective-permute-done((bf16[32,1024]{1,0:T(8,128)(2,1)S(1)}, bf16[32,1024]{1,0:T(8,128)(2,1)S(1)}, u32[]{:S(2)}, u32[]{:S(2)}) %collective-permute-start.38) | collective-permute-done | bytes 65568 | tf_op jit(solution)/shard_map/ppermute | solution.py:14
  123.8 1.3 collective-permute-start.40
  125.2 1.5 %collective-permute-start.41 = (bf16[32,1024]{1,0:T(8,128)(2,1)S(1)}, bf16[32,1024]{1,0:T(8,128)(2,1)S(1)}, u32[]{:S(2)}, u32[]{:S(2)}) collective-permute-start(bf16[32,1024]{1,0:T(8,128)(2,1)S(1)} %add_convert_fusion.5), channel_id=1, source_target_pairs={{0,16},{4,20},{8,24},{12,28},{16,0},{20,4},{24,8},{28,12},{1,17},{... | collective-permute-start | bytes 196616 | tf_op jit(solution)/shard_map/ppermute | solution.py:14
  126.7 1.6 %collective-permute-start.42 = (bf16[32,1024]{1,0:T(8,128)(2,1)S(1)}, bf16[32,1024]{1,0:T(8,128)(2,1)S(1)}, u32[]{:S(2)}, u32[]{:S(2)}) collective-permute-start(bf16[32,1024]{1,0:T(8,128)(2,1)S(1)} %add_convert_fusion.5), channel_id=1, source_target_pairs={{0,24},{4,28},{8,16},{12,20},{16,8},{20,12},{24,0},{28,4},{1,25},{... | collective-permute-start | bytes 196616 | tf_op jit(solution)/shard_map/ppermute | solution.py:14
  128.3 2.7 %collective-permute-done.41 = bf16[32,1024]{1,0:T(8,128)(2,1)S(1)} collective-permute-done((bf16[32,1024]{1,0:T(8,128)(2,1)S(1)}, bf16[32,1024]{1,0:T(8,128)(2,1)S(1)}, u32[]{:S(2)}, u32[]{:S(2)}) %collective-permute-start.41) | collective-permute-done | bytes 65568 | tf_op jit(solution)/shard_map/ppermute | solution.py:14
  131.0 1.7 %collective-permute-done.42 = bf16[32,1024]{1,0:T(8,128)(2,1)S(1)} collective-permute-done((bf16[32,1024]{1,0:T(8,128)(2,1)S(1)}, bf16[32,1024]{1,0:T(8,128)(2,1)S(1)}, u32[]{:S(2)}, u32[]{:S(2)}) %collective-permute-start.42) | collective-permute-done | bytes 65568 | tf_op jit(solution)/shard_map/ppermute | solution.py:14
  133.0 1.5 %collective-permute-done.43 = bf16[128,1024]{1,0:T(8,128)(2,1)S(1)} collective-permute-done((bf16[128,1024]{1,0:T(8,128)(2,1)S(1)}, bf16[128,1024]{1,0:T(8,128)(2,1)S(1)}, u32[]{:S(2)}, u32[]{:S(2)}) %collective-permute-start.43) | collective-permute-done | bytes 262176 | tf_op jit(solution)/shard_map/ppermute | solution.py:14
  (182 shorter events, 26.7 us)
Async XLA Ops:
  0.6 36.8 %copy-start = (bf16[512,1024]{1,0:T(8,128)(2,1)S(1)}, bf16[512,1024]{1,0:T(8,128)(2,1)}, u32[]{:S(2)}) copy-start(bf16[512,1024]{1,0:T(8,128)(2,1)} %param.32) | copy-start | bytes 3145732
  0.7 9.0 %collective-permute-start = (bf16[64,512]{1,0:T(8,128)(2,1)}, bf16[64,512]{1,0:T(8,128)(2,1)S(1)}, u32[]{:S(2)}, u32[]{:S(2)}) collective-permute-start(bf16[64,512]{1,0:T(8,128)(2,1)} %param.23), channel_id=1, source_target_pairs={{0,1},{1,0},{2,3},{3,2},{4,5},{5,4},{6,7},{7,6},{8,9},{9,8},{10,11... | collective-permute-start | bytes 196616 | tf_op jit(solution)/shard_map/ppermute | solution.py:14
  3.7 6.0 %collective-permute-start.1 = (bf16[64,512]{1,0:T(8,128)(2,1)}, bf16[64,512]{1,0:T(8,128)(2,1)S(1)}, u32[]{:S(2)}, u32[]{:S(2)}) collective-permute-start(bf16[64,512]{1,0:T(8,128)(2,1)} %param.23), channel_id=1, source_target_pairs={{0,2},{1,3},{2,0},{3,1},{4,6},{5,7},{6,4},{7,5},{8,10},{9,11},{10,... | collective-permute-start | bytes 196616 | tf_op jit(solution)/shard_map/ppermute | solution.py:14
  5.2 5.4 %collective-permute-start.2 = (bf16[64,512]{1,0:T(8,128)(2,1)}, bf16[64,512]{1,0:T(8,128)(2,1)S(1)}, u32[]{:S(2)}, u32[]{:S(2)}) collective-permute-start(bf16[64,512]{1,0:T(8,128)(2,1)} %param.23), channel_id=1, source_target_pairs={{0,3},{1,2},{2,1},{3,0},{4,7},{5,6},{6,5},{7,4},{8,11},{9,10},{10,... | collective-permute-start | bytes 196616 | tf_op jit(solution)/shard_map/ppermute | solution.py:14
  11.9 1.4 %collective-permute-start.3 = (f32[64,288]{1,0:T(8,128)S(1)}, f32[64,288]{1,0:T(8,128)S(1)}, u32[]{:S(2)}, u32[]{:S(2)}) collective-permute-start(f32[64,288]{1,0:T(8,128)S(1)} %fusion.67), channel_id=1, source_target_pairs={{0,4},{4,0},{8,12},{12,8},{16,20},{20,16},{24,28},{28,24},{1,5},{5... | collective-permute-start | bytes 221192 | tf_op jit(solution)/shard_map/ppermute | solution.py:14
  13.4 10.6 %collective-permute-start.4 = (bf16[64,288]{1,0:T(8,128)(2,1)S(1)}, bf16[64,288]{1,0:T(8,128)(2,1)S(1)}, u32[]{:S(2)}, u32[]{:S(2)}) collective-permute-start(bf16[64,288]{1,0:T(8,128)(2,1)S(1)} %convert_element_type.148), channel_id=1, source_target_pairs={{0,8},{4,12},{8,0},{12,4},{16,24},{20,28},{24,16},{28,20},{1,9},{5... | collective-permute-start | bytes 110600 | tf_op jit(solution)/shard_map/ppermute | solution.py:14
  15.0 9.8 %collective-permute-start.5 = (bf16[64,288]{1,0:T(8,128)(2,1)S(1)}, bf16[64,288]{1,0:T(8,128)(2,1)S(1)}, u32[]{:S(2)}, u32[]{:S(2)}) collective-permute-start(bf16[64,288]{1,0:T(8,128)(2,1)S(1)} %convert_element_type.148), channel_id=1, source_target_pairs={{0,16},{4,20},{8,24},{12,28},{16,0},{20,4},{24,8},{28,12},{1,17},{... | collective-permute-start | bytes 110600 | tf_op jit(solution)/shard_map/ppermute | solution.py:14
  17.6 7.2 %collective-permute-start.6 = (bf16[64,288]{1,0:T(8,128)(2,1)S(1)}, bf16[64,288]{1,0:T(8,128)(2,1)S(1)}, u32[]{:S(2)}, u32[]{:S(2)}) collective-permute-start(bf16[64,288]{1,0:T(8,128)(2,1)S(1)} %convert_element_type.148), channel_id=1, source_target_pairs={{0,24},{4,28},{8,16},{12,20},{16,8},{20,12},{24,0},{28,4},{1,25},{... | collective-permute-start | bytes 110600 | tf_op jit(solution)/shard_map/ppermute | solution.py:14
  17.8 8.5 %collective-permute-start.7 = (bf16[64,512]{1,0:T(8,128)(2,1)S(1)}, bf16[64,512]{1,0:T(8,128)(2,1)S(1)}, u32[]{:S(2)}, u32[]{:S(2)}) collective-permute-start(bf16[64,512]{1,0:T(8,128)(2,1)S(1)} %copy-done.22), channel_id=1, source_target_pairs={{0,1},{1,0},{2,3},{3,2},{4,5},{5,4},{6,7},{7,6},{8,9},{9,8},{10,11... | collective-permute-start | bytes 196616 | tf_op jit(solution)/shard_map/ppermute | solution.py:14
  18.9 7.5 %collective-permute-start.8 = (bf16[64,512]{1,0:T(8,128)(2,1)S(1)}, bf16[64,512]{1,0:T(8,128)(2,1)S(1)}, u32[]{:S(2)}, u32[]{:S(2)}) collective-permute-start(bf16[64,512]{1,0:T(8,128)(2,1)S(1)} %copy-done.22), channel_id=1, source_target_pairs={{0,2},{1,3},{2,0},{3,1},{4,6},{5,7},{6,4},{7,5},{8,10},{9,11},{10,... | collective-permute-start | bytes 196616 | tf_op jit(solution)/shard_map/ppermute | solution.py:14
  23.9 5.2 %collective-permute-start.9 = (bf16[64,512]{1,0:T(8,128)(2,1)S(1)}, bf16[64,512]{1,0:T(8,128)(2,1)S(1)}, u32[]{:S(2)}, u32[]{:S(2)}) collective-permute-start(bf16[64,512]{1,0:T(8,128)(2,1)S(1)} %copy-done.22), channel_id=1, source_target_pairs={{0,3},{1,2},{2,1},{3,0},{4,7},{5,6},{6,5},{7,4},{8,11},{9,10},{10,... | collective-permute-start | bytes 196616 | tf_op jit(solution)/shard_map/ppermute | solution.py:14
  29.4 8.0 %collective-permute-start.10 = (bf16[64,512]{1,0:T(8,128)(2,1)S(1)}, bf16[64,512]{1,0:T(8,128)(2,1)S(1)}, u32[]{:S(2)}, u32[]{:S(2)}) collective-permute-start(bf16[64,512]{1,0:T(8,128)(2,1)S(1)} %fusion.29), channel_id=1, source_target_pairs={{0,1},{1,0},{2,3},{3,2},{4,5},{5,4},{6,7},{7,6},{8,9},{9,8},{10,11... | collective-permute-start | bytes 196616 | tf_op jit(solution)/shard_map/ppermute | solution.py:14
  30.0 7.4 %collective-permute-start.11 = (bf16[64,512]{1,0:T(8,128)(2,1)S(1)}, bf16[64,512]{1,0:T(8,128)(2,1)S(1)}, u32[]{:S(2)}, u32[]{:S(2)}) collective-permute-start(bf16[64,512]{1,0:T(8,128)(2,1)S(1)} %fusion.29), channel_id=1, source_target_pairs={{0,2},{1,3},{2,0},{3,1},{4,6},{5,7},{6,4},{7,5},{8,10},{9,11},{10,... | collective-permute-start | bytes 196616 | tf_op jit(solution)/shard_map/ppermute | solution.py:14
  30.9 6.5 %collective-permute-start.12 = (bf16[64,512]{1,0:T(8,128)(2,1)S(1)}, bf16[64,512]{1,0:T(8,128)(2,1)S(1)}, u32[]{:S(2)}, u32[]{:S(2)}) collective-permute-start(bf16[64,512]{1,0:T(8,128)(2,1)S(1)} %fusion.29), channel_id=1, source_target_pairs={{0,3},{1,2},{2,1},{3,0},{4,7},{5,6},{6,5},{7,4},{8,11},{9,10},{10,... | collective-permute-start | bytes 196616 | tf_op jit(solution)/shard_map/ppermute | solution.py:14
  38.0 22.6 %copy-start.20 = (f32[256,2]{0,1:T(2,128)S(1)}, f32[256,2]{0,1:T(2,128)}, u32[]{:S(2)}) copy-start(f32[256,2]{0,1:T(2,128)} %param.36) | copy-start | bytes 6148
  38.1 22.6 %copy-start.21 = (s32[256,2]{0,1:T(2,128)S(1)}, s32[256,2]{0,1:T(2,128)}, u32[]{:S(2)}) copy-start(s32[256,2]{0,1:T(2,128)} %param.35) | copy-start | bytes 6148
  38.1 1.6 %collective-permute-start.13 = (bf16[128,1024]{1,0:T(8,128)(2,1)S(1)}, bf16[128,1024]{1,0:T(8,128)(2,1)S(1)}, u32[]{:S(2)}, u32[]{:S(2)}) collective-permute-start(bf16[128,1024]{1,0:T(8,128)(2,1)S(1)} %slice.96), channel_id=1, source_target_pairs={{0,4},{4,0},{8,12},{12,8},{16,20},{20,16},{24,28},{28,24},{1,5},{5... | collective-permute-start | bytes 786440 | tf_op jit(solution)/shard_map/ppermute | solution.py:14
  38.2 21.7 %collective-permute-start.20 = (bf16[36,16,512]{2,1,0:T(8,128)(2,1)}, bf16[36,16,512]{2,1,0:T(8,128)(2,1)S(1)}, u32[]{:S(2)}, u32[]{:S(2)}) collective-permute-start(bf16[36,16,512]{2,1,0:T(8,128)(2,1)} %get-tuple-element.62), channel_id=1, source_target_pairs={{0,1},{1,0},{2,3},{3,2},{4,5},{5,4},{6,7},{7,6},{8,9},{9,8},{10,11... | collective-permute-start | bytes 1769480 | tf_op jit(solution)/shard_map/ppermute | solution.py:14
  38.8 21.1 %collective-permute-start.21 = (bf16[36,16,512]{2,1,0:T(8,128)(2,1)}, bf16[36,16,512]{2,1,0:T(8,128)(2,1)}, u32[]{:S(2)}, u32[]{:S(2)}) collective-permute-start(bf16[36,16,512]{2,1,0:T(8,128)(2,1)} %get-tuple-element.63), channel_id=1, source_target_pairs={{0,2},{1,3},{2,0},{3,1},{4,6},{5,7},{6,4},{7,5},{8,10},{9,11},{10,... | collective-permute-start | bytes 1769480 | tf_op jit(solution)/shard_map/ppermute | solution.py:14
  39.8 4.5 %collective-permute-start.14 = (bf16[32,1024]{1,0:T(8,128)(2,1)S(1)}, bf16[32,1024]{1,0:T(8,128)(2,1)S(1)}, u32[]{:S(2)}, u32[]{:S(2)}) collective-permute-start(bf16[32,1024]{1,0:T(8,128)(2,1)S(1)} %get-tuple-element.112), channel_id=1, source_target_pairs={{0,8},{4,12},{8,0},{12,4},{16,24},{20,28},{24,16},{28,20},{1,9},{5... | collective-permute-start | bytes 196616 | tf_op jit(solution)/shard_map/ppermute | solution.py:14
  40.6 7.5 %collective-permute-start.15 = (bf16[32,1024]{1,0:T(8,128)(2,1)S(1)}, bf16[32,1024]{1,0:T(8,128)(2,1)S(1)}, u32[]{:S(2)}, u32[]{:S(2)}) collective-permute-start(bf16[32,1024]{1,0:T(8,128)(2,1)S(1)} %get-tuple-element.114), channel_id=1, source_target_pairs={{0,16},{4,20},{8,24},{12,28},{16,0},{20,4},{24,8},{28,12},{1,17},{... | collective-permute-start | bytes 196616 | tf_op jit(solution)/shard_map/ppermute | solution.py:14
  44.1 6.2 %collective-permute-start.16 = (bf16[32,1024]{1,0:T(8,128)(2,1)S(1)}, bf16[32,1024]{1,0:T(8,128)(2,1)S(1)}, u32[]{:S(2)}, u32[]{:S(2)}) collective-permute-start(bf16[32,1024]{1,0:T(8,128)(2,1)S(1)} %get-tuple-element.113), channel_id=1, source_target_pairs={{0,24},{4,28},{8,16},{12,20},{16,8},{20,12},{24,0},{28,4},{1,25},{... | collective-permute-start | bytes 196616 | tf_op jit(solution)/shard_map/ppermute | solution.py:14
  51.1 4.5 %collective-permute-start.17 = (bf16[32,1024]{1,0:T(8,128)(2,1)S(1)}, bf16[32,1024]{1,0:T(8,128)(2,1)S(1)}, u32[]{:S(2)}, u32[]{:S(2)}) collective-permute-start(bf16[32,1024]{1,0:T(8,128)(2,1)S(1)} %fusion.33), channel_id=1, source_target_pairs={{0,8},{4,12},{8,0},{12,4},{16,24},{20,28},{24,16},{28,20},{1,9},{5... | collective-permute-start | bytes 196616 | tf_op jit(solution)/shard_map/ppermute | solution.py:14
  51.9 6.7 %collective-permute-start.18 = (bf16[32,1024]{1,0:T(8,128)(2,1)S(1)}, bf16[32,1024]{1,0:T(8,128)(2,1)S(1)}, u32[]{:S(2)}, u32[]{:S(2)}) collective-permute-start(bf16[32,1024]{1,0:T(8,128)(2,1)S(1)} %fusion.33), channel_id=1, source_target_pairs={{0,16},{4,20},{8,24},{12,28},{16,0},{20,4},{24,8},{28,12},{1,17},{... | collective-permute-start | bytes 196616 | tf_op jit(solution)/shard_map/ppermute | solution.py:14
  53.6 6.2 %collective-permute-start.19 = (bf16[32,1024]{1,0:T(8,128)(2,1)S(1)}, bf16[32,1024]{1,0:T(8,128)(2,1)S(1)}, u32[]{:S(2)}, u32[]{:S(2)}) collective-permute-start(bf16[32,1024]{1,0:T(8,128)(2,1)S(1)} %fusion.33), channel_id=1, source_target_pairs={{0,24},{4,28},{8,16},{12,20},{16,8},{20,12},{24,0},{28,4},{1,25},{... | collective-permute-start | bytes 196616 | tf_op jit(solution)/shard_map/ppermute | solution.py:14
  59.8 35.2 %copy-start.3 = (bf16[36,16,512]{2,1,0:T(8,128)(2,1)}, bf16[36,16,512]{2,1,0:T(8,128)(2,1)S(1)}, u32[]{:S(2)}) copy-start(bf16[36,16,512]{2,1,0:T(8,128)(2,1)S(1)} %collective-permute-done.20.refs_1_) | copy-start | bytes 1769476
  59.9 8.6 %collective-permute-start.25 = (bf16[128,1024]{1,0:T(8,128)(2,1)S(1)}, bf16[128,1024]{1,0:T(8,128)(2,1)S(1)}, u32[]{:S(2)}, u32[]{:S(2)}) collective-permute-start(bf16[128,1024]{1,0:T(8,128)(2,1)S(1)} %pad_maximum_fusion.1.refs_0_), channel_id=1, source_target_pairs={{0,1},{1,0},{2,3},{3,2},{4,5},{5,4},{6,7},{7,6},{8,9},{9,8},{10,11... | collective-permute-start | bytes 786440 | tf_op jit(solution)/shard_map/ppermute | solution.py:14
  60.9 16.8 %collective-permute-start.22 = (bf16[128,1024]{1,0:T(8,128)(2,1)S(1)}, bf16[128,1024]{1,0:T(8,128)(2,1)S(1)}, u32[]{:S(2)}, u32[]{:S(2)}) collective-permute-start(bf16[128,1024]{1,0:T(8,128)(2,1)S(1)} %pad_maximum_fusion.1.refs_0_), channel_id=1, source_target_pairs={{0,2},{1,3},{2,0},{3,1},{4,6},{5,7},{6,4},{7,5},{8,10},{9,11},{10,... | collective-permute-start | bytes 786440 | tf_op jit(solution)/shard_map/ppermute | solution.py:14
  62.5 15.2 %collective-permute-start.23 = (bf16[128,1024]{1,0:T(8,128)(2,1)S(1)}, bf16[128,1024]{1,0:T(8,128)(2,1)S(1)}, u32[]{:S(2)}, u32[]{:S(2)}) collective-permute-start(bf16[128,1024]{1,0:T(8,128)(2,1)S(1)} %pad_maximum_fusion.1.refs_0_), channel_id=1, source_target_pairs={{0,3},{1,2},{2,1},{3,0},{4,7},{5,6},{6,5},{7,4},{8,11},{9,10},{10,... | collective-permute-start | bytes 786440 | tf_op jit(solution)/shard_map/ppermute | solution.py:14
  63.7 5.3 %collective-permute-start.24 = (bf16[128,1024]{1,0:T(8,128)(2,1)S(1)}, bf16[128,1024]{1,0:T(8,128)(2,1)S(1)}, u32[]{:S(2)}, u32[]{:S(2)}) collective-permute-start(bf16[128,1024]{1,0:T(8,128)(2,1)S(1)} %pad_maximum_fusion.1.refs_0_), channel_id=1, source_target_pairs={{0,4},{4,0},{8,12},{12,8},{16,20},{20,16},{24,28},{28,24},{1,5},{5... | collective-permute-start | bytes 786440 | tf_op jit(solution)/shard_map/ppermute | solution.py:14
  68.5 1.5 %collective-permute-start.26 = (bf16[128,1024]{1,0:T(8,128)(2,1)S(1)}, bf16[128,1024]{1,0:T(8,128)(2,1)S(1)}, u32[]{:S(2)}, u32[]{:S(2)}) collective-permute-start(bf16[128,1024]{1,0:T(8,128)(2,1)S(1)} %collective-permute-done.25.refs_2_), channel_id=1, source_target_pairs={{0,4},{4,0},{8,12},{12,8},{16,20},{20,16},{24,28},{28,24},{1,5},{5... | collective-permute-start | bytes 786440 | tf_op jit(solution)/shard_map/ppermute | solution.py:14
  77.7 4.0 %collective-permute-start.27 = (bf16[128,1024]{1,0:T(8,128)(2,1)S(1)}, bf16[128,1024]{1,0:T(8,128)(2,1)S(1)}, u32[]{:S(2)}, u32[]{:S(2)}) collective-permute-start(bf16[128,1024]{1,0:T(8,128)(2,1)S(1)} %collective-permute-done.22.refs_0_), channel_id=1, source_target_pairs={{0,4},{4,0},{8,12},{12,8},{16,20},{20,16},{24,28},{28,24},{1,5},{5... | collective-permute-start | bytes 786440 | tf_op jit(solution)/shard_map/ppermute | solution.py:14
  77.9 3.8 %collective-permute-start.28 = (bf16[128,1024]{1,0:T(8,128)(2,1)S(1)}, bf16[128,1024]{1,0:T(8,128)(2,1)}, u32[]{:S(2)}, u32[]{:S(2)}) collective-permute-start(bf16[128,1024]{1,0:T(8,128)(2,1)S(1)} %collective-permute-done.23.refs_2_), channel_id=1, source_target_pairs={{0,4},{4,0},{8,12},{12,8},{16,20},{20,16},{24,28},{28,24},{1,5},{5... | collective-permute-start | bytes 786440 | tf_op jit(solution)/shard_map/ppermute | solution.py:14
  78.3 17.8 %collective-permute-start.33 = (bf16[36,16,512]{2,1,0:T(8,128)(2,1)}, bf16[36,16,512]{2,1,0:T(8,128)(2,1)S(1)}, u32[]{:S(2)}, u32[]{:S(2)}) collective-permute-start(bf16[36,16,512]{2,1,0:T(8,128)(2,1)} %get-tuple-element.81), channel_id=1, source_target_pairs={{0,3},{1,2},{2,1},{3,0},{4,7},{5,6},{6,5},{7,4},{8,11},{9,10},{10,... | collective-permute-start | bytes 1769480 | tf_op jit(solution)/shard_map/ppermute | solution.py:14
  93.1 2.8 %collective-permute-start.29 = (bf16[128,1024]{1,0:T(8,128)(2,1)}, bf16[128,1024]{1,0:T(8,128)(2,1)S(1)}, u32[]{:S(2)}, u32[]{:S(2)}) collective-permute-start(bf16[128,1024]{1,0:T(8,128)(2,1)} %get-tuple-element.77), channel_id=1, source_target_pairs={{0,4},{4,0},{8,12},{12,8},{16,20},{20,16},{24,28},{28,24},{1,5},{5... | collective-permute-start | bytes 786440 | tf_op jit(solution)/shard_map/ppermute | solution.py:14
  93.2 2.7 %collective-permute-start.30 = (bf16[128,1024]{1,0:T(8,128)(2,1)}, bf16[128,1024]{1,0:T(8,128)(2,1)}, u32[]{:S(2)}, u32[]{:S(2)}) collective-permute-start(bf16[128,1024]{1,0:T(8,128)(2,1)} %get-tuple-element.78), channel_id=1, source_target_pairs={{0,4},{4,0},{8,12},{12,8},{16,20},{20,16},{24,28},{28,24},{1,5},{5... | collective-permute-start | bytes 786440 | tf_op jit(solution)/shard_map/ppermute | solution.py:14
  93.7 2.2 %collective-permute-start.31 = (bf16[128,1024]{1,0:T(8,128)(2,1)}, bf16[128,1024]{1,0:T(8,128)(2,1)S(1)}, u32[]{:S(2)}, u32[]{:S(2)}) collective-permute-start(bf16[128,1024]{1,0:T(8,128)(2,1)} %get-tuple-element.79), channel_id=1, source_target_pairs={{0,4},{4,0},{8,12},{12,8},{16,20},{20,16},{24,28},{28,24},{1,5},{5... | collective-permute-start | bytes 786440 | tf_op jit(solution)/shard_map/ppermute | solution.py:14
  93.8 2.3 %collective-permute-start.32 = (bf16[128,1024]{1,0:T(8,128)(2,1)}, bf16[128,1024]{1,0:T(8,128)(2,1)S(1)}, u32[]{:S(2)}, u32[]{:S(2)}) collective-permute-start(bf16[128,1024]{1,0:T(8,128)(2,1)} %get-tuple-element.80), channel_id=1, source_target_pairs={{0,4},{4,0},{8,12},{12,8},{16,20},{20,16},{24,28},{28,24},{1,5},{5... | collective-permute-start | bytes 786440 | tf_op jit(solution)/shard_map/ppermute | solution.py:14
  97.9 10.7 %collective-permute-start.34 = (bf16[128,1024]{1,0:T(8,128)(2,1)S(1)}, bf16[128,1024]{1,0:T(8,128)(2,1)S(1)}, u32[]{:S(2)}, u32[]{:S(2)}) collective-permute-start(bf16[128,1024]{1,0:T(8,128)(2,1)S(1)} %add_convert_fusion.3), channel_id=1, source_target_pairs={{0,1},{1,0},{2,3},{3,2},{4,5},{5,4},{6,7},{7,6},{8,9},{9,8},{10,11... | collective-permute-start | bytes 786440 | tf_op jit(solution)/shard_map/ppermute | solution.py:14
  100.3 13.9 %collective-permute-start.35 = (bf16[128,1024]{1,0:T(8,128)(2,1)}, bf16[128,1024]{1,0:T(8,128)(2,1)S(1)}, u32[]{:S(2)}, u32[]{:S(2)}) collective-permute-start(bf16[128,1024]{1,0:T(8,128)(2,1)} %add_convert_fusion.2), channel_id=1, source_target_pairs={{0,2},{1,3},{2,0},{3,1},{4,6},{5,7},{6,4},{7,5},{8,10},{9,11},{10,... | collective-permute-start | bytes 786440 | tf_op jit(solution)/shard_map/ppermute | solution.py:14
  102.3 11.8 %collective-permute-start.36 = (bf16[128,1024]{1,0:T(8,128)(2,1)}, bf16[128,1024]{1,0:T(8,128)(2,1)S(1)}, u32[]{:S(2)}, u32[]{:S(2)}) collective-permute-start(bf16[128,1024]{1,0:T(8,128)(2,1)} %add_convert_fusion.1), channel_id=1, source_target_pairs={{0,3},{1,2},{2,1},{3,0},{4,7},{5,6},{6,5},{7,4},{8,11},{9,10},{10,... | collective-permute-start | bytes 786440 | tf_op jit(solution)/shard_map/ppermute | solution.py:14
  115.4 4.7 %collective-permute-start.37 = (bf16[32,1024]{1,0:T(8,128)(2,1)S(1)}, bf16[32,1024]{1,0:T(8,128)(2,1)S(1)}, u32[]{:S(2)}, u32[]{:S(2)}) collective-permute-start(bf16[32,1024]{1,0:T(8,128)(2,1)S(1)} %get-tuple-element.109), channel_id=1, source_target_pairs={{0,8},{4,12},{8,0},{12,4},{16,24},{20,28},{24,16},{28,20},{1,9},{5... | collective-permute-start | bytes 196616 | tf_op jit(solution)/shard_map/ppermute | solution.py:14
  116.4 7.4 %collective-permute-start.38 = (bf16[32,1024]{1,0:T(8,128)(2,1)S(1)}, bf16[32,1024]{1,0:T(8,128)(2,1)S(1)}, u32[]{:S(2)}, u32[]{:S(2)}) collective-permute-start(bf16[32,1024]{1,0:T(8,128)(2,1)S(1)} %get-tuple-element.111), channel_id=1, source_target_pairs={{0,16},{4,20},{8,24},{12,28},{16,0},{20,4},{24,8},{28,12},{1,17},{... | collective-permute-start | bytes 196616 | tf_op jit(solution)/shard_map/ppermute | solution.py:14
  117.7 6.1 %collective-permute-start.39 = (bf16[32,1024]{1,0:T(8,128)(2,1)S(1)}, bf16[32,1024]{1,0:T(8,128)(2,1)S(1)}, u32[]{:S(2)}, u32[]{:S(2)}) collective-permute-start(bf16[32,1024]{1,0:T(8,128)(2,1)S(1)} %get-tuple-element.110), channel_id=1, source_target_pairs={{0,24},{4,28},{8,16},{12,20},{16,8},{20,12},{24,0},{28,4},{1,25},{... | collective-permute-start | bytes 196616 | tf_op jit(solution)/shard_map/ppermute | solution.py:14
  123.8 4.5 %collective-permute-start.40 = (bf16[32,1024]{1,0:T(8,128)(2,1)S(1)}, bf16[32,1024]{1,0:T(8,128)(2,1)S(1)}, u32[]{:S(2)}, u32[]{:S(2)}) collective-permute-start(bf16[32,1024]{1,0:T(8,128)(2,1)S(1)} %add_convert_fusion.5), channel_id=1, source_target_pairs={{0,8},{4,12},{8,0},{12,4},{16,24},{20,28},{24,16},{28,20},{1,9},{5... | collective-permute-start | bytes 196616 | tf_op jit(solution)/shard_map/ppermute | solution.py:14
  125.2 5.9 %collective-permute-start.41 = (bf16[32,1024]{1,0:T(8,128)(2,1)S(1)}, bf16[32,1024]{1,0:T(8,128)(2,1)S(1)}, u32[]{:S(2)}, u32[]{:S(2)}) collective-permute-start(bf16[32,1024]{1,0:T(8,128)(2,1)S(1)} %add_convert_fusion.5), channel_id=1, source_target_pairs={{0,16},{4,20},{8,24},{12,28},{16,0},{20,4},{24,8},{28,12},{1,17},{... | collective-permute-start | bytes 196616 | tf_op jit(solution)/shard_map/ppermute | solution.py:14
  126.7 6.1 %collective-permute-start.42 = (bf16[32,1024]{1,0:T(8,128)(2,1)S(1)}, bf16[32,1024]{1,0:T(8,128)(2,1)S(1)}, u32[]{:S(2)}, u32[]{:S(2)}) collective-permute-start(bf16[32,1024]{1,0:T(8,128)(2,1)S(1)} %add_convert_fusion.5), channel_id=1, source_target_pairs={{0,24},{4,28},{8,16},{12,20},{16,8},{20,12},{24,0},{28,4},{1,25},{... | collective-permute-start | bytes 196616 | tf_op jit(solution)/shard_map/ppermute | solution.py:14
  132.9 1.6 %collective-permute-start.43 = (bf16[128,1024]{1,0:T(8,128)(2,1)S(1)}, bf16[128,1024]{1,0:T(8,128)(2,1)S(1)}, u32[]{:S(2)}, u32[]{:S(2)}) collective-permute-start(bf16[128,1024]{1,0:T(8,128)(2,1)S(1)} %pad_maximum_fusion.3), channel_id=1, source_target_pairs={{0,4},{4,0},{8,12},{12,8},{16,20},{20,16},{24,28},{28,24},{1,5},{5... | collective-permute-start | bytes 786440 | tf_op jit(solution)/shard_map/ppermute | solution.py:14
  (20 other events, 165.8 us)

commit v3 on v2

--- a/solution.py
+++ b/solution.py
@@ -131,35 +131,38 @@
     )(source_rows, *parts)
 
 
-def expert_kernel(owner_ids, blocks, gains, gate_w, up_w, carry=None, down=None):
+def expert_kernel(owner_ids, first, blocks, gains, gate_w, up_w, row_weight, carry=None, down_w=None):
     half, width = blocks[0][0].shape
     rows = 2 * half
     depth, hidden_dim = gate_w.shape
     count = len(blocks)
     tile = 256
-    last = down is not None
-    out_count = down[2] if last else 0
+    last = down_w is not None
+    out_count = owner_ids.shape[0] if last else 0
 
     def kernel(ids_ref, *refs):
         block_refs, refs = refs[: 2 * count], refs[2 * count :]
-        gains_ref, gate_ref, up_ref = refs[:3]
-        refs = list(refs[3:])
+        gains_ref, gate_ref, up_ref, weight_ref = refs[:4]
+        refs = list(refs[4:])
         if carry is not None:
             gate_in, up_in, square_in = (refs.pop(0) for _ in range(3))
             gate_carry, up_carry, carry_sems = (refs.pop() for _ in range(3))
         if last:
-            down_ref, weight_ref = (refs.pop(0) for _ in range(2))
+            down_ref = refs.pop(0)
             out_refs = [refs.pop(0) for _ in range(2 * out_count)]
             hidden, down_buf, outs, tail_sems = (refs.pop() for _ in range(4))
-        gate_sum, up_sum, square, mixed, gate_buf, up_buf, sems = refs
+        gate_sum, up_sum, square, raw, raw_sems, mixed, gate_buf, up_buf, sems = refs
+
+        def fetch_block(b, h):
+            return pltpu.make_async_copy(block_refs[2 * b + h], raw.at[b, h], raw_sems.at[b, h])
 
         def fetch(b, w):
             source, buf = ((gate_ref, gate_buf), (up_ref, up_buf))[w]
-            at = pl.multiple_of(ids_ref[b] * width, width)
+            at = pl.multiple_of(ids_ref[first + b] * width, width)
             return pltpu.make_async_copy(source.at[pl.ds(at, width)], buf.at[b], sems.at[b, w])
 
         def fetch_down(k):
-            at = pl.multiple_of(ids_ref[count + k] * width, width)
+            at = pl.multiple_of(ids_ref[k] * width, width)
             return pltpu.make_async_copy(down_ref.at[:, pl.ds(at, width)], down_buf.at[k], tail_sems.at[0, k])
 
         def fetch_carry(w):
@@ -174,6 +177,10 @@
             queue.append([fetch_carry(0), fetch_carry(1)])
         queue += [[fetch_down(k)] for k in range(out_count)]
 
+        for b in range(count):
+            fetch_block(b, 0).start()
+            fetch_block(b, 1).start()
+
         def start_next():
             if queue:
                 for copy in queue.pop(0):
@@ -183,9 +190,10 @@
         start_next()
         square[...] = jnp.zeros_like(square) if carry is None else square_in[...]
         for b in range(count):
-            gain = gains_ref[ids_ref[b]]
+            gain = gains_ref[ids_ref[first + b]]
             for h in range(2):
-                values = block_refs[2 * b + h][...].astype(F32)
+                fetch_block(b, h).wait()
+                values = raw[b, h].astype(F32)
                 square[h * half : (h + 1) * half] += jnp.sum(values * values, axis=1, keepdims=True)
                 mixed[b, h * half : (h + 1) * half] = (values * gain).astype(BF16)
         for b in range(count):
@@ -228,10 +236,12 @@
 
     here = pl.BlockSpec(memory_space=pltpu.VMEM)
     anywhere = pl.BlockSpec(memory_space=pl.ANY)
-    operands = [owner_ids] + [part for block in blocks for part in block] + [gains, gate_w, up_w]
-    in_specs = [pl.BlockSpec(memory_space=pltpu.SMEM)] + [here] * (2 * count + 1) + [anywhere] * 2
+    operands = [owner_ids] + [part for block in blocks for part in block] + [gains, gate_w, up_w, row_weight]
+    in_specs = [pl.BlockSpec(memory_space=pltpu.SMEM)] + [anywhere] * (2 * count) + [here, anywhere, anywhere, here]
     sums = [(rows, hidden_dim), (rows, hidden_dim), (rows, 1)]
     scratch = [
+        pltpu.VMEM((count, 2, half, width), BF16),
+        pltpu.SemaphoreType.DMA((count, 2)),
         pltpu.VMEM((count, rows, width), BF16),
         pltpu.VMEM((count, width, hidden_dim), BF16),
         pltpu.VMEM((count, width, hidden_dim), BF16),
@@ -241,8 +251,8 @@
         operands += list(carry)
         in_specs += [anywhere, anywhere, here]
     if last:
-        operands += [down[0], down[1]]
-        in_specs += [anywhere, here]
+        operands += [down_w]
+        in_specs += [anywhere]
         out_shape = [jax.ShapeDtypeStruct((half, width), BF16)] * (2 * out_count)
         out_specs = [anywhere] * (2 * out_count)
         scratch = [pltpu.VMEM(shape, F32) for shape in sums] + scratch
@@ -270,6 +280,51 @@
         compiler_params=pltpu.CompilerParams(vmem_limit_bytes=56 * 1024 * 1024),
         name="expert_outputs" if last else "expert_sums",
     )(*operands)
+
+
+def add_pairs(lefts, rights, cut):
+    count = len(lefts)
+    rows, width = lefts[0].shape
+
+    def kernel(*refs):
+        left_refs, right_refs, out_refs = refs[:count], refs[count : 2 * count], refs[2 * count : 4 * count]
+        held, sums, in_sems, out_sems = refs[4 * count :]
+
+        def take(k, w):
+            return pltpu.make_async_copy((left_refs, right_refs)[w][k], held.at[k, w], in_sems.at[k, w])
+
+        def give(k, w):
+            part = sums.at[k, pl.ds(w * cut, rows - cut if w else cut)]
+            return pltpu.make_async_copy(part, out_refs[2 * k + w], out_sems.at[k, w])
+
+        order = range(count - 1, -1, -1)
+        for k in order:
+            take(k, 0).start()
+            take(k, 1).start()
+        for k in order:
+            take(k, 0).wait()
+            take(k, 1).wait()
+            sums[k] = (held[k, 0].astype(F32) + held[k, 1].astype(F32)).astype(BF16)
+            give(k, 0).start()
+            give(k, 1).start()
+        for k in order:
+            give(k, 0).wait()
+            give(k, 1).wait()
+
+    anywhere = pl.BlockSpec(memory_space=pl.ANY)
+    return pl.pallas_call(
+        kernel,
+        out_shape=[jax.ShapeDtypeStruct((size, width), BF16) for _ in lefts for size in (cut, rows - cut)],
+        in_specs=[anywhere] * (2 * count),
+        out_specs=[anywhere] * (2 * count),
+        scratch_shapes=[
+            pltpu.VMEM((count, 2, rows, width), BF16),
+            pltpu.VMEM((count, rows, width), BF16),
+            pltpu.SemaphoreType.DMA((count, 2)),
+            pltpu.SemaphoreType.DMA((count, 2)),
+        ],
+        name="add_pairs",
+    )(*lefts, *rights)
 
 
 def body(
@@ -306,7 +361,10 @@
     chunk = half // planes
     tap_count = conv_weight.shape[0]
 
-    conv_all = jnp.concatenate(gather_pairs(conv_input, "expert"), axis=0)
+    last = swap(jnp.concatenate([conv_input, gate_input], axis=0), "expert", owners - 1)
+    conv_all = jnp.concatenate(
+        [conv_input] + [swap(conv_input, "expert", flip) for flip in range(1, owners - 1)] + [last[:row_count]], axis=0
+    )
     my_slots = lax.dynamic_slice_in_dim(new_slot, own * row_count, row_count)
     near_ids = (
         (jnp.arange(owners) ^ own)[:, None] * row_count + jnp.arange(row_count)[None, :]
@@ -325,7 +383,9 @@
     new_slot, my_slots, gate_input, projected = lax.optimization_barrier(
         (new_slot, my_slots, gate_input, projected)
     )
-    gate_all = jnp.concatenate(gather_pairs(gate_input, "expert"), axis=0)
+    gate_all = jnp.concatenate(
+        [gate_input] + [swap(gate_input, "expert", flip) for flip in range(1, owners - 1)] + [last[row_count:]], axis=0
+    )
     projected = scatter_pairs([projected] * planes, "dp", 2)
 
     move_cap = 2 * row_count // owners
@@ -399,12 +459,14 @@
     ).reshape(-1)
     order_hot = (near_rows[:, None] == near_slots[None, :]).astype(BF16)
     gated_new = jnp.dot(order_hot, gated_all, preferred_element_type=F32).astype(BF16)
-    mix = jnp.dot(gated_new, out_proj_weight, preferred_element_type=F32)
-    width = mix.shape[1]
+    sent = jnp.dot(gated_new[half:], out_proj_weight, preferred_element_type=F32).astype(BF16)
+    gated_half, sent = lax.optimization_barrier((gated_new[:half], sent))
+    kept = jnp.dot(gated_half, out_proj_weight, preferred_element_type=F32)
+    width = kept.shape[1]
 
     now = [swap(part, "expert", flip) for flip, part in enumerate(packed[:early], 1)]
 
-    mix_half = mix[:half] + swap(mix[half:].astype(BF16), "dp", 1).astype(F32)
+    mix_half = kept + swap(sent, "dp", 1).astype(F32)
     gate_w, up_w, down_w = expert_gate[0], expert_up[0], expert_down[0]
     capacity = min(row_count, 5 * row_count * routes.shape[1] // (2 * owners))
     dense = capacity == row_count
@@ -424,7 +486,7 @@
             core == 0, jnp.concatenate([own_half, other], axis=0), jnp.concatenate([other, own_half], axis=0)
         )
 
-    def finish_states(later):
+    def finish_states(later, now):
         ssm_new = place_rows(ssm_source, [ssm_old] + now + later)
         conv_rows = [conv_keep.reshape(row_count, -1)] + [
             part[-tail_rows:].reshape(move_cap, -1) for part in now + later
@@ -451,7 +513,7 @@
             row_count,
             capacity,
         )
-        return (*finish_states(later), layer_out)
+        return (*finish_states(later, now), layer_out)
 
     blocks = gather_pairs(stream_half, "expert")
     gains = norm_gain.reshape(owners, 1, width)
@@ -461,34 +523,35 @@
         jnp.where(near_rows[:, None] == jnp.arange(rows)[None, :], row_weight[None, :], 0.0), axis=1, keepdims=True
     )
     near_weight, blocks[0] = lax.optimization_barrier((near_weight, blocks[0]))
-    pairs = [(block, swap(block, "dp", 1)) for block in blocks[:early]]
-    sums = expert_kernel(near_owners[:early], pairs, gains, gate_w, up_w)
-    last_count = owners - early
-    tied = lax.optimization_barrier((*blocks[early:], *packed[early:], *sums))
-    pairs = [(block, swap(block, "dp", 1)) for block in tied[:last_count]]
-    later = [swap(part, "expert", flip) for flip, part in enumerate(tied[last_count:-3], early + 1)]
-    outs = expert_kernel(
-        jnp.concatenate([near_owners[early:], near_owners]),
-        pairs,
-        gains,
-        gate_w,
-        up_w,
-        tied[-3:],
-        (down_w, near_weight, owners),
-    )
+    pair = (blocks[0], swap(blocks[0], "dp", 1))
+    sums = expert_kernel(near_owners, 0, [pair], gains, gate_w, up_w, near_weight)
+    tied = lax.optimization_barrier((*blocks[1:], *packed[early:], *sums))
+    pairs = [(block, swap(block, "dp", 1)) for block in tied[: owners - 1]]
+    later = [swap(part, "expert", flip) for flip, part in enumerate(tied[owners - 1 : -3], early + 1)]
+    outs = expert_kernel(near_owners, 1, pairs, gains, gate_w, up_w, near_weight, tied[-3:], down_w)
 
     others = [swap(outs[2 * k + 1], "dp", 1) for k in range(owners)]
     tied = lax.optimization_barrier((*others, *later))
     others, later = tied[:owners], list(tied[owners:])
-    own_columns = scatter_pairs(
-        [(outs[2 * k].astype(F32) + others[k].astype(F32)).astype(BF16) for k in range(owners)], "expert"
-    )
-    own_columns, *done = lax.optimization_barrier((own_columns, *finish_states(later)))
-
-    mix_rows = scatter_pairs(list(own_columns.reshape(planes, chunk, width)), "dp", 2)
+    near_planes = planes // 2
+    parts = add_pairs(outs[::2], others, near_planes * chunk)
+    arrived = [swap(parts[2 * flip + 1], "expert", flip) for flip in range(1, owners)]
+    arrived[0], *tied = lax.optimization_barrier((arrived[0], *later, *now))
+    done = finish_states(list(tied[: len(later)]), list(tied[len(later) :]))
+    *arrived, ssm_new, conv_new = lax.optimization_barrier((*arrived, *done))
+    far_sum = parts[1].astype(F32) + sum(part.astype(F32) for part in arrived)
+    far_rows = far_sum.astype(BF16).reshape(planes - near_planes, chunk, width)
+    from_far = [
+        swap(far_rows[k], "dp", 2 * (near_planes + k)).astype(F32) for k in range(planes - near_planes)
+    ]
+    arrived = [parts[0]] + [swap(parts[2 * flip], "expert", flip) for flip in range(1, owners)]
+    tied = lax.optimization_barrier((*arrived, *from_far))
+    arrived, from_far = tied[:owners], tied[owners:]
+    near_sum = sum(part.astype(F32) for part in arrived).reshape(near_planes, chunk, width)
+    mix_rows = scatter_pairs(list(near_sum), "dp", 2) + sum(from_far)
     layer_chunk = (stream_chunk.astype(F32) + mix_rows).astype(BF16)
     layer_half = jnp.concatenate(gather_pairs(layer_chunk, "dp", 2), axis=0)
-    return (*done, in_order(layer_half))
+    return (ssm_new, conv_new, in_order(layer_half))
 
 
 def solution(mesh):

time: 136 us -> 133 us (0.978)
  Pallas kernels: 24.1 us -> 27.9 us
  waiting for transfers between devices: 36.3 us -> 32.9 us
  other arithmetic: 15 us -> 12.8 us
  local copies, waits for them, and re-layouts: 9.61 us -> 7.57 us
    ppermute x44 -> x46, waiting for transfers between devices: 36.3 us -> 32.9 us  [swap(): return lax.ppermute(values, axis, [(i, i ^ flip) for i in range(size)])]
    convert_element_type x3, other arithmetic: 3.61 us -> 1 us  [the longest x1 0.98 us: body(): far_rows = far_sum.astype(BF16).reshape(planes - near_planes, chunk, width)]
    pallas_call x0 -> x1, Pallas kernels: none -> 2.61 us  [add_pairs(): pl.pallas_call(kernel, out_shape=[jax.ShapeDtypeStruct((size, width), BF1...]
    ppermute x44 -> x46, starting transfers between devices: 46.1 us -> 46.5 us  [swap(): return lax.ppermute(values, axis, [(i, i ^ flip) for i in range(size)])]
  transfers between devices with their start and end apart: 44 -> 46, of which waited for: 16 -> 20; matrix products, arithmetic and copies ran while one was open for 15% -> 13% of each run, Pallas kernels for 18% -> 19%
where the time goes in v3:
time: 133 us; the launch traced here: 132 us
  starting transfers between devices  46.5 us (35%)
  waiting for transfers between devices  32.9 us (25%)
  Pallas kernels  27.9 us (21%)
  other arithmetic  12.8 us (10%)
  local copies, waits for them, and re-layouts  7.57 us (6%)
  matrix products  3.31 us (2%)
  between operations  1.5 us (1%)
    ppermute x46, starting transfers between devices, swap(): return lax.ppermute(values, axis, [(i, i ^ flip) for i in range(size)])  46.5 us
    ppermute x46, waiting for transfers between devices, swap(): return lax.ppermute(values, axis, [(i, i ^ flip) for i in range(size)])  32.9 us
    pallas_call x2, Pallas kernels, expert_kernel(): pl.pallas_call(kernel, out_shape=out_shape, in_specs=in_specs, out_specs=...  18.8 us
    pallas_call x1, Pallas kernels, place_rows(): pl.pallas_call(kernel, out_shape=jax.ShapeDtypeStruct((row_count,) + row_...  3.63 us
    pallas_call x1, Pallas kernels, pack_rows(): pl.pallas_call(kernel, out_shape=[jax.ShapeDtypeStruct((count + (0 if tai...  2.85 us
  transfers between devices with their start and end apart: 46, of which 20 were waited for; matrix products, arithmetic and copies ran while one was open for 13% of the time, Pallas kernels for 19%

profile of v3, /device:TPU:0, one launch (start us, length us, event | category | flops | bytes accessed | tf_op | source)
XLA Modules:
  0.0 132.5 jit_solution(13133710378374189646)
XLA Ops:
  0.7 3.0 %collective-permute-start = (bf16[64,512]{1,0:T(8,128)(2,1)}, bf16[64,512]{1,0:T(8,128)(2,1)S(1)}, u32[]{:S(2)}, u32[]{:S(2)}) collective-permute-start(bf16[64,512]{1,0:T(8,128)(2,1)} %param.23), channel_id=1, source_target_pairs={{0,1},{1,0},{2,3},{3,2},{4,5},{5,4},{6,7},{7,6},{8,9},{9,8},{10,11... | collective-permute-start | bytes 196616 | tf_op jit(solution)/shard_map/ppermute | solution.py:14
  3.7 1.5 %collective-permute-start.1 = (bf16[64,512]{1,0:T(8,128)(2,1)}, bf16[64,512]{1,0:T(8,128)(2,1)S(1)}, u32[]{:S(2)}, u32[]{:S(2)}) collective-permute-start(bf16[64,512]{1,0:T(8,128)(2,1)} %param.23), channel_id=1, source_target_pairs={{0,2},{1,3},{2,0},{3,1},{4,6},{5,7},{6,4},{7,5},{8,10},{9,11},{10,... | collective-permute-start | bytes 196616 | tf_op jit(solution)/shard_map/ppermute | solution.py:14
  5.2 0.9 pad_maximum_fusion.5
  7.0 0.9 slice_bitcast_fusion
  9.6 1.0 multiply_reduce_fusion.1
  10.6 1.4 %collective-permute-done.2 = bf16[128,512]{1,0:T(8,128)(2,1)S(1)} collective-permute-done((bf16[128,512]{1,0:T(8,128)(2,1)S(1)}, bf16[128,512]{1,0:T(8,128)(2,1)S(1)}, u32[]{:S(2)}, u32[]{:S(2)}) %collective-permute-start.2) | collective-permute-done | bytes 131104 | tf_op jit(solution)/shard_map/ppermute | solution.py:14
  12.1 1.1 multiply_convert_fusion
  13.7 1.1 collective-permute-done.3
  14.8 1.6 %collective-permute-start.4 = (bf16[64,288]{1,0:T(8,128)(2,1)S(1)}, bf16[64,288]{1,0:T(8,128)(2,1)S(1)}, u32[]{:S(2)}, u32[]{:S(2)}) collective-permute-start(bf16[64,288]{1,0:T(8,128)(2,1)S(1)} %convert_element_type.127), channel_id=1, source_target_pairs={{0,8},{4,12},{8,0},{12,4},{16,24},{20,28},{24,16},{28,20},{1,9},{5... | collective-permute-start | bytes 110600 | tf_op jit(solution)/shard_map/ppermute | solution.py:14
  16.5 2.6 %collective-permute-start.5 = (bf16[64,288]{1,0:T(8,128)(2,1)S(1)}, bf16[64,288]{1,0:T(8,128)(2,1)S(1)}, u32[]{:S(2)}, u32[]{:S(2)}) collective-permute-start(bf16[64,288]{1,0:T(8,128)(2,1)S(1)} %convert_element_type.127), channel_id=1, source_target_pairs={{0,16},{4,20},{8,24},{12,28},{16,0},{20,4},{24,8},{28,12},{1,17},{... | collective-permute-start | bytes 110600 | tf_op jit(solution)/shard_map/ppermute | solution.py:14
  19.8 1.5 %collective-permute-start.8 = (bf16[64,512]{1,0:T(8,128)(2,1)S(1)}, bf16[64,512]{1,0:T(8,128)(2,1)S(1)}, u32[]{:S(2)}, u32[]{:S(2)}) collective-permute-start(bf16[64,512]{1,0:T(8,128)(2,1)S(1)} %copy-done.18), channel_id=1, source_target_pairs={{0,2},{1,3},{2,0},{3,1},{4,6},{5,7},{6,4},{7,5},{8,10},{9,11},{10,... | collective-permute-start | bytes 196616 | tf_op jit(solution)/shard_map/ppermute | solution.py:14
  25.5 0.9 multiply_reduce_fusion
  27.4 1.4 %collective-permute-start.11 = (bf16[64,512]{1,0:T(8,128)(2,1)S(1)}, bf16[64,512]{1,0:T(8,128)(2,1)S(1)}, u32[]{:S(2)}, u32[]{:S(2)}) collective-permute-start(bf16[64,512]{1,0:T(8,128)(2,1)S(1)} %fusion.27), channel_id=1, source_target_pairs={{0,3},{1,2},{2,1},{3,0},{4,7},{5,6},{6,5},{7,4},{8,11},{9,10},{10,... | collective-permute-start | bytes 196616 | tf_op jit(solution)/shard_map/ppermute | solution.py:14
  28.8 1.5 %collective-permute-start.9 = (bf16[64,512]{1,0:T(8,128)(2,1)S(1)}, bf16[64,512]{1,0:T(8,128)(2,1)S(1)}, u32[]{:S(2)}, u32[]{:S(2)}) collective-permute-start(bf16[64,512]{1,0:T(8,128)(2,1)S(1)} %fusion.27), channel_id=1, source_target_pairs={{0,1},{1,0},{2,3},{3,2},{4,5},{5,4},{6,7},{7,6},{8,9},{9,8},{10,11... | collective-permute-start | bytes 196616 | tf_op jit(solution)/shard_map/ppermute | solution.py:14
  30.3 1.6 %add_convert_fusion.states_ref.refs_0_ = bf16[64,16,512]{2,1,0:T(8,128)(2,1)} fusion(bf16[64,16,512]{2,1,0:T(8,128)(2,1)S(1)} %copy-done.1, f32[64,16]{1,0:T(8,128)S(1)} %get-tuple-element.80, f32[64,512]{1,0:T(8,128)S(1)} %convert_multiply_fusion, f32[16,512]{1,0:T(8,128)S(1)} %exponential_negate_fusion, f32[64,512]{1,0:T(8,128)S(1)} %get-tuple-element.77), kind=kLoop, calls=%fused_computation | loop fusion | flops 3145728 | bytes 2396160 | tf_op jit(solution)/shard_map/convert_element_type | solution.py:444
  31.9 2.8 %pack_rows.1 = (bf16[36,16,512]{2,1,0:T(8,128)(2,1)}, bf16[36,16,512]{2,1,0:T(8,128)(2,1)}, bf16[36,16,512]{2,1,0:T(8,128)(2,1)}) custom-call(s32[128]{0:T(128)} %select_reduce_fusion.1.rows_ref, bf16[64,16,512]{2,1,0:T(8,128)(2,1)} %add_convert_fusion.states_ref.refs_0_, bf16[4,16,512]{2,1,0:T(8,128)(2,1)} %squeeze.33.refs_0_, ...), custom_call_target="tpu_custom_call" | custom-call | tf_op jit(solution)/shard_map/pack_rows/pallas_call | solution.py:86
  36.1 1.5 %collective-permute-start.20 = (bf16[36,16,512]{2,1,0:T(8,128)(2,1)}, bf16[36,16,512]{2,1,0:T(8,128)(2,1)S(1)}, u32[]{:S(2)}, u32[]{:S(2)}) collective-permute-start(bf16[36,16,512]{2,1,0:T(8,128)(2,1)} %get-tuple-element.88), channel_id=1, source_target_pairs={{0,2},{1,3},{2,0},{3,1},{4,6},{5,7},{6,4},{7,5},{8,10},{9,11},{10,... | collective-permute-start | bytes 1769480 | tf_op jit(solution)/shard_map/ppermute | solution.py:14
  38.6 3.5 %collective-permute-start.14 = (bf16[32,1024]{1,0:T(8,128)(2,1)S(1)}, bf16[32,1024]{1,0:T(8,128)(2,1)S(1)}, u32[]{:S(2)}, u32[]{:S(2)}) collective-permute-start(bf16[32,1024]{1,0:T(8,128)(2,1)S(1)} %get-tuple-element.157), channel_id=1, source_target_pairs={{0,16},{4,20},{8,24},{12,28},{16,0},{20,4},{24,8},{28,12},{1,17},{... | collective-permute-start | bytes 196616 | tf_op jit(solution)/shard_map/ppermute | solution.py:14
  42.5 4.2 %collective-permute-done.14 = bf16[32,1024]{1,0:T(8,128)(2,1)S(1)} collective-permute-done((bf16[32,1024]{1,0:T(8,128)(2,1)S(1)}, bf16[32,1024]{1,0:T(8,128)(2,1)S(1)}, u32[]{:S(2)}, u32[]{:S(2)}) %collective-permute-start.14) | collective-permute-done | bytes 65568 | tf_op jit(solution)/shard_map/ppermute | solution.py:14
  46.7 1.5 %collective-permute-done.15 = bf16[32,1024]{1,0:T(8,128)(2,1)S(1)} collective-permute-done((bf16[32,1024]{1,0:T(8,128)(2,1)S(1)}, bf16[32,1024]{1,0:T(8,128)(2,1)S(1)}, u32[]{:S(2)}, u32[]{:S(2)}) %collective-permute-start.15) | collective-permute-done | bytes 65568 | tf_op jit(solution)/shard_map/ppermute | solution.py:14
  48.2 0.9 fusion.34
  49.1 2.3 %collective-permute-start.17 = (bf16[32,1024]{1,0:T(8,128)(2,1)S(1)}, bf16[32,1024]{1,0:T(8,128)(2,1)S(1)}, u32[]{:S(2)}, u32[]{:S(2)}) collective-permute-start(bf16[32,1024]{1,0:T(8,128)(2,1)S(1)} %fusion.34), channel_id=1, source_target_pairs={{0,16},{4,20},{8,24},{12,28},{16,0},{20,4},{24,8},{28,12},{1,17},{... | collective-permute-start | bytes 196616 | tf_op jit(solution)/shard_map/ppermute | solution.py:14
  51.4 2.1 %collective-permute-start.18 = (bf16[32,1024]{1,0:T(8,128)(2,1)S(1)}, bf16[32,1024]{1,0:T(8,128)(2,1)S(1)}, u32[]{:S(2)}, u32[]{:S(2)}) collective-permute-start(bf16[32,1024]{1,0:T(8,128)(2,1)S(1)} %fusion.34), channel_id=1, source_target_pairs={{0,24},{4,28},{8,16},{12,20},{16,8},{20,12},{24,0},{28,4},{1,25},{... | collective-permute-start | bytes 196616 | tf_op jit(solution)/shard_map/ppermute | solution.py:14
  53.7 2.3 %collective-permute-done.17 = bf16[32,1024]{1,0:T(8,128)(2,1)S(1)} collective-permute-done((bf16[32,1024]{1,0:T(8,128)(2,1)S(1)}, bf16[32,1024]{1,0:T(8,128)(2,1)S(1)}, u32[]{:S(2)}, u32[]{:S(2)}) %collective-permute-start.17) | collective-permute-done | bytes 65568 | tf_op jit(solution)/shard_map/ppermute | solution.py:14
  55.9 1.5 %collective-permute-done.18 = bf16[32,1024]{1,0:T(8,128)(2,1)S(1)} collective-permute-done((bf16[32,1024]{1,0:T(8,128)(2,1)S(1)}, bf16[32,1024]{1,0:T(8,128)(2,1)S(1)}, u32[]{:S(2)}, u32[]{:S(2)}) %collective-permute-start.18) | collective-permute-done | bytes 65568 | tf_op jit(solution)/shard_map/ppermute | solution.py:14
  58.2 1.5 %collective-permute-start.22 = (bf16[128,1024]{1,0:T(8,128)(2,1)S(1)}, bf16[128,1024]{1,0:T(8,128)(2,1)}, u32[]{:S(2)}, u32[]{:S(2)}) collective-permute-start(bf16[128,1024]{1,0:T(8,128)(2,1)S(1)} %pad_maximum_fusion.1.refs_0_), channel_id=1, source_target_pairs={{0,2},{1,3},{2,0},{3,1},{4,6},{5,7},{6,4},{7,5},{8,10},{9,11},{10,... | collective-permute-start | bytes 786440 | tf_op jit(solution)/shard_map/ppermute | solution.py:14
  59.7 1.4 %collective-permute-start.23 = (bf16[128,1024]{1,0:T(8,128)(2,1)S(1)}, bf16[128,1024]{1,0:T(8,128)(2,1)}, u32[]{:S(2)}, u32[]{:S(2)}) collective-permute-start(bf16[128,1024]{1,0:T(8,128)(2,1)S(1)} %pad_maximum_fusion.1.refs_0_), channel_id=1, source_target_pairs={{0,3},{1,2},{2,1},{3,0},{4,7},{5,6},{6,5},{7,4},{8,11},{9,10},{10,... | collective-permute-start | bytes 786440 | tf_op jit(solution)/shard_map/ppermute | solution.py:14
  63.2 5.6 %expert_sums.1 = (f32[256,896]{1,0:T(8,128)}, f32[256,896]{1,0:T(8,128)}, f32[256,1]{1,0:T(8,128)}) custom-call(s32[4]{0:T(128)} %iota_xor_fusion.ids_ref, bf16[128,1024]{1,0:T(8,128)(2,1)} %copy-done.2, bf16[128,1024]{1,0:T(8,128)(2,1)} %copy-done.11, f32[4,1,1024]{2,1,0:T(1,128)} %bitcast.50, bf16[4096,896]{1,0:T(8,128)(2,1)} %bitcast.36, ...), custom_call_target="tpu_custom_call" | custom-call | tf_op jit(solution)/shard_map/expert_sums/pallas_call | solution.py:274
  68.8 3.5 %collective-permute-done.22.refs_2_ = bf16[128,1024]{1,0:T(8,128)(2,1)} collective-permute-done((bf16[128,1024]{1,0:T(8,128)(2,1)S(1)}, bf16[128,1024]{1,0:T(8,128)(2,1)}, u32[]{:S(2)}, u32[]{:S(2)}) %collective-permute-start.22) | collective-permute-done | bytes 262176 | tf_op jit(solution)/shard_map/ppermute | solution.py:14
  72.8 1.5 %collective-permute-start.32 = (bf16[36,16,512]{2,1,0:T(8,128)(2,1)}, bf16[36,16,512]{2,1,0:T(8,128)(2,1)S(1)}, u32[]{:S(2)}, u32[]{:S(2)}) collective-permute-start(bf16[36,16,512]{2,1,0:T(8,128)(2,1)} %get-tuple-element.110), channel_id=1, source_target_pairs={{0,3},{1,2},{2,1},{3,0},{4,7},{5,6},{6,5},{7,4},{8,11},{9,10},{10,... | collective-permute-start | bytes 1769480 | tf_op jit(solution)/shard_map/ppermute | solution.py:14
  75.5 13.2 %expert_outputs.1 = (bf16[128,1024]{1,0:T(8,128)(2,1)}, bf16[128,1024]{1,0:T(8,128)(2,1)}, bf16[128,1024]{1,0:T(8,128)(2,1)}, bf16[128,1024]{1,0:T(8,128)(2,1)},...) custom-call(s32[4]{0:T(128)} %iota_xor_fusion.ids_ref, ...), custom_call_target="tpu_custom_call" | custom-call | tf_op jit(solution)/shard_map/expert_outputs/pallas_call | solution.py:274
  91.8 2.6 %add_pairs.1 = (bf16[64,1024]{1,0:T(8,128)(2,1)}, bf16[64,1024]{1,0:T(8,128)(2,1)}, bf16[64,1024]{1,0:T(8,128)(2,1)}, bf16[64,1024]{1,0:T(8,128)(2,1)}, bf16[64,...) custom-call(bf16[128,1024]{1,0:T(8,128)(2,1)} %get-tuple-element.102.refs_0_, ...), custom_call_target="tpu_custom_call" | custom-call | tf_op jit(solution)/shard_map/add_pairs/pallas_call | solution.py:315
  94.4 1.6 %collective-permute-start.33 = (bf16[64,1024]{1,0:T(8,128)(2,1)}, bf16[64,1024]{1,0:T(8,128)(2,1)S(1)}, u32[]{:S(2)}, u32[]{:S(2)}) collective-permute-start(bf16[64,1024]{1,0:T(8,128)(2,1)} %get-tuple-element.115), channel_id=1, source_target_pairs={{0,1},{1,0},{2,3},{3,2},{4,5},{5,4},{6,7},{7,6},{8,9},{9,8},{10,11... | collective-permute-start | bytes 393224 | tf_op jit(solution)/shard_map/ppermute | solution.py:14
  97.3 1.4 %collective-permute-start.35 = (bf16[64,1024]{1,0:T(8,128)(2,1)}, bf16[64,1024]{1,0:T(8,128)(2,1)}, u32[]{:S(2)}, u32[]{:S(2)}) collective-permute-start(bf16[64,1024]{1,0:T(8,128)(2,1)} %get-tuple-element.121), channel_id=1, source_target_pairs={{0,3},{1,2},{2,1},{3,0},{4,7},{5,6},{6,5},{7,4},{8,11},{9,10},{10,... | collective-permute-start | bytes 393224 | tf_op jit(solution)/shard_map/ppermute | solution.py:14
  98.7 1.5 %collective-permute-start.36 = (bf16[64,1024]{1,0:T(8,128)(2,1)}, bf16[64,1024]{1,0:T(8,128)(2,1)}, u32[]{:S(2)}, u32[]{:S(2)}) collective-permute-start(bf16[64,1024]{1,0:T(8,128)(2,1)} %get-tuple-element.128), channel_id=1, source_target_pairs={{0,1},{1,0},{2,3},{3,2},{4,5},{5,4},{6,7},{7,6},{8,9},{9,8},{10,11... | collective-permute-start | bytes 393224 | tf_op jit(solution)/shard_map/ppermute | solution.py:14
  100.7 1.4 %collective-permute-start.38 = (bf16[64,1024]{1,0:T(8,128)(2,1)}, bf16[64,1024]{1,0:T(8,128)(2,1)}, u32[]{:S(2)}, u32[]{:S(2)}) collective-permute-start(bf16[64,1024]{1,0:T(8,128)(2,1)} %get-tuple-element.130), channel_id=1, source_target_pairs={{0,3},{1,2},{2,1},{3,0},{4,7},{5,6},{6,5},{7,4},{8,11},{9,10},{10,... | collective-permute-start | bytes 393224 | tf_op jit(solution)/shard_map/ppermute | solution.py:14
  102.6 3.6 %place_rows.1 = bf16[64,16,512]{2,1,0:T(8,128)(2,1)} custom-call(s32[64]{0:T(128)} %get-tuple-element.142.rows_ref, bf16[64,16,512]{2,1,0:T(8,128)(2,1)} %add_convert_fusion.states_ref.refs_0_, bf16[36,16,512]{2,1,0:T(8,128)(2,1)} %copy-done.3, bf16[36,16,512]{2,1,0:T(8,128)(2,1)} %copy-done.4, bf16[36,16,512]{2,1,0:T(8,128)(2,1)} %copy-done.5), custom_call_target="tpu_custom_call" | custom-call | tf_op jit(solution)/shard_map/place_rows/pallas_call | solution.py:121
  107.0 1.0 add_convert_fusion.1
  108.0 1.4 %collective-permute-start.39 = (bf16[32,1024]{1,0:T(8,128)(2,1)S(1)}, bf16[32,1024]{1,0:T(8,128)(2,1)S(1)}, u32[]{:S(2)}, u32[]{:S(2)}) collective-permute-start(bf16[32,1024]{1,0:T(8,128)(2,1)S(1)} %get-tuple-element.162), channel_id=1, source_target_pairs={{0,16},{4,20},{8,24},{12,28},{16,0},{20,4},{24,8},{28,12},{1,17},{... | collective-permute-start | bytes 196616 | tf_op jit(solution)/shard_map/ppermute | solution.py:14
  109.4 0.9 collective-permute-start.40
  110.3 3.6 %collective-permute-done.39 = bf16[32,1024]{1,0:T(8,128)(2,1)S(1)} collective-permute-done((bf16[32,1024]{1,0:T(8,128)(2,1)S(1)}, bf16[32,1024]{1,0:T(8,128)(2,1)S(1)}, u32[]{:S(2)}, u32[]{:S(2)}) %collective-permute-start.39) | collective-permute-done | bytes 65568 | tf_op jit(solution)/shard_map/ppermute | solution.py:14
  114.0 1.5 %collective-permute-done.40 = bf16[32,1024]{1,0:T(8,128)(2,1)S(1)} collective-permute-done((bf16[32,1024]{1,0:T(8,128)(2,1)S(1)}, bf16[32,1024]{1,0:T(8,128)(2,1)S(1)}, u32[]{:S(2)}, u32[]{:S(2)}) %collective-permute-start.40) | collective-permute-done | bytes 65568 | tf_op jit(solution)/shard_map/ppermute | solution.py:14
  115.5 1.1 convert_add_fusion.1
  116.7 4.9 %collective-permute-done.41 = bf16[32,1024]{1,0:T(8,128)(2,1)S(1)} collective-permute-done((bf16[32,1024]{1,0:T(8,128)(2,1)S(1)}, bf16[32,1024]{1,0:T(8,128)(2,1)S(1)}, u32[]{:S(2)}, u32[]{:S(2)}) %collective-permute-start.41) | collective-permute-done | bytes 65568 | tf_op jit(solution)/shard_map/ppermute | solution.py:14
  121.7 2.0 %collective-permute-start.43 = (bf16[32,1024]{1,0:T(8,128)(2,1)S(1)}, bf16[32,1024]{1,0:T(8,128)(2,1)S(1)}, u32[]{:S(2)}, u32[]{:S(2)}) collective-permute-start(bf16[32,1024]{1,0:T(8,128)(2,1)S(1)} %fusion.30), channel_id=1, source_target_pairs={{0,16},{4,20},{8,24},{12,28},{16,0},{20,4},{24,8},{28,12},{1,17},{... | collective-permute-start | bytes 196616 | tf_op jit(solution)/shard_map/ppermute | solution.py:14
  123.7 2.4 %collective-permute-start.44 = (bf16[32,1024]{1,0:T(8,128)(2,1)S(1)}, bf16[32,1024]{1,0:T(8,128)(2,1)S(1)}, u32[]{:S(2)}, u32[]{:S(2)}) collective-permute-start(bf16[32,1024]{1,0:T(8,128)(2,1)S(1)} %fusion.30), channel_id=1, source_target_pairs={{0,24},{4,28},{8,16},{12,20},{16,8},{20,12},{24,0},{28,4},{1,25},{... | collective-permute-start | bytes 196616 | tf_op jit(solution)/shard_map/ppermute | solution.py:14
  127.0 2.8 %collective-permute-done.44 = bf16[32,1024]{1,0:T(8,128)(2,1)S(1)} collective-permute-done((bf16[32,1024]{1,0:T(8,128)(2,1)S(1)}, bf16[32,1024]{1,0:T(8,128)(2,1)S(1)}, u32[]{:S(2)}, u32[]{:S(2)}) %collective-permute-start.44) | collective-permute-done | bytes 65568 | tf_op jit(solution)/shard_map/ppermute | solution.py:14
  130.0 1.5 %collective-permute-done.45 = bf16[128,1024]{1,0:T(8,128)(2,1)S(1)} collective-permute-done((bf16[128,1024]{1,0:T(8,128)(2,1)S(1)}, bf16[128,1024]{1,0:T(8,128)(2,1)S(1)}, u32[]{:S(2)}, u32[]{:S(2)}) %collective-permute-start.45) | collective-permute-done | bytes 262176 | tf_op jit(solution)/shard_map/ppermute | solution.py:14
  (188 shorter events, 24.2 us)
Async XLA Ops:
  0.7 11.4 %collective-permute-start = (bf16[64,512]{1,0:T(8,128)(2,1)}, bf16[64,512]{1,0:T(8,128)(2,1)S(1)}, u32[]{:S(2)}, u32[]{:S(2)}) collective-permute-start(bf16[64,512]{1,0:T(8,128)(2,1)} %param.23), channel_id=1, source_target_pairs={{0,1},{1,0},{2,3},{3,2},{4,5},{5,4},{6,7},{7,6},{8,9},{9,8},{10,11... | collective-permute-start | bytes 196616 | tf_op jit(solution)/shard_map/ppermute | solution.py:14
  3.7 8.4 %collective-permute-start.1 = (bf16[64,512]{1,0:T(8,128)(2,1)}, bf16[64,512]{1,0:T(8,128)(2,1)S(1)}, u32[]{:S(2)}, u32[]{:S(2)}) collective-permute-start(bf16[64,512]{1,0:T(8,128)(2,1)} %param.23), channel_id=1, source_target_pairs={{0,2},{1,3},{2,0},{3,1},{4,6},{5,7},{6,4},{7,5},{8,10},{9,11},{10,... | collective-permute-start | bytes 196616 | tf_op jit(solution)/shard_map/ppermute | solution.py:14
  6.1 5.9 %collective-permute-start.2 = (bf16[128,512]{1,0:T(8,128)(2,1)S(1)}, bf16[128,512]{1,0:T(8,128)(2,1)S(1)}, u32[]{:S(2)}, u32[]{:S(2)}) collective-permute-start(bf16[128,512]{1,0:T(8,128)(2,1)S(1)} %pad_maximum_fusion.5), channel_id=1, source_target_pairs={{0,3},{1,2},{2,1},{3,0},{4,7},{5,6},{6,5},{7,4},{8,11},{9,10},{10,... | collective-permute-start | bytes 393224 | tf_op jit(solution)/shard_map/ppermute | solution.py:14
  13.4 1.4 %collective-permute-start.3 = (f32[64,288]{1,0:T(8,128)S(1)}, f32[64,288]{1,0:T(8,128)S(1)}, u32[]{:S(2)}, u32[]{:S(2)}) collective-permute-start(f32[64,288]{1,0:T(8,128)S(1)} %fusion.67), channel_id=1, source_target_pairs={{0,4},{4,0},{8,12},{12,8},{16,20},{20,16},{24,28},{28,24},{1,5},{5... | collective-permute-start | bytes 221192 | tf_op jit(solution)/shard_map/ppermute | solution.py:14
  14.8 10.0 %collective-permute-start.4 = (bf16[64,288]{1,0:T(8,128)(2,1)S(1)}, bf16[64,288]{1,0:T(8,128)(2,1)S(1)}, u32[]{:S(2)}, u32[]{:S(2)}) collective-permute-start(bf16[64,288]{1,0:T(8,128)(2,1)S(1)} %convert_element_type.127), channel_id=1, source_target_pairs={{0,8},{4,12},{8,0},{12,4},{16,24},{20,28},{24,16},{28,20},{1,9},{5... | collective-permute-start | bytes 110600 | tf_op jit(solution)/shard_map/ppermute | solution.py:14
  16.5 8.4 %collective-permute-start.5 = (bf16[64,288]{1,0:T(8,128)(2,1)S(1)}, bf16[64,288]{1,0:T(8,128)(2,1)S(1)}, u32[]{:S(2)}, u32[]{:S(2)}) collective-permute-start(bf16[64,288]{1,0:T(8,128)(2,1)S(1)} %convert_element_type.127), channel_id=1, source_target_pairs={{0,16},{4,20},{8,24},{12,28},{16,0},{20,4},{24,8},{28,12},{1,17},{... | collective-permute-start | bytes 110600 | tf_op jit(solution)/shard_map/ppermute | solution.py:14
  19.1 5.9 %collective-permute-start.6 = (bf16[64,288]{1,0:T(8,128)(2,1)S(1)}, bf16[64,288]{1,0:T(8,128)(2,1)S(1)}, u32[]{:S(2)}, u32[]{:S(2)}) collective-permute-start(bf16[64,288]{1,0:T(8,128)(2,1)S(1)} %convert_element_type.127), channel_id=1, source_target_pairs={{0,24},{4,28},{8,16},{12,20},{16,8},{20,12},{24,0},{28,4},{1,25},{... | collective-permute-start | bytes 110600 | tf_op jit(solution)/shard_map/ppermute | solution.py:14
  19.3 7.1 %collective-permute-start.7 = (bf16[64,512]{1,0:T(8,128)(2,1)S(1)}, bf16[64,512]{1,0:T(8,128)(2,1)S(1)}, u32[]{:S(2)}, u32[]{:S(2)}) collective-permute-start(bf16[64,512]{1,0:T(8,128)(2,1)S(1)} %copy-done.18), channel_id=1, source_target_pairs={{0,1},{1,0},{2,3},{3,2},{4,5},{5,4},{6,7},{7,6},{8,9},{9,8},{10,11... | collective-permute-start | bytes 196616 | tf_op jit(solution)/shard_map/ppermute | solution.py:14
  19.8 6.6 %collective-permute-start.8 = (bf16[64,512]{1,0:T(8,128)(2,1)S(1)}, bf16[64,512]{1,0:T(8,128)(2,1)S(1)}, u32[]{:S(2)}, u32[]{:S(2)}) collective-permute-start(bf16[64,512]{1,0:T(8,128)(2,1)S(1)} %copy-done.18), channel_id=1, source_target_pairs={{0,2},{1,3},{2,0},{3,1},{4,6},{5,7},{6,4},{7,5},{8,10},{9,11},{10,... | collective-permute-start | bytes 196616 | tf_op jit(solution)/shard_map/ppermute | solution.py:14
  26.7 8.0 %collective-permute-start.10 = (bf16[64,512]{1,0:T(8,128)(2,1)S(1)}, bf16[64,512]{1,0:T(8,128)(2,1)S(1)}, u32[]{:S(2)}, u32[]{:S(2)}) collective-permute-start(bf16[64,512]{1,0:T(8,128)(2,1)S(1)} %fusion.27), channel_id=1, source_target_pairs={{0,2},{1,3},{2,0},{3,1},{4,6},{5,7},{6,4},{7,5},{8,10},{9,11},{10,... | collective-permute-start | bytes 196616 | tf_op jit(solution)/shard_map/ppermute | solution.py:14
  27.4 7.4 %collective-permute-start.11 = (bf16[64,512]{1,0:T(8,128)(2,1)S(1)}, bf16[64,512]{1,0:T(8,128)(2,1)S(1)}, u32[]{:S(2)}, u32[]{:S(2)}) collective-permute-start(bf16[64,512]{1,0:T(8,128)(2,1)S(1)} %fusion.27), channel_id=1, source_target_pairs={{0,3},{1,2},{2,1},{3,0},{4,7},{5,6},{6,5},{7,4},{8,11},{9,10},{10,... | collective-permute-start | bytes 196616 | tf_op jit(solution)/shard_map/ppermute | solution.py:14
  28.8 6.0 %collective-permute-start.9 = (bf16[64,512]{1,0:T(8,128)(2,1)S(1)}, bf16[64,512]{1,0:T(8,128)(2,1)S(1)}, u32[]{:S(2)}, u32[]{:S(2)}) collective-permute-start(bf16[64,512]{1,0:T(8,128)(2,1)S(1)} %fusion.27), channel_id=1, source_target_pairs={{0,1},{1,0},{2,3},{3,2},{4,5},{5,4},{6,7},{7,6},{8,9},{9,8},{10,11... | collective-permute-start | bytes 196616 | tf_op jit(solution)/shard_map/ppermute | solution.py:14
  35.4 2.2 %collective-permute-start.12 = (bf16[128,1024]{1,0:T(8,128)(2,1)S(1)}, bf16[128,1024]{1,0:T(8,128)(2,1)S(1)}, u32[]{:S(2)}, u32[]{:S(2)}) collective-permute-start(bf16[128,1024]{1,0:T(8,128)(2,1)S(1)} %convolution_convert_fusion), channel_id=1, source_target_pairs={{0,4},{4,0},{8,12},{12,8},{16,20},{20,16},{24,28},{28,24},{1,5},{5... | collective-permute-start | bytes 786440 | tf_op jit(solution)/shard_map/ppermute | solution.py:14
  35.5 22.0 %collective-permute-start.19 = (bf16[36,16,512]{2,1,0:T(8,128)(2,1)}, bf16[36,16,512]{2,1,0:T(8,128)(2,1)S(1)}, u32[]{:S(2)}, u32[]{:S(2)}) collective-permute-start(bf16[36,16,512]{2,1,0:T(8,128)(2,1)} %get-tuple-element.87), channel_id=1, source_target_pairs={{0,1},{1,0},{2,3},{3,2},{4,5},{5,4},{6,7},{7,6},{8,9},{9,8},{10,11... | collective-permute-start | bytes 1769480 | tf_op jit(solution)/shard_map/ppermute | solution.py:14
  36.1 21.4 %collective-permute-start.20 = (bf16[36,16,512]{2,1,0:T(8,128)(2,1)}, bf16[36,16,512]{2,1,0:T(8,128)(2,1)S(1)}, u32[]{:S(2)}, u32[]{:S(2)}) collective-permute-start(bf16[36,16,512]{2,1,0:T(8,128)(2,1)} %get-tuple-element.88), channel_id=1, source_target_pairs={{0,2},{1,3},{2,0},{3,1},{4,6},{5,7},{6,4},{7,5},{8,10},{9,11},{10,... | collective-permute-start | bytes 1769480 | tf_op jit(solution)/shard_map/ppermute | solution.py:14
  38.0 4.5 %collective-permute-start.13 = (bf16[32,1024]{1,0:T(8,128)(2,1)S(1)}, bf16[32,1024]{1,0:T(8,128)(2,1)S(1)}, u32[]{:S(2)}, u32[]{:S(2)}) collective-permute-start(bf16[32,1024]{1,0:T(8,128)(2,1)S(1)} %get-tuple-element.155), channel_id=1, source_target_pairs={{0,8},{4,12},{8,0},{12,4},{16,24},{20,28},{24,16},{28,20},{1,9},{5... | collective-permute-start | bytes 196616 | tf_op jit(solution)/shard_map/ppermute | solution.py:14
  38.6 8.1 %collective-permute-start.14 = (bf16[32,1024]{1,0:T(8,128)(2,1)S(1)}, bf16[32,1024]{1,0:T(8,128)(2,1)S(1)}, u32[]{:S(2)}, u32[]{:S(2)}) collective-permute-start(bf16[32,1024]{1,0:T(8,128)(2,1)S(1)} %get-tuple-element.157), channel_id=1, source_target_pairs={{0,16},{4,20},{8,24},{12,28},{16,0},{20,4},{24,8},{28,12},{1,17},{... | collective-permute-start | bytes 196616 | tf_op jit(solution)/shard_map/ppermute | solution.py:14
  42.1 6.1 %collective-permute-start.15 = (bf16[32,1024]{1,0:T(8,128)(2,1)S(1)}, bf16[32,1024]{1,0:T(8,128)(2,1)S(1)}, u32[]{:S(2)}, u32[]{:S(2)}) collective-permute-start(bf16[32,1024]{1,0:T(8,128)(2,1)S(1)} %get-tuple-element.156), channel_id=1, source_target_pairs={{0,24},{4,28},{8,16},{12,20},{16,8},{20,12},{24,0},{28,4},{1,25},{... | collective-permute-start | bytes 196616 | tf_op jit(solution)/shard_map/ppermute | solution.py:14
  49.0 4.6 %collective-permute-start.16 = (bf16[32,1024]{1,0:T(8,128)(2,1)S(1)}, bf16[32,1024]{1,0:T(8,128)(2,1)S(1)}, u32[]{:S(2)}, u32[]{:S(2)}) collective-permute-start(bf16[32,1024]{1,0:T(8,128)(2,1)S(1)} %fusion.34), channel_id=1, source_target_pairs={{0,8},{4,12},{8,0},{12,4},{16,24},{20,28},{24,16},{28,20},{1,9},{5... | collective-permute-start | bytes 196616 | tf_op jit(solution)/shard_map/ppermute | solution.py:14
  49.1 6.8 %collective-permute-start.17 = (bf16[32,1024]{1,0:T(8,128)(2,1)S(1)}, bf16[32,1024]{1,0:T(8,128)(2,1)S(1)}, u32[]{:S(2)}, u32[]{:S(2)}) collective-permute-start(bf16[32,1024]{1,0:T(8,128)(2,1)S(1)} %fusion.34), channel_id=1, source_target_pairs={{0,16},{4,20},{8,24},{12,28},{16,0},{20,4},{24,8},{28,12},{1,17},{... | collective-permute-start | bytes 196616 | tf_op jit(solution)/shard_map/ppermute | solution.py:14
  51.4 6.1 %collective-permute-start.18 = (bf16[32,1024]{1,0:T(8,128)(2,1)S(1)}, bf16[32,1024]{1,0:T(8,128)(2,1)S(1)}, u32[]{:S(2)}, u32[]{:S(2)}) collective-permute-start(bf16[32,1024]{1,0:T(8,128)(2,1)S(1)} %fusion.34), channel_id=1, source_target_pairs={{0,24},{4,28},{8,16},{12,20},{16,8},{20,12},{24,0},{28,4},{1,25},{... | collective-permute-start | bytes 196616 | tf_op jit(solution)/shard_map/ppermute | solution.py:14
  57.5 44.7 %copy-start.3 = (bf16[36,16,512]{2,1,0:T(8,128)(2,1)}, bf16[36,16,512]{2,1,0:T(8,128)(2,1)S(1)}, u32[]{:S(2)}) copy-start(bf16[36,16,512]{2,1,0:T(8,128)(2,1)S(1)} %collective-permute-done.19.refs_1_) | copy-start | bytes 1769476
  57.5 44.7 %copy-start.4 = (bf16[36,16,512]{2,1,0:T(8,128)(2,1)}, bf16[36,16,512]{2,1,0:T(8,128)(2,1)S(1)}, u32[]{:S(2)}) copy-start(bf16[36,16,512]{2,1,0:T(8,128)(2,1)S(1)} %collective-permute-done.20.refs_2_) | copy-start | bytes 1769476
  57.5 4.9 %collective-permute-start.24 = (bf16[128,1024]{1,0:T(8,128)(2,1)S(1)}, bf16[128,1024]{1,0:T(8,128)(2,1)S(1)}, u32[]{:S(2)}, u32[]{:S(2)}) collective-permute-start(bf16[128,1024]{1,0:T(8,128)(2,1)S(1)} %pad_maximum_fusion.1.refs_0_), channel_id=1, source_target_pairs={{0,4},{4,0},{8,12},{12,8},{16,20},{20,16},{24,28},{28,24},{1,5},{5... | collective-permute-start | bytes 786440 | tf_op jit(solution)/shard_map/ppermute | solution.py:14
  57.6 11.1 %collective-permute-start.21 = (bf16[128,1024]{1,0:T(8,128)(2,1)S(1)}, bf16[128,1024]{1,0:T(8,128)(2,1)S(1)}, u32[]{:S(2)}, u32[]{:S(2)}) collective-permute-start(bf16[128,1024]{1,0:T(8,128)(2,1)S(1)} %pad_maximum_fusion.1.refs_0_), channel_id=1, source_target_pairs={{0,1},{1,0},{2,3},{3,2},{4,5},{5,4},{6,7},{7,6},{8,9},{9,8},{10,11... | collective-permute-start | bytes 786440 | tf_op jit(solution)/shard_map/ppermute | solution.py:14
  58.2 14.1 %collective-permute-start.22 = (bf16[128,1024]{1,0:T(8,128)(2,1)S(1)}, bf16[128,1024]{1,0:T(8,128)(2,1)}, u32[]{:S(2)}, u32[]{:S(2)}) collective-permute-start(bf16[128,1024]{1,0:T(8,128)(2,1)S(1)} %pad_maximum_fusion.1.refs_0_), channel_id=1, source_target_pairs={{0,2},{1,3},{2,0},{3,1},{4,6},{5,7},{6,4},{7,5},{8,10},{9,11},{10,... | collective-permute-start | bytes 786440 | tf_op jit(solution)/shard_map/ppermute | solution.py:14
  59.7 12.6 %collective-permute-start.23 = (bf16[128,1024]{1,0:T(8,128)(2,1)S(1)}, bf16[128,1024]{1,0:T(8,128)(2,1)}, u32[]{:S(2)}, u32[]{:S(2)}) collective-permute-start(bf16[128,1024]{1,0:T(8,128)(2,1)S(1)} %pad_maximum_fusion.1.refs_0_), channel_id=1, source_target_pairs={{0,3},{1,2},{2,1},{3,0},{4,7},{5,6},{6,5},{7,4},{8,11},{9,10},{10,... | collective-permute-start | bytes 786440 | tf_op jit(solution)/shard_map/ppermute | solution.py:14
  72.3 2.0 %collective-permute-start.25 = (bf16[128,1024]{1,0:T(8,128)(2,1)S(1)}, bf16[128,1024]{1,0:T(8,128)(2,1)S(1)}, u32[]{:S(2)}, u32[]{:S(2)}) collective-permute-start(bf16[128,1024]{1,0:T(8,128)(2,1)S(1)} %collective-permute-done.21.refs_0_), channel_id=1, source_target_pairs={{0,4},{4,0},{8,12},{12,8},{16,20},{20,16},{24,28},{28,24},{1,5},{5... | collective-permute-start | bytes 786440 | tf_op jit(solution)/shard_map/ppermute | solution.py:14
  72.3 2.1 %collective-permute-start.26 = (bf16[128,1024]{1,0:T(8,128)(2,1)}, bf16[128,1024]{1,0:T(8,128)(2,1)S(1)}, u32[]{:S(2)}, u32[]{:S(2)}) collective-permute-start(bf16[128,1024]{1,0:T(8,128)(2,1)} %collective-permute-done.22.refs_2_), channel_id=1, source_target_pairs={{0,4},{4,0},{8,12},{12,8},{16,20},{20,16},{24,28},{28,24},{1,5},{5... | collective-permute-start | bytes 786440 | tf_op jit(solution)/shard_map/ppermute | solution.py:14
  72.8 2.0 %collective-permute-start.27 = (bf16[128,1024]{1,0:T(8,128)(2,1)}, bf16[128,1024]{1,0:T(8,128)(2,1)S(1)}, u32[]{:S(2)}, u32[]{:S(2)}) collective-permute-start(bf16[128,1024]{1,0:T(8,128)(2,1)} %collective-permute-done.23.refs_4_), channel_id=1, source_target_pairs={{0,4},{4,0},{8,12},{12,8},{16,20},{20,16},{24,28},{28,24},{1,5},{5... | collective-permute-start | bytes 786440 | tf_op jit(solution)/shard_map/ppermute | solution.py:14
  72.8 19.0 %collective-permute-start.32 = (bf16[36,16,512]{2,1,0:T(8,128)(2,1)}, bf16[36,16,512]{2,1,0:T(8,128)(2,1)S(1)}, u32[]{:S(2)}, u32[]{:S(2)}) collective-permute-start(bf16[36,16,512]{2,1,0:T(8,128)(2,1)} %get-tuple-element.110), channel_id=1, source_target_pairs={{0,3},{1,2},{2,1},{3,0},{4,7},{5,6},{6,5},{7,4},{8,11},{9,10},{10,... | collective-permute-start | bytes 1769480 | tf_op jit(solution)/shard_map/ppermute | solution.py:14
  88.7 1.8 %collective-permute-start.28 = (bf16[128,1024]{1,0:T(8,128)(2,1)}, bf16[128,1024]{1,0:T(8,128)(2,1)S(1)}, u32[]{:S(2)}, u32[]{:S(2)}) collective-permute-start(bf16[128,1024]{1,0:T(8,128)(2,1)} %get-tuple-element.106), channel_id=1, source_target_pairs={{0,4},{4,0},{8,12},{12,8},{16,20},{20,16},{24,28},{28,24},{1,5},{5... | collective-permute-start | bytes 786440 | tf_op jit(solution)/shard_map/ppermute | solution.py:14
  88.9 2.0 %collective-permute-start.29 = (bf16[128,1024]{1,0:T(8,128)(2,1)}, bf16[128,1024]{1,0:T(8,128)(2,1)S(1)}, u32[]{:S(2)}, u32[]{:S(2)}) collective-permute-start(bf16[128,1024]{1,0:T(8,128)(2,1)} %get-tuple-element.107), channel_id=1, source_target_pairs={{0,4},{4,0},{8,12},{12,8},{16,20},{20,16},{24,28},{28,24},{1,5},{5... | collective-permute-start | bytes 786440 | tf_op jit(solution)/shard_map/ppermute | solution.py:14
  89.3 2.1 %collective-permute-start.30 = (bf16[128,1024]{1,0:T(8,128)(2,1)}, bf16[128,1024]{1,0:T(8,128)(2,1)}, u32[]{:S(2)}, u32[]{:S(2)}) collective-permute-start(bf16[128,1024]{1,0:T(8,128)(2,1)} %get-tuple-element.108), channel_id=1, source_target_pairs={{0,4},{4,0},{8,12},{12,8},{16,20},{20,16},{24,28},{28,24},{1,5},{5... | collective-permute-start | bytes 786440 | tf_op jit(solution)/shard_map/ppermute | solution.py:14
  89.4 2.4 %collective-permute-start.31 = (bf16[128,1024]{1,0:T(8,128)(2,1)}, bf16[128,1024]{1,0:T(8,128)(2,1)}, u32[]{:S(2)}, u32[]{:S(2)}) collective-permute-start(bf16[128,1024]{1,0:T(8,128)(2,1)} %get-tuple-element.109), channel_id=1, source_target_pairs={{0,4},{4,0},{8,12},{12,8},{16,20},{20,16},{24,28},{28,24},{1,5},{5... | collective-permute-start | bytes 786440 | tf_op jit(solution)/shard_map/ppermute | solution.py:14
  94.4 6.3 %collective-permute-start.33 = (bf16[64,1024]{1,0:T(8,128)(2,1)}, bf16[64,1024]{1,0:T(8,128)(2,1)S(1)}, u32[]{:S(2)}, u32[]{:S(2)}) collective-permute-start(bf16[64,1024]{1,0:T(8,128)(2,1)} %get-tuple-element.115), channel_id=1, source_target_pairs={{0,1},{1,0},{2,3},{3,2},{4,5},{5,4},{6,7},{7,6},{8,9},{9,8},{10,11... | collective-permute-start | bytes 393224 | tf_op jit(solution)/shard_map/ppermute | solution.py:14
  96.7 10.3 %collective-permute-start.34 = (bf16[64,1024]{1,0:T(8,128)(2,1)}, bf16[64,1024]{1,0:T(8,128)(2,1)S(1)}, u32[]{:S(2)}, u32[]{:S(2)}) collective-permute-start(bf16[64,1024]{1,0:T(8,128)(2,1)} %get-tuple-element.120), channel_id=1, source_target_pairs={{0,2},{1,3},{2,0},{3,1},{4,6},{5,7},{6,4},{7,5},{8,10},{9,11},{10,... | collective-permute-start | bytes 393224 | tf_op jit(solution)/shard_map/ppermute | solution.py:14
  97.3 9.7 %collective-permute-start.35 = (bf16[64,1024]{1,0:T(8,128)(2,1)}, bf16[64,1024]{1,0:T(8,128)(2,1)}, u32[]{:S(2)}, u32[]{:S(2)}) collective-permute-start(bf16[64,1024]{1,0:T(8,128)(2,1)} %get-tuple-element.121), channel_id=1, source_target_pairs={{0,3},{1,2},{2,1},{3,0},{4,7},{5,6},{6,5},{7,4},{8,11},{9,10},{10,... | collective-permute-start | bytes 393224 | tf_op jit(solution)/shard_map/ppermute | solution.py:14
  98.7 16.8 %collective-permute-start.36 = (bf16[64,1024]{1,0:T(8,128)(2,1)}, bf16[64,1024]{1,0:T(8,128)(2,1)}, u32[]{:S(2)}, u32[]{:S(2)}) collective-permute-start(bf16[64,1024]{1,0:T(8,128)(2,1)} %get-tuple-element.128), channel_id=1, source_target_pairs={{0,1},{1,0},{2,3},{3,2},{4,5},{5,4},{6,7},{7,6},{8,9},{9,8},{10,11... | collective-permute-start | bytes 393224 | tf_op jit(solution)/shard_map/ppermute | solution.py:14
  100.2 15.3 %collective-permute-start.37 = (bf16[64,1024]{1,0:T(8,128)(2,1)}, bf16[64,1024]{1,0:T(8,128)(2,1)}, u32[]{:S(2)}, u32[]{:S(2)}) collective-permute-start(bf16[64,1024]{1,0:T(8,128)(2,1)} %get-tuple-element.129), channel_id=1, source_target_pairs={{0,2},{1,3},{2,0},{3,1},{4,6},{5,7},{6,4},{7,5},{8,10},{9,11},{10,... | collective-permute-start | bytes 393224 | tf_op jit(solution)/shard_map/ppermute | solution.py:14
  100.7 14.8 %collective-permute-start.38 = (bf16[64,1024]{1,0:T(8,128)(2,1)}, bf16[64,1024]{1,0:T(8,128)(2,1)}, u32[]{:S(2)}, u32[]{:S(2)}) collective-permute-start(bf16[64,1024]{1,0:T(8,128)(2,1)} %get-tuple-element.130), channel_id=1, source_target_pairs={{0,3},{1,2},{2,1},{3,0},{4,7},{5,6},{6,5},{7,4},{8,11},{9,10},{10,... | collective-permute-start | bytes 393224 | tf_op jit(solution)/shard_map/ppermute | solution.py:14
  108.0 6.0 %collective-permute-start.39 = (bf16[32,1024]{1,0:T(8,128)(2,1)S(1)}, bf16[32,1024]{1,0:T(8,128)(2,1)S(1)}, u32[]{:S(2)}, u32[]{:S(2)}) collective-permute-start(bf16[32,1024]{1,0:T(8,128)(2,1)S(1)} %get-tuple-element.162), channel_id=1, source_target_pairs={{0,16},{4,20},{8,24},{12,28},{16,0},{20,4},{24,8},{28,12},{1,17},{... | collective-permute-start | bytes 196616 | tf_op jit(solution)/shard_map/ppermute | solution.py:14
  109.4 6.1 %collective-permute-start.40 = (bf16[32,1024]{1,0:T(8,128)(2,1)S(1)}, bf16[32,1024]{1,0:T(8,128)(2,1)S(1)}, u32[]{:S(2)}, u32[]{:S(2)}) collective-permute-start(bf16[32,1024]{1,0:T(8,128)(2,1)S(1)} %get-tuple-element.161), channel_id=1, source_target_pairs={{0,24},{4,28},{8,16},{12,20},{16,8},{20,12},{24,0},{28,4},{1,25},{... | collective-permute-start | bytes 196616 | tf_op jit(solution)/shard_map/ppermute | solution.py:14
  116.7 4.9 %collective-permute-start.41 = (bf16[32,1024]{1,0:T(8,128)(2,1)S(1)}, bf16[32,1024]{1,0:T(8,128)(2,1)S(1)}, u32[]{:S(2)}, u32[]{:S(2)}) collective-permute-start(bf16[32,1024]{1,0:T(8,128)(2,1)S(1)} %unstack.53), channel_id=1, source_target_pairs={{0,8},{4,12},{8,0},{12,4},{16,24},{20,28},{24,16},{28,20},{1,9},{5... | collective-permute-start | bytes 196616 | tf_op jit(solution)/shard_map/ppermute | solution.py:14
  121.6 4.5 %collective-permute-start.42 = (bf16[32,1024]{1,0:T(8,128)(2,1)S(1)}, bf16[32,1024]{1,0:T(8,128)(2,1)S(1)}, u32[]{:S(2)}, u32[]{:S(2)}) collective-permute-start(bf16[32,1024]{1,0:T(8,128)(2,1)S(1)} %fusion.30), channel_id=1, source_target_pairs={{0,8},{4,12},{8,0},{12,4},{16,24},{20,28},{24,16},{28,20},{1,9},{5... | collective-permute-start | bytes 196616 | tf_op jit(solution)/shard_map/ppermute | solution.py:14
  121.7 5.2 %collective-permute-start.43 = (bf16[32,1024]{1,0:T(8,128)(2,1)S(1)}, bf16[32,1024]{1,0:T(8,128)(2,1)S(1)}, u32[]{:S(2)}, u32[]{:S(2)}) collective-permute-start(bf16[32,1024]{1,0:T(8,128)(2,1)S(1)} %fusion.30), channel_id=1, source_target_pairs={{0,16},{4,20},{8,24},{12,28},{16,0},{20,4},{24,8},{28,12},{1,17},{... | collective-permute-start | bytes 196616 | tf_op jit(solution)/shard_map/ppermute | solution.py:14
  123.7 6.1 %collective-permute-start.44 = (bf16[32,1024]{1,0:T(8,128)(2,1)S(1)}, bf16[32,1024]{1,0:T(8,128)(2,1)S(1)}, u32[]{:S(2)}, u32[]{:S(2)}) collective-permute-start(bf16[32,1024]{1,0:T(8,128)(2,1)S(1)} %fusion.30), channel_id=1, source_target_pairs={{0,24},{4,28},{8,16},{12,20},{16,8},{20,12},{24,0},{28,4},{1,25},{... | collective-permute-start | bytes 196616 | tf_op jit(solution)/shard_map/ppermute | solution.py:14
  129.9 1.6 %collective-permute-start.45 = (bf16[128,1024]{1,0:T(8,128)(2,1)S(1)}, bf16[128,1024]{1,0:T(8,128)(2,1)S(1)}, u32[]{:S(2)}, u32[]{:S(2)}) collective-permute-start(bf16[128,1024]{1,0:T(8,128)(2,1)S(1)} %pad_maximum_fusion.3), channel_id=1, source_target_pairs={{0,4},{4,0},{8,12},{12,8},{16,20},{20,16},{24,28},{28,24},{1,5},{5... | collective-permute-start | bytes 786440 | tf_op jit(solution)/shard_map/ppermute | solution.py:14
  (22 other events, 191.5 us)

commit v4 on v3

--- a/solution.py
+++ b/solution.py
@@ -128,7 +128,7 @@
             pltpu.SemaphoreType.DMA((len(parts),)),
         ],
         name="place_rows",
-    )(source_rows, *parts)
+    )(source_rows, *[pltpu.with_memory_space_constraint(part, pltpu.HBM) for part in parts])
 
 
 def expert_kernel(owner_ids, first, blocks, gains, gate_w, up_w, row_weight, carry=None, down_w=None):
@@ -253,8 +253,8 @@
     if last:
         operands += [down_w]
         in_specs += [anywhere]
-        out_shape = [jax.ShapeDtypeStruct((half, width), BF16)] * (2 * out_count)
-        out_specs = [anywhere] * (2 * out_count)
+        out_shape = [pltpu.HBM((half, width), BF16)] * (2 * out_count)
+        out_specs = [pl.BlockSpec(memory_space=pltpu.HBM)] * (2 * out_count)
         scratch = [pltpu.VMEM(shape, F32) for shape in sums] + scratch
         scratch += [
             pltpu.SemaphoreType.DMA((3, out_count)),
@@ -277,7 +277,7 @@
         in_specs=in_specs,
         out_specs=out_specs,
         scratch_shapes=scratch,
-        compiler_params=pltpu.CompilerParams(vmem_limit_bytes=56 * 1024 * 1024),
+        compiler_params=pltpu.CompilerParams(vmem_limit_bytes=50 * 1024 * 1024),
         name="expert_outputs" if last else "expert_sums",
     )(*operands)
 

time: 133 us -> 130 us (0.977)
  waiting for transfers between devices: 32.9 us -> 36.7 us
  Pallas kernels: 27.9 us -> 24.5 us
  other arithmetic: 12.8 us -> 10.5 us
    ppermute x46, waiting for transfers between devices: 32.9 us -> 36.7 us  [swap(): return lax.ppermute(values, axis, [(i, i ^ flip) for i in range(size)])]
    pallas_call x2, Pallas kernels: 18.8 us -> 15.4 us  [expert_kernel(): pl.pallas_call(kernel, out_shape=out_shape, in_specs=in_specs, out_specs=...]
  transfers between devices with their start and end apart: 46 -> 46, of which waited for: 20 -> 20; matrix products, arithmetic and copies ran while one was open for 13% -> 12% of each run, Pallas kernels for 19% -> 17%
where the time goes in v4:
time: 130 us; the launch traced here: 129 us
  starting transfers between devices  46.4 us (36%)
  waiting for transfers between devices  36.7 us (28%)
  Pallas kernels  24.5 us (19%)
  other arithmetic  10.5 us (8%)
  local copies, waits for them, and re-layouts  6.4 us (5%)
  matrix products  3.31 us (3%)
  between operations  1.5 us (1%)
    ppermute x46, starting transfers between devices, swap(): return lax.ppermute(values, axis, [(i, i ^ flip) for i in range(size)])  46.4 us
    ppermute x46, waiting for transfers between devices, swap(): return lax.ppermute(values, axis, [(i, i ^ flip) for i in range(size)])  36.7 us
    pallas_call x2, Pallas kernels, expert_kernel(): pl.pallas_call(kernel, out_shape=out_shape, in_specs=in_specs, out_specs=...  15.4 us
    pallas_call x1, Pallas kernels, place_rows(): pl.pallas_call(kernel, out_shape=jax.ShapeDtypeStruct((row_count,) + row_...  3.63 us
    pallas_call x1, Pallas kernels, pack_rows(): pl.pallas_call(kernel, out_shape=[jax.ShapeDtypeStruct((count + (0 if tai...  2.85 us
  transfers between devices with their start and end apart: 46, of which 20 were waited for; matrix products, arithmetic and copies ran while one was open for 12% of the time, Pallas kernels for 17%

profile of v4, /device:TPU:0, one launch (start us, length us, event | category | flops | bytes accessed | tf_op | source)
XLA Modules:
  0.0 129.3 jit_solution(520861600072797478)
XLA Ops:
  0.7 3.0 %collective-permute-start = (bf16[64,512]{1,0:T(8,128)(2,1)}, bf16[64,512]{1,0:T(8,128)(2,1)S(1)}, u32[]{:S(2)}, u32[]{:S(2)}) collective-permute-start(bf16[64,512]{1,0:T(8,128)(2,1)} %param.23), channel_id=1, source_target_pairs={{0,1},{1,0},{2,3},{3,2},{4,5},{5,4},{6,7},{7,6},{8,9},{9,8},{10,11... | collective-permute-start | bytes 196616 | tf_op jit(solution)/shard_map/ppermute | solution.py:14
  3.7 1.5 %collective-permute-start.1 = (bf16[64,512]{1,0:T(8,128)(2,1)}, bf16[64,512]{1,0:T(8,128)(2,1)S(1)}, u32[]{:S(2)}, u32[]{:S(2)}) collective-permute-start(bf16[64,512]{1,0:T(8,128)(2,1)} %param.23), channel_id=1, source_target_pairs={{0,2},{1,3},{2,0},{3,1},{4,6},{5,7},{6,4},{7,5},{8,10},{9,11},{10,... | collective-permute-start | bytes 196616 | tf_op jit(solution)/shard_map/ppermute | solution.py:14
  5.2 0.9 pad_maximum_fusion.5
  7.0 0.9 slice_bitcast_fusion
  9.6 1.0 multiply_reduce_fusion.1
  10.6 1.4 %collective-permute-done.2 = bf16[128,512]{1,0:T(8,128)(2,1)S(1)} collective-permute-done((bf16[128,512]{1,0:T(8,128)(2,1)S(1)}, bf16[128,512]{1,0:T(8,128)(2,1)S(1)}, u32[]{:S(2)}, u32[]{:S(2)}) %collective-permute-start.2) | collective-permute-done | bytes 131104 | tf_op jit(solution)/shard_map/ppermute | solution.py:14
  12.1 1.1 multiply_convert_fusion
  13.7 1.1 collective-permute-done.3
  14.8 1.6 %collective-permute-start.4 = (bf16[64,288]{1,0:T(8,128)(2,1)S(1)}, bf16[64,288]{1,0:T(8,128)(2,1)S(1)}, u32[]{:S(2)}, u32[]{:S(2)}) collective-permute-start(bf16[64,288]{1,0:T(8,128)(2,1)S(1)} %convert_element_type.127), channel_id=1, source_target_pairs={{0,8},{4,12},{8,0},{12,4},{16,24},{20,28},{24,16},{28,20},{1,9},{5... | collective-permute-start | bytes 110600 | tf_op jit(solution)/shard_map/ppermute | solution.py:14
  16.5 2.6 %collective-permute-start.5 = (bf16[64,288]{1,0:T(8,128)(2,1)S(1)}, bf16[64,288]{1,0:T(8,128)(2,1)S(1)}, u32[]{:S(2)}, u32[]{:S(2)}) collective-permute-start(bf16[64,288]{1,0:T(8,128)(2,1)S(1)} %convert_element_type.127), channel_id=1, source_target_pairs={{0,16},{4,20},{8,24},{12,28},{16,0},{20,4},{24,8},{28,12},{1,17},{... | collective-permute-start | bytes 110600 | tf_op jit(solution)/shard_map/ppermute | solution.py:14
  19.8 1.5 %collective-permute-start.8 = (bf16[64,512]{1,0:T(8,128)(2,1)S(1)}, bf16[64,512]{1,0:T(8,128)(2,1)S(1)}, u32[]{:S(2)}, u32[]{:S(2)}) collective-permute-start(bf16[64,512]{1,0:T(8,128)(2,1)S(1)} %copy-done.14), channel_id=1, source_target_pairs={{0,2},{1,3},{2,0},{3,1},{4,6},{5,7},{6,4},{7,5},{8,10},{9,11},{10,... | collective-permute-start | bytes 196616 | tf_op jit(solution)/shard_map/ppermute | solution.py:14
  25.5 0.9 multiply_reduce_fusion
  27.4 1.4 %collective-permute-start.11 = (bf16[64,512]{1,0:T(8,128)(2,1)S(1)}, bf16[64,512]{1,0:T(8,128)(2,1)S(1)}, u32[]{:S(2)}, u32[]{:S(2)}) collective-permute-start(bf16[64,512]{1,0:T(8,128)(2,1)S(1)} %fusion.27), channel_id=1, source_target_pairs={{0,3},{1,2},{2,1},{3,0},{4,7},{5,6},{6,5},{7,4},{8,11},{9,10},{10,... | collective-permute-start | bytes 196616 | tf_op jit(solution)/shard_map/ppermute | solution.py:14
  28.8 1.5 %collective-permute-start.9 = (bf16[64,512]{1,0:T(8,128)(2,1)S(1)}, bf16[64,512]{1,0:T(8,128)(2,1)S(1)}, u32[]{:S(2)}, u32[]{:S(2)}) collective-permute-start(bf16[64,512]{1,0:T(8,128)(2,1)S(1)} %fusion.27), channel_id=1, source_target_pairs={{0,1},{1,0},{2,3},{3,2},{4,5},{5,4},{6,7},{7,6},{8,9},{9,8},{10,11... | collective-permute-start | bytes 196616 | tf_op jit(solution)/shard_map/ppermute | solution.py:14
  30.3 1.6 %add_convert_fusion.states_ref.refs_0_ = bf16[64,16,512]{2,1,0:T(8,128)(2,1)} fusion(bf16[64,16,512]{2,1,0:T(8,128)(2,1)S(1)} %copy-done.2, f32[64,16]{1,0:T(8,128)S(1)} %get-tuple-element.80, f32[64,512]{1,0:T(8,128)S(1)} %convert_multiply_fusion, f32[16,512]{1,0:T(8,128)S(1)} %exponential_negate_fusion, f32[64,512]{1,0:T(8,128)S(1)} %get-tuple-element.77), kind=kLoop, calls=%fused_computation | loop fusion | flops 3145728 | bytes 2396160 | tf_op jit(solution)/shard_map/convert_element_type | solution.py:444
  31.9 2.9 %pack_rows.1 = (bf16[36,16,512]{2,1,0:T(8,128)(2,1)}, bf16[36,16,512]{2,1,0:T(8,128)(2,1)}, bf16[36,16,512]{2,1,0:T(8,128)(2,1)}) custom-call(s32[128]{0:T(128)} %select_reduce_fusion.1.rows_ref, bf16[64,16,512]{2,1,0:T(8,128)(2,1)} %add_convert_fusion.states_ref.refs_0_, bf16[4,16,512]{2,1,0:T(8,128)(2,1)} %squeeze.33.refs_0_, ...), custom_call_target="tpu_custom_call" | custom-call | tf_op jit(solution)/shard_map/pack_rows/pallas_call | solution.py:86
  36.2 1.5 %collective-permute-start.20 = (bf16[36,16,512]{2,1,0:T(8,128)(2,1)}, bf16[36,16,512]{2,1,0:T(8,128)(2,1)S(1)}, u32[]{:S(2)}, u32[]{:S(2)}) collective-permute-start(bf16[36,16,512]{2,1,0:T(8,128)(2,1)} %get-tuple-element.88), channel_id=1, source_target_pairs={{0,2},{1,3},{2,0},{3,1},{4,6},{5,7},{6,4},{7,5},{8,10},{9,11},{10,... | collective-permute-start | bytes 1769480 | tf_op jit(solution)/shard_map/ppermute | solution.py:14
  38.7 3.5 %collective-permute-start.14 = (bf16[32,1024]{1,0:T(8,128)(2,1)S(1)}, bf16[32,1024]{1,0:T(8,128)(2,1)S(1)}, u32[]{:S(2)}, u32[]{:S(2)}) collective-permute-start(bf16[32,1024]{1,0:T(8,128)(2,1)S(1)} %get-tuple-element.157), channel_id=1, source_target_pairs={{0,16},{4,20},{8,24},{12,28},{16,0},{20,4},{24,8},{28,12},{1,17},{... | collective-permute-start | bytes 196616 | tf_op jit(solution)/shard_map/ppermute | solution.py:14
  42.5 4.3 %collective-permute-done.14 = bf16[32,1024]{1,0:T(8,128)(2,1)S(1)} collective-permute-done((bf16[32,1024]{1,0:T(8,128)(2,1)S(1)}, bf16[32,1024]{1,0:T(8,128)(2,1)S(1)}, u32[]{:S(2)}, u32[]{:S(2)}) %collective-permute-start.14) | collective-permute-done | bytes 65568 | tf_op jit(solution)/shard_map/ppermute | solution.py:14
  46.8 1.5 %collective-permute-done.15 = bf16[32,1024]{1,0:T(8,128)(2,1)S(1)} collective-permute-done((bf16[32,1024]{1,0:T(8,128)(2,1)S(1)}, bf16[32,1024]{1,0:T(8,128)(2,1)S(1)}, u32[]{:S(2)}, u32[]{:S(2)}) %collective-permute-start.15) | collective-permute-done | bytes 65568 | tf_op jit(solution)/shard_map/ppermute | solution.py:14
  48.3 0.9 fusion.34
  49.2 2.3 %collective-permute-start.17 = (bf16[32,1024]{1,0:T(8,128)(2,1)S(1)}, bf16[32,1024]{1,0:T(8,128)(2,1)S(1)}, u32[]{:S(2)}, u32[]{:S(2)}) collective-permute-start(bf16[32,1024]{1,0:T(8,128)(2,1)S(1)} %fusion.34), channel_id=1, source_target_pairs={{0,16},{4,20},{8,24},{12,28},{16,0},{20,4},{24,8},{28,12},{1,17},{... | collective-permute-start | bytes 196616 | tf_op jit(solution)/shard_map/ppermute | solution.py:14
  51.5 2.1 %collective-permute-start.18 = (bf16[32,1024]{1,0:T(8,128)(2,1)S(1)}, bf16[32,1024]{1,0:T(8,128)(2,1)S(1)}, u32[]{:S(2)}, u32[]{:S(2)}) collective-permute-start(bf16[32,1024]{1,0:T(8,128)(2,1)S(1)} %fusion.34), channel_id=1, source_target_pairs={{0,24},{4,28},{8,16},{12,20},{16,8},{20,12},{24,0},{28,4},{1,25},{... | collective-permute-start | bytes 196616 | tf_op jit(solution)/shard_map/ppermute | solution.py:14
  53.8 2.3 %collective-permute-done.17 = bf16[32,1024]{1,0:T(8,128)(2,1)S(1)} collective-permute-done((bf16[32,1024]{1,0:T(8,128)(2,1)S(1)}, bf16[32,1024]{1,0:T(8,128)(2,1)S(1)}, u32[]{:S(2)}, u32[]{:S(2)}) %collective-permute-start.17) | collective-permute-done | bytes 65568 | tf_op jit(solution)/shard_map/ppermute | solution.py:14
  56.1 1.5 %collective-permute-done.18 = bf16[32,1024]{1,0:T(8,128)(2,1)S(1)} collective-permute-done((bf16[32,1024]{1,0:T(8,128)(2,1)S(1)}, bf16[32,1024]{1,0:T(8,128)(2,1)S(1)}, u32[]{:S(2)}, u32[]{:S(2)}) %collective-permute-start.18) | collective-permute-done | bytes 65568 | tf_op jit(solution)/shard_map/ppermute | solution.py:14
  57.6 0.9 copy-done.4
  59.0 1.5 %collective-permute-start.22 = (bf16[128,1024]{1,0:T(8,128)(2,1)S(1)}, bf16[128,1024]{1,0:T(8,128)(2,1)S(1)}, u32[]{:S(2)}, u32[]{:S(2)}) collective-permute-start(bf16[128,1024]{1,0:T(8,128)(2,1)S(1)} %pad_maximum_fusion.1.refs_0_), channel_id=1, source_target_pairs={{0,2},{1,3},{2,0},{3,1},{4,6},{5,7},{6,4},{7,5},{8,10},{9,11},{10,... | collective-permute-start | bytes 786440 | tf_op jit(solution)/shard_map/ppermute | solution.py:14
  60.6 1.4 %collective-permute-start.23 = (bf16[128,1024]{1,0:T(8,128)(2,1)S(1)}, bf16[128,1024]{1,0:T(8,128)(2,1)S(1)}, u32[]{:S(2)}, u32[]{:S(2)}) collective-permute-start(bf16[128,1024]{1,0:T(8,128)(2,1)S(1)} %pad_maximum_fusion.1.refs_0_), channel_id=1, source_target_pairs={{0,3},{1,2},{2,1},{3,0},{4,7},{5,6},{6,5},{7,4},{8,11},{9,10},{10,... | collective-permute-start | bytes 786440 | tf_op jit(solution)/shard_map/ppermute | solution.py:14
  62.2 3.9 %expert_sums.1 = (f32[256,896]{1,0:T(8,128)S(1)}, f32[256,896]{1,0:T(8,128)S(1)}, f32[256,1]{1,0:T(8,128)S(1)}) custom-call(s32[4]{0:T(128)S(1)} %iota_xor_fusion.ids_ref, bf16[128,1024]{1,0:T(8,128)(2,1)S(1)} %pad_maximum_fusion.1.refs_0_, bf16[128,1024]{1,0:T(8,128)(2,1)S(1)} %collective-permute-done.24.refs_1_, f32[4,1,1024]{2,1,0:T(1,128)S(1)} %bitcast.36, ...), custom_call_target="tpu_custom_call" | custom-call | tf_op jit(solution)/shard_map/expert_sums/pallas_call | solution.py:274
  66.1 1.5 %collective-permute-done.21.refs_0_ = bf16[128,1024]{1,0:T(8,128)(2,1)S(1)} collective-permute-done((bf16[128,1024]{1,0:T(8,128)(2,1)S(1)}, bf16[128,1024]{1,0:T(8,128)(2,1)S(1)}, u32[]{:S(2)}, u32[]{:S(2)}) %collective-permute-start.21) | collective-permute-done | bytes 262176 | tf_op jit(solution)/shard_map/ppermute | solution.py:14
  67.6 5.5 %collective-permute-done.22.refs_2_ = bf16[128,1024]{1,0:T(8,128)(2,1)S(1)} collective-permute-done((bf16[128,1024]{1,0:T(8,128)(2,1)S(1)}, bf16[128,1024]{1,0:T(8,128)(2,1)S(1)}, u32[]{:S(2)}, u32[]{:S(2)}) %collective-permute-start.22) | collective-permute-done | bytes 262176 | tf_op jit(solution)/shard_map/ppermute | solution.py:14
  73.6 1.5 %collective-permute-start.32 = (bf16[36,16,512]{2,1,0:T(8,128)(2,1)}, bf16[36,16,512]{2,1,0:T(8,128)(2,1)S(1)}, u32[]{:S(2)}, u32[]{:S(2)}) collective-permute-start(bf16[36,16,512]{2,1,0:T(8,128)(2,1)} %get-tuple-element.110), channel_id=1, source_target_pairs={{0,3},{1,2},{2,1},{3,0},{4,7},{5,6},{6,5},{7,4},{8,11},{9,10},{10,... | collective-permute-start | bytes 1769480 | tf_op jit(solution)/shard_map/ppermute | solution.py:14
  75.4 11.5 %expert_outputs.1 = (bf16[128,1024]{1,0:T(8,128)(2,1)}, bf16[128,1024]{1,0:T(8,128)(2,1)}, bf16[128,1024]{1,0:T(8,128)(2,1)}, bf16[128,1024]{1,0:T(8,128)(2,1)},...) custom-call(s32[4]{0:T(128)S(1)} %iota_xor_fusion.ids_ref, ...), custom_call_target="tpu_custom_call" | custom-call | tf_op jit(solution)/shard_map/expert_outputs/pallas_call | solution.py:274
  90.5 2.6 %add_pairs.1 = (bf16[64,1024]{1,0:T(8,128)(2,1)}, bf16[64,1024]{1,0:T(8,128)(2,1)}, bf16[64,1024]{1,0:T(8,128)(2,1)}, bf16[64,1024]{1,0:T(8,128)(2,1)}, bf16[64,...) custom-call(bf16[128,1024]{1,0:T(8,128)(2,1)} %get-tuple-element.102.refs_0_, ...), custom_call_target="tpu_custom_call" | custom-call | tf_op jit(solution)/shard_map/add_pairs/pallas_call | solution.py:315
  93.1 1.6 %collective-permute-start.33 = (bf16[64,1024]{1,0:T(8,128)(2,1)}, bf16[64,1024]{1,0:T(8,128)(2,1)S(1)}, u32[]{:S(2)}, u32[]{:S(2)}) collective-permute-start(bf16[64,1024]{1,0:T(8,128)(2,1)} %get-tuple-element.115), channel_id=1, source_target_pairs={{0,1},{1,0},{2,3},{3,2},{4,5},{5,4},{6,7},{7,6},{8,9},{9,8},{10,11... | collective-permute-start | bytes 393224 | tf_op jit(solution)/shard_map/ppermute | solution.py:14
  95.9 1.4 %collective-permute-start.35 = (bf16[64,1024]{1,0:T(8,128)(2,1)}, bf16[64,1024]{1,0:T(8,128)(2,1)S(1)}, u32[]{:S(2)}, u32[]{:S(2)}) collective-permute-start(bf16[64,1024]{1,0:T(8,128)(2,1)} %get-tuple-element.121), channel_id=1, source_target_pairs={{0,3},{1,2},{2,1},{3,0},{4,7},{5,6},{6,5},{7,4},{8,11},{9,10},{10,... | collective-permute-start | bytes 393224 | tf_op jit(solution)/shard_map/ppermute | solution.py:14
  97.4 1.5 %collective-permute-start.36 = (bf16[64,1024]{1,0:T(8,128)(2,1)}, bf16[64,1024]{1,0:T(8,128)(2,1)S(1)}, u32[]{:S(2)}, u32[]{:S(2)}) collective-permute-start(bf16[64,1024]{1,0:T(8,128)(2,1)} %get-tuple-element.128), channel_id=1, source_target_pairs={{0,1},{1,0},{2,3},{3,2},{4,5},{5,4},{6,7},{7,6},{8,9},{9,8},{10,11... | collective-permute-start | bytes 393224 | tf_op jit(solution)/shard_map/ppermute | solution.py:14
  99.4 1.4 %collective-permute-start.38 = (bf16[64,1024]{1,0:T(8,128)(2,1)}, bf16[64,1024]{1,0:T(8,128)(2,1)S(1)}, u32[]{:S(2)}, u32[]{:S(2)}) collective-permute-start(bf16[64,1024]{1,0:T(8,128)(2,1)} %get-tuple-element.130), channel_id=1, source_target_pairs={{0,3},{1,2},{2,1},{3,0},{4,7},{5,6},{6,5},{7,4},{8,11},{9,10},{10,... | collective-permute-start | bytes 393224 | tf_op jit(solution)/shard_map/ppermute | solution.py:14
  101.3 3.6 %place_rows.1 = bf16[64,16,512]{2,1,0:T(8,128)(2,1)} custom-call(s32[64]{0:T(128)} %get-tuple-element.142.rows_ref, bf16[64,16,512]{2,1,0:T(8,128)(2,1)} %add_convert_fusion.states_ref.refs_0_, bf16[36,16,512]{2,1,0:T(8,128)(2,1)} %copy-done.3, bf16[36,16,512]{2,1,0:T(8,128)(2,1)} %copy-done.4, bf16[36,16,512]{2,1,0:T(8,128)(2,1)} %copy-done.5), custom_call_target="tpu_custom_call" | custom-call | tf_op jit(solution)/shard_map/place_rows/pallas_call | solution.py:121
  105.8 1.4 %collective-permute-start.39 = (bf16[32,1024]{1,0:T(8,128)(2,1)S(1)}, bf16[32,1024]{1,0:T(8,128)(2,1)S(1)}, u32[]{:S(2)}, u32[]{:S(2)}) collective-permute-start(bf16[32,1024]{1,0:T(8,128)(2,1)S(1)} %get-tuple-element.162), channel_id=1, source_target_pairs={{0,16},{4,20},{8,24},{12,28},{16,0},{20,4},{24,8},{28,12},{1,17},{... | collective-permute-start | bytes 196616 | tf_op jit(solution)/shard_map/ppermute | solution.py:14
  107.2 0.9 collective-permute-start.40
  108.1 3.6 %collective-permute-done.39 = bf16[32,1024]{1,0:T(8,128)(2,1)S(1)} collective-permute-done((bf16[32,1024]{1,0:T(8,128)(2,1)S(1)}, bf16[32,1024]{1,0:T(8,128)(2,1)S(1)}, u32[]{:S(2)}, u32[]{:S(2)}) %collective-permute-start.39) | collective-permute-done | bytes 65568 | tf_op jit(solution)/shard_map/ppermute | solution.py:14
  111.7 1.6 %collective-permute-done.40 = bf16[32,1024]{1,0:T(8,128)(2,1)S(1)} collective-permute-done((bf16[32,1024]{1,0:T(8,128)(2,1)S(1)}, bf16[32,1024]{1,0:T(8,128)(2,1)S(1)}, u32[]{:S(2)}, u32[]{:S(2)}) %collective-permute-start.40) | collective-permute-done | bytes 65568 | tf_op jit(solution)/shard_map/ppermute | solution.py:14
  113.5 5.5 %collective-permute-done.41 = bf16[32,1024]{1,0:T(8,128)(2,1)S(1)} collective-permute-done((bf16[32,1024]{1,0:T(8,128)(2,1)S(1)}, bf16[32,1024]{1,0:T(8,128)(2,1)S(1)}, u32[]{:S(2)}, u32[]{:S(2)}) %collective-permute-start.41) | collective-permute-done | bytes 65568 | tf_op jit(solution)/shard_map/ppermute | solution.py:14
  119.1 1.2 collective-permute-start.43
  120.3 3.2 %collective-permute-start.44 = (bf16[32,1024]{1,0:T(8,128)(2,1)S(1)}, bf16[32,1024]{1,0:T(8,128)(2,1)S(1)}, u32[]{:S(2)}, u32[]{:S(2)}) collective-permute-start(bf16[32,1024]{1,0:T(8,128)(2,1)S(1)} %fusion.30), channel_id=1, source_target_pairs={{0,24},{4,28},{8,16},{12,20},{16,8},{20,12},{24,0},{28,4},{1,25},{... | collective-permute-start | bytes 196616 | tf_op jit(solution)/shard_map/ppermute | solution.py:14
  124.4 2.2 %collective-permute-done.44 = bf16[32,1024]{1,0:T(8,128)(2,1)S(1)} collective-permute-done((bf16[32,1024]{1,0:T(8,128)(2,1)S(1)}, bf16[32,1024]{1,0:T(8,128)(2,1)S(1)}, u32[]{:S(2)}, u32[]{:S(2)}) %collective-permute-start.44) | collective-permute-done | bytes 65568 | tf_op jit(solution)/shard_map/ppermute | solution.py:14
  126.8 1.5 %collective-permute-done.45 = bf16[128,1024]{1,0:T(8,128)(2,1)S(1)} collective-permute-done((bf16[128,1024]{1,0:T(8,128)(2,1)S(1)}, bf16[128,1024]{1,0:T(8,128)(2,1)S(1)}, u32[]{:S(2)}, u32[]{:S(2)}) %collective-permute-start.45) | collective-permute-done | bytes 262176 | tf_op jit(solution)/shard_map/ppermute | solution.py:14
  (181 shorter events, 22.0 us)
Async XLA Ops:
  0.6 34.5 %copy-start = (bf16[512,1024]{1,0:T(8,128)(2,1)S(1)}, bf16[512,1024]{1,0:T(8,128)(2,1)}, u32[]{:S(2)}) copy-start(bf16[512,1024]{1,0:T(8,128)(2,1)} %param.32) | copy-start | bytes 3145732
  0.7 11.4 %collective-permute-start = (bf16[64,512]{1,0:T(8,128)(2,1)}, bf16[64,512]{1,0:T(8,128)(2,1)S(1)}, u32[]{:S(2)}, u32[]{:S(2)}) collective-permute-start(bf16[64,512]{1,0:T(8,128)(2,1)} %param.23), channel_id=1, source_target_pairs={{0,1},{1,0},{2,3},{3,2},{4,5},{5,4},{6,7},{7,6},{8,9},{9,8},{10,11... | collective-permute-start | bytes 196616 | tf_op jit(solution)/shard_map/ppermute | solution.py:14
  3.7 8.4 %collective-permute-start.1 = (bf16[64,512]{1,0:T(8,128)(2,1)}, bf16[64,512]{1,0:T(8,128)(2,1)S(1)}, u32[]{:S(2)}, u32[]{:S(2)}) collective-permute-start(bf16[64,512]{1,0:T(8,128)(2,1)} %param.23), channel_id=1, source_target_pairs={{0,2},{1,3},{2,0},{3,1},{4,6},{5,7},{6,4},{7,5},{8,10},{9,11},{10,... | collective-permute-start | bytes 196616 | tf_op jit(solution)/shard_map/ppermute | solution.py:14
  6.1 5.9 %collective-permute-start.2 = (bf16[128,512]{1,0:T(8,128)(2,1)S(1)}, bf16[128,512]{1,0:T(8,128)(2,1)S(1)}, u32[]{:S(2)}, u32[]{:S(2)}) collective-permute-start(bf16[128,512]{1,0:T(8,128)(2,1)S(1)} %pad_maximum_fusion.5), channel_id=1, source_target_pairs={{0,3},{1,2},{2,1},{3,0},{4,7},{5,6},{6,5},{7,4},{8,11},{9,10},{10,... | collective-permute-start | bytes 393224 | tf_op jit(solution)/shard_map/ppermute | solution.py:14
  13.4 1.4 %collective-permute-start.3 = (f32[64,288]{1,0:T(8,128)S(1)}, f32[64,288]{1,0:T(8,128)S(1)}, u32[]{:S(2)}, u32[]{:S(2)}) collective-permute-start(f32[64,288]{1,0:T(8,128)S(1)} %fusion.67), channel_id=1, source_target_pairs={{0,4},{4,0},{8,12},{12,8},{16,20},{20,16},{24,28},{28,24},{1,5},{5... | collective-permute-start | bytes 221192 | tf_op jit(solution)/shard_map/ppermute | solution.py:14
  14.8 10.1 %collective-permute-start.4 = (bf16[64,288]{1,0:T(8,128)(2,1)S(1)}, bf16[64,288]{1,0:T(8,128)(2,1)S(1)}, u32[]{:S(2)}, u32[]{:S(2)}) collective-permute-start(bf16[64,288]{1,0:T(8,128)(2,1)S(1)} %convert_element_type.127), channel_id=1, source_target_pairs={{0,8},{4,12},{8,0},{12,4},{16,24},{20,28},{24,16},{28,20},{1,9},{5... | collective-permute-start | bytes 110600 | tf_op jit(solution)/shard_map/ppermute | solution.py:14
  16.5 8.5 %collective-permute-start.5 = (bf16[64,288]{1,0:T(8,128)(2,1)S(1)}, bf16[64,288]{1,0:T(8,128)(2,1)S(1)}, u32[]{:S(2)}, u32[]{:S(2)}) collective-permute-start(bf16[64,288]{1,0:T(8,128)(2,1)S(1)} %convert_element_type.127), channel_id=1, source_target_pairs={{0,16},{4,20},{8,24},{12,28},{16,0},{20,4},{24,8},{28,12},{1,17},{... | collective-permute-start | bytes 110600 | tf_op jit(solution)/shard_map/ppermute | solution.py:14
  19.1 5.9 %collective-permute-start.6 = (bf16[64,288]{1,0:T(8,128)(2,1)S(1)}, bf16[64,288]{1,0:T(8,128)(2,1)S(1)}, u32[]{:S(2)}, u32[]{:S(2)}) collective-permute-start(bf16[64,288]{1,0:T(8,128)(2,1)S(1)} %convert_element_type.127), channel_id=1, source_target_pairs={{0,24},{4,28},{8,16},{12,20},{16,8},{20,12},{24,0},{28,4},{1,25},{... | collective-permute-start | bytes 110600 | tf_op jit(solution)/shard_map/ppermute | solution.py:14
  19.3 7.2 %collective-permute-start.7 = (bf16[64,512]{1,0:T(8,128)(2,1)S(1)}, bf16[64,512]{1,0:T(8,128)(2,1)S(1)}, u32[]{:S(2)}, u32[]{:S(2)}) collective-permute-start(bf16[64,512]{1,0:T(8,128)(2,1)S(1)} %copy-done.14), channel_id=1, source_target_pairs={{0,1},{1,0},{2,3},{3,2},{4,5},{5,4},{6,7},{7,6},{8,9},{9,8},{10,11... | collective-permute-start | bytes 196616 | tf_op jit(solution)/shard_map/ppermute | solution.py:14
  19.8 6.6 %collective-permute-start.8 = (bf16[64,512]{1,0:T(8,128)(2,1)S(1)}, bf16[64,512]{1,0:T(8,128)(2,1)S(1)}, u32[]{:S(2)}, u32[]{:S(2)}) collective-permute-start(bf16[64,512]{1,0:T(8,128)(2,1)S(1)} %copy-done.14), channel_id=1, source_target_pairs={{0,2},{1,3},{2,0},{3,1},{4,6},{5,7},{6,4},{7,5},{8,10},{9,11},{10,... | collective-permute-start | bytes 196616 | tf_op jit(solution)/shard_map/ppermute | solution.py:14
  26.7 8.0 %collective-permute-start.10 = (bf16[64,512]{1,0:T(8,128)(2,1)S(1)}, bf16[64,512]{1,0:T(8,128)(2,1)S(1)}, u32[]{:S(2)}, u32[]{:S(2)}) collective-permute-start(bf16[64,512]{1,0:T(8,128)(2,1)S(1)} %fusion.27), channel_id=1, source_target_pairs={{0,2},{1,3},{2,0},{3,1},{4,6},{5,7},{6,4},{7,5},{8,10},{9,11},{10,... | collective-permute-start | bytes 196616 | tf_op jit(solution)/shard_map/ppermute | solution.py:14
  27.4 7.4 %collective-permute-start.11 = (bf16[64,512]{1,0:T(8,128)(2,1)S(1)}, bf16[64,512]{1,0:T(8,128)(2,1)S(1)}, u32[]{:S(2)}, u32[]{:S(2)}) collective-permute-start(bf16[64,512]{1,0:T(8,128)(2,1)S(1)} %fusion.27), channel_id=1, source_target_pairs={{0,3},{1,2},{2,1},{3,0},{4,7},{5,6},{6,5},{7,4},{8,11},{9,10},{10,... | collective-permute-start | bytes 196616 | tf_op jit(solution)/shard_map/ppermute | solution.py:14
  28.8 6.0 %collective-permute-start.9 = (bf16[64,512]{1,0:T(8,128)(2,1)S(1)}, bf16[64,512]{1,0:T(8,128)(2,1)S(1)}, u32[]{:S(2)}, u32[]{:S(2)}) collective-permute-start(bf16[64,512]{1,0:T(8,128)(2,1)S(1)} %fusion.27), channel_id=1, source_target_pairs={{0,1},{1,0},{2,3},{3,2},{4,5},{5,4},{6,7},{7,6},{8,9},{9,8},{10,11... | collective-permute-start | bytes 196616 | tf_op jit(solution)/shard_map/ppermute | solution.py:14
  35.5 2.2 %collective-permute-start.12 = (bf16[128,1024]{1,0:T(8,128)(2,1)S(1)}, bf16[128,1024]{1,0:T(8,128)(2,1)S(1)}, u32[]{:S(2)}, u32[]{:S(2)}) collective-permute-start(bf16[128,1024]{1,0:T(8,128)(2,1)S(1)} %convolution_convert_fusion), channel_id=1, source_target_pairs={{0,4},{4,0},{8,12},{12,8},{16,20},{20,16},{24,28},{28,24},{1,5},{5... | collective-permute-start | bytes 786440 | tf_op jit(solution)/shard_map/ppermute | solution.py:14
  35.6 22.0 %collective-permute-start.19 = (bf16[36,16,512]{2,1,0:T(8,128)(2,1)}, bf16[36,16,512]{2,1,0:T(8,128)(2,1)S(1)}, u32[]{:S(2)}, u32[]{:S(2)}) collective-permute-start(bf16[36,16,512]{2,1,0:T(8,128)(2,1)} %get-tuple-element.87), channel_id=1, source_target_pairs={{0,1},{1,0},{2,3},{3,2},{4,5},{5,4},{6,7},{7,6},{8,9},{9,8},{10,11... | collective-permute-start | bytes 1769480 | tf_op jit(solution)/shard_map/ppermute | solution.py:14
  36.2 21.5 %collective-permute-start.20 = (bf16[36,16,512]{2,1,0:T(8,128)(2,1)}, bf16[36,16,512]{2,1,0:T(8,128)(2,1)S(1)}, u32[]{:S(2)}, u32[]{:S(2)}) collective-permute-start(bf16[36,16,512]{2,1,0:T(8,128)(2,1)} %get-tuple-element.88), channel_id=1, source_target_pairs={{0,2},{1,3},{2,0},{3,1},{4,6},{5,7},{6,4},{7,5},{8,10},{9,11},{10,... | collective-permute-start | bytes 1769480 | tf_op jit(solution)/shard_map/ppermute | solution.py:14
  38.0 4.5 %collective-permute-start.13 = (bf16[32,1024]{1,0:T(8,128)(2,1)S(1)}, bf16[32,1024]{1,0:T(8,128)(2,1)S(1)}, u32[]{:S(2)}, u32[]{:S(2)}) collective-permute-start(bf16[32,1024]{1,0:T(8,128)(2,1)S(1)} %get-tuple-element.155), channel_id=1, source_target_pairs={{0,8},{4,12},{8,0},{12,4},{16,24},{20,28},{24,16},{28,20},{1,9},{5... | collective-permute-start | bytes 196616 | tf_op jit(solution)/shard_map/ppermute | solution.py:14
  38.7 8.1 %collective-permute-start.14 = (bf16[32,1024]{1,0:T(8,128)(2,1)S(1)}, bf16[32,1024]{1,0:T(8,128)(2,1)S(1)}, u32[]{:S(2)}, u32[]{:S(2)}) collective-permute-start(bf16[32,1024]{1,0:T(8,128)(2,1)S(1)} %get-tuple-element.157), channel_id=1, source_target_pairs={{0,16},{4,20},{8,24},{12,28},{16,0},{20,4},{24,8},{28,12},{1,17},{... | collective-permute-start | bytes 196616 | tf_op jit(solution)/shard_map/ppermute | solution.py:14
  42.2 6.1 %collective-permute-start.15 = (bf16[32,1024]{1,0:T(8,128)(2,1)S(1)}, bf16[32,1024]{1,0:T(8,128)(2,1)S(1)}, u32[]{:S(2)}, u32[]{:S(2)}) collective-permute-start(bf16[32,1024]{1,0:T(8,128)(2,1)S(1)} %get-tuple-element.156), channel_id=1, source_target_pairs={{0,24},{4,28},{8,16},{12,20},{16,8},{20,12},{24,0},{28,4},{1,25},{... | collective-permute-start | bytes 196616 | tf_op jit(solution)/shard_map/ppermute | solution.py:14
  49.2 4.6 %collective-permute-start.16 = (bf16[32,1024]{1,0:T(8,128)(2,1)S(1)}, bf16[32,1024]{1,0:T(8,128)(2,1)S(1)}, u32[]{:S(2)}, u32[]{:S(2)}) collective-permute-start(bf16[32,1024]{1,0:T(8,128)(2,1)S(1)} %fusion.34), channel_id=1, source_target_pairs={{0,8},{4,12},{8,0},{12,4},{16,24},{20,28},{24,16},{28,20},{1,9},{5... | collective-permute-start | bytes 196616 | tf_op jit(solution)/shard_map/ppermute | solution.py:14
  49.2 6.8 %collective-permute-start.17 = (bf16[32,1024]{1,0:T(8,128)(2,1)S(1)}, bf16[32,1024]{1,0:T(8,128)(2,1)S(1)}, u32[]{:S(2)}, u32[]{:S(2)}) collective-permute-start(bf16[32,1024]{1,0:T(8,128)(2,1)S(1)} %fusion.34), channel_id=1, source_target_pairs={{0,16},{4,20},{8,24},{12,28},{16,0},{20,4},{24,8},{28,12},{1,17},{... | collective-permute-start | bytes 196616 | tf_op jit(solution)/shard_map/ppermute | solution.py:14
  51.5 6.1 %collective-permute-start.18 = (bf16[32,1024]{1,0:T(8,128)(2,1)S(1)}, bf16[32,1024]{1,0:T(8,128)(2,1)S(1)}, u32[]{:S(2)}, u32[]{:S(2)}) collective-permute-start(bf16[32,1024]{1,0:T(8,128)(2,1)S(1)} %fusion.34), channel_id=1, source_target_pairs={{0,24},{4,28},{8,16},{12,20},{16,8},{20,12},{24,0},{28,4},{1,25},{... | collective-permute-start | bytes 196616 | tf_op jit(solution)/shard_map/ppermute | solution.py:14
  57.6 43.2 %copy-start.3 = (bf16[36,16,512]{2,1,0:T(8,128)(2,1)}, bf16[36,16,512]{2,1,0:T(8,128)(2,1)S(1)}, u32[]{:S(2)}) copy-start(bf16[36,16,512]{2,1,0:T(8,128)(2,1)S(1)} %collective-permute-done.19.refs_1_) | copy-start | bytes 1769476
  58.5 3.6 %collective-permute-start.24 = (bf16[128,1024]{1,0:T(8,128)(2,1)S(1)}, bf16[128,1024]{1,0:T(8,128)(2,1)S(1)}, u32[]{:S(2)}, u32[]{:S(2)}) collective-permute-start(bf16[128,1024]{1,0:T(8,128)(2,1)S(1)} %pad_maximum_fusion.1.refs_0_), channel_id=1, source_target_pairs={{0,4},{4,0},{8,12},{12,8},{16,20},{20,16},{24,28},{28,24},{1,5},{5... | collective-permute-start | bytes 786440 | tf_op jit(solution)/shard_map/ppermute | solution.py:14
  58.5 9.1 %collective-permute-start.21 = (bf16[128,1024]{1,0:T(8,128)(2,1)S(1)}, bf16[128,1024]{1,0:T(8,128)(2,1)S(1)}, u32[]{:S(2)}, u32[]{:S(2)}) collective-permute-start(bf16[128,1024]{1,0:T(8,128)(2,1)S(1)} %pad_maximum_fusion.1.refs_0_), channel_id=1, source_target_pairs={{0,1},{1,0},{2,3},{3,2},{4,5},{5,4},{6,7},{7,6},{8,9},{9,8},{10,11... | collective-permute-start | bytes 786440 | tf_op jit(solution)/shard_map/ppermute | solution.py:14
  59.0 14.1 %collective-permute-start.22 = (bf16[128,1024]{1,0:T(8,128)(2,1)S(1)}, bf16[128,1024]{1,0:T(8,128)(2,1)S(1)}, u32[]{:S(2)}, u32[]{:S(2)}) collective-permute-start(bf16[128,1024]{1,0:T(8,128)(2,1)S(1)} %pad_maximum_fusion.1.refs_0_), channel_id=1, source_target_pairs={{0,2},{1,3},{2,0},{3,1},{4,6},{5,7},{6,4},{7,5},{8,10},{9,11},{10,... | collective-permute-start | bytes 786440 | tf_op jit(solution)/shard_map/ppermute | solution.py:14
  60.6 12.5 %collective-permute-start.23 = (bf16[128,1024]{1,0:T(8,128)(2,1)S(1)}, bf16[128,1024]{1,0:T(8,128)(2,1)S(1)}, u32[]{:S(2)}, u32[]{:S(2)}) collective-permute-start(bf16[128,1024]{1,0:T(8,128)(2,1)S(1)} %pad_maximum_fusion.1.refs_0_), channel_id=1, source_target_pairs={{0,3},{1,2},{2,1},{3,0},{4,7},{5,6},{6,5},{7,4},{8,11},{9,10},{10,... | collective-permute-start | bytes 786440 | tf_op jit(solution)/shard_map/ppermute | solution.py:14
  73.1 2.0 %collective-permute-start.25 = (bf16[128,1024]{1,0:T(8,128)(2,1)S(1)}, bf16[128,1024]{1,0:T(8,128)(2,1)S(1)}, u32[]{:S(2)}, u32[]{:S(2)}) collective-permute-start(bf16[128,1024]{1,0:T(8,128)(2,1)S(1)} %collective-permute-done.21.refs_0_), channel_id=1, source_target_pairs={{0,4},{4,0},{8,12},{12,8},{16,20},{20,16},{24,28},{28,24},{1,5},{5... | collective-permute-start | bytes 786440 | tf_op jit(solution)/shard_map/ppermute | solution.py:14
  73.1 2.0 %collective-permute-start.26 = (bf16[128,1024]{1,0:T(8,128)(2,1)S(1)}, bf16[128,1024]{1,0:T(8,128)(2,1)S(1)}, u32[]{:S(2)}, u32[]{:S(2)}) collective-permute-start(bf16[128,1024]{1,0:T(8,128)(2,1)S(1)} %collective-permute-done.22.refs_2_), channel_id=1, source_target_pairs={{0,4},{4,0},{8,12},{12,8},{16,20},{20,16},{24,28},{28,24},{1,5},{5... | collective-permute-start | bytes 786440 | tf_op jit(solution)/shard_map/ppermute | solution.py:14
  73.6 1.8 %collective-permute-start.27 = (bf16[128,1024]{1,0:T(8,128)(2,1)S(1)}, bf16[128,1024]{1,0:T(8,128)(2,1)S(1)}, u32[]{:S(2)}, u32[]{:S(2)}) collective-permute-start(bf16[128,1024]{1,0:T(8,128)(2,1)S(1)} %collective-permute-done.23.refs_4_), channel_id=1, source_target_pairs={{0,4},{4,0},{8,12},{12,8},{16,20},{20,16},{24,28},{28,24},{1,5},{5... | collective-permute-start | bytes 786440 | tf_op jit(solution)/shard_map/ppermute | solution.py:14
  73.6 16.8 %collective-permute-start.32 = (bf16[36,16,512]{2,1,0:T(8,128)(2,1)}, bf16[36,16,512]{2,1,0:T(8,128)(2,1)S(1)}, u32[]{:S(2)}, u32[]{:S(2)}) collective-permute-start(bf16[36,16,512]{2,1,0:T(8,128)(2,1)} %get-tuple-element.110), channel_id=1, source_target_pairs={{0,3},{1,2},{2,1},{3,0},{4,7},{5,6},{6,5},{7,4},{8,11},{9,10},{10,... | collective-permute-start | bytes 1769480 | tf_op jit(solution)/shard_map/ppermute | solution.py:14
  86.9 1.8 %collective-permute-start.28 = (bf16[128,1024]{1,0:T(8,128)(2,1)}, bf16[128,1024]{1,0:T(8,128)(2,1)S(1)}, u32[]{:S(2)}, u32[]{:S(2)}) collective-permute-start(bf16[128,1024]{1,0:T(8,128)(2,1)} %get-tuple-element.106), channel_id=1, source_target_pairs={{0,4},{4,0},{8,12},{12,8},{16,20},{20,16},{24,28},{28,24},{1,5},{5... | collective-permute-start | bytes 786440 | tf_op jit(solution)/shard_map/ppermute | solution.py:14
  87.1 2.0 %collective-permute-start.29 = (bf16[128,1024]{1,0:T(8,128)(2,1)}, bf16[128,1024]{1,0:T(8,128)(2,1)S(1)}, u32[]{:S(2)}, u32[]{:S(2)}) collective-permute-start(bf16[128,1024]{1,0:T(8,128)(2,1)} %get-tuple-element.107), channel_id=1, source_target_pairs={{0,4},{4,0},{8,12},{12,8},{16,20},{20,16},{24,28},{28,24},{1,5},{5... | collective-permute-start | bytes 786440 | tf_op jit(solution)/shard_map/ppermute | solution.py:14
  87.5 2.4 %collective-permute-start.30 = (bf16[128,1024]{1,0:T(8,128)(2,1)}, bf16[128,1024]{1,0:T(8,128)(2,1)S(1)}, u32[]{:S(2)}, u32[]{:S(2)}) collective-permute-start(bf16[128,1024]{1,0:T(8,128)(2,1)} %get-tuple-element.108), channel_id=1, source_target_pairs={{0,4},{4,0},{8,12},{12,8},{16,20},{20,16},{24,28},{28,24},{1,5},{5... | collective-permute-start | bytes 786440 | tf_op jit(solution)/shard_map/ppermute | solution.py:14
  87.6 2.4 %collective-permute-start.31 = (bf16[128,1024]{1,0:T(8,128)(2,1)}, bf16[128,1024]{1,0:T(8,128)(2,1)}, u32[]{:S(2)}, u32[]{:S(2)}) collective-permute-start(bf16[128,1024]{1,0:T(8,128)(2,1)} %get-tuple-element.109), channel_id=1, source_target_pairs={{0,4},{4,0},{8,12},{12,8},{16,20},{20,16},{24,28},{28,24},{1,5},{5... | collective-permute-start | bytes 786440 | tf_op jit(solution)/shard_map/ppermute | solution.py:14
  93.1 6.3 %collective-permute-start.33 = (bf16[64,1024]{1,0:T(8,128)(2,1)}, bf16[64,1024]{1,0:T(8,128)(2,1)S(1)}, u32[]{:S(2)}, u32[]{:S(2)}) collective-permute-start(bf16[64,1024]{1,0:T(8,128)(2,1)} %get-tuple-element.115), channel_id=1, source_target_pairs={{0,1},{1,0},{2,3},{3,2},{4,5},{5,4},{6,7},{7,6},{8,9},{9,8},{10,11... | collective-permute-start | bytes 393224 | tf_op jit(solution)/shard_map/ppermute | solution.py:14
  95.4 10.3 %collective-permute-start.34 = (bf16[64,1024]{1,0:T(8,128)(2,1)}, bf16[64,1024]{1,0:T(8,128)(2,1)S(1)}, u32[]{:S(2)}, u32[]{:S(2)}) collective-permute-start(bf16[64,1024]{1,0:T(8,128)(2,1)} %get-tuple-element.120), channel_id=1, source_target_pairs={{0,2},{1,3},{2,0},{3,1},{4,6},{5,7},{6,4},{7,5},{8,10},{9,11},{10,... | collective-permute-start | bytes 393224 | tf_op jit(solution)/shard_map/ppermute | solution.py:14
  95.9 9.7 %collective-permute-start.35 = (bf16[64,1024]{1,0:T(8,128)(2,1)}, bf16[64,1024]{1,0:T(8,128)(2,1)S(1)}, u32[]{:S(2)}, u32[]{:S(2)}) collective-permute-start(bf16[64,1024]{1,0:T(8,128)(2,1)} %get-tuple-element.121), channel_id=1, source_target_pairs={{0,3},{1,2},{2,1},{3,0},{4,7},{5,6},{6,5},{7,4},{8,11},{9,10},{10,... | collective-permute-start | bytes 393224 | tf_op jit(solution)/shard_map/ppermute | solution.py:14
  97.4 15.9 %collective-permute-start.36 = (bf16[64,1024]{1,0:T(8,128)(2,1)}, bf16[64,1024]{1,0:T(8,128)(2,1)S(1)}, u32[]{:S(2)}, u32[]{:S(2)}) collective-permute-start(bf16[64,1024]{1,0:T(8,128)(2,1)} %get-tuple-element.128), channel_id=1, source_target_pairs={{0,1},{1,0},{2,3},{3,2},{4,5},{5,4},{6,7},{7,6},{8,9},{9,8},{10,11... | collective-permute-start | bytes 393224 | tf_op jit(solution)/shard_map/ppermute | solution.py:14
  98.9 14.4 %collective-permute-start.37 = (bf16[64,1024]{1,0:T(8,128)(2,1)}, bf16[64,1024]{1,0:T(8,128)(2,1)S(1)}, u32[]{:S(2)}, u32[]{:S(2)}) collective-permute-start(bf16[64,1024]{1,0:T(8,128)(2,1)} %get-tuple-element.129), channel_id=1, source_target_pairs={{0,2},{1,3},{2,0},{3,1},{4,6},{5,7},{6,4},{7,5},{8,10},{9,11},{10,... | collective-permute-start | bytes 393224 | tf_op jit(solution)/shard_map/ppermute | solution.py:14
  99.4 13.9 %collective-permute-start.38 = (bf16[64,1024]{1,0:T(8,128)(2,1)}, bf16[64,1024]{1,0:T(8,128)(2,1)S(1)}, u32[]{:S(2)}, u32[]{:S(2)}) collective-permute-start(bf16[64,1024]{1,0:T(8,128)(2,1)} %get-tuple-element.130), channel_id=1, source_target_pairs={{0,3},{1,2},{2,1},{3,0},{4,7},{5,6},{6,5},{7,4},{8,11},{9,10},{10,... | collective-permute-start | bytes 393224 | tf_op jit(solution)/shard_map/ppermute | solution.py:14
  105.8 5.9 %collective-permute-start.39 = (bf16[32,1024]{1,0:T(8,128)(2,1)S(1)}, bf16[32,1024]{1,0:T(8,128)(2,1)S(1)}, u32[]{:S(2)}, u32[]{:S(2)}) collective-permute-start(bf16[32,1024]{1,0:T(8,128)(2,1)S(1)} %get-tuple-element.162), channel_id=1, source_target_pairs={{0,16},{4,20},{8,24},{12,28},{16,0},{20,4},{24,8},{28,12},{1,17},{... | collective-permute-start | bytes 196616 | tf_op jit(solution)/shard_map/ppermute | solution.py:14
  107.2 6.1 %collective-permute-start.40 = (bf16[32,1024]{1,0:T(8,128)(2,1)S(1)}, bf16[32,1024]{1,0:T(8,128)(2,1)S(1)}, u32[]{:S(2)}, u32[]{:S(2)}) collective-permute-start(bf16[32,1024]{1,0:T(8,128)(2,1)S(1)} %get-tuple-element.161), channel_id=1, source_target_pairs={{0,24},{4,28},{8,16},{12,20},{16,8},{20,12},{24,0},{28,4},{1,25},{... | collective-permute-start | bytes 196616 | tf_op jit(solution)/shard_map/ppermute | solution.py:14
  113.4 5.6 %collective-permute-start.41 = (bf16[32,1024]{1,0:T(8,128)(2,1)S(1)}, bf16[32,1024]{1,0:T(8,128)(2,1)S(1)}, u32[]{:S(2)}, u32[]{:S(2)}) collective-permute-start(bf16[32,1024]{1,0:T(8,128)(2,1)S(1)} %unstack.53), channel_id=1, source_target_pairs={{0,8},{4,12},{8,0},{12,4},{16,24},{20,28},{24,16},{28,20},{1,9},{5... | collective-permute-start | bytes 196616 | tf_op jit(solution)/shard_map/ppermute | solution.py:14
  119.0 4.5 %collective-permute-start.42 = (bf16[32,1024]{1,0:T(8,128)(2,1)S(1)}, bf16[32,1024]{1,0:T(8,128)(2,1)S(1)}, u32[]{:S(2)}, u32[]{:S(2)}) collective-permute-start(bf16[32,1024]{1,0:T(8,128)(2,1)S(1)} %fusion.30), channel_id=1, source_target_pairs={{0,8},{4,12},{8,0},{12,4},{16,24},{20,28},{24,16},{28,20},{1,9},{5... | collective-permute-start | bytes 196616 | tf_op jit(solution)/shard_map/ppermute | solution.py:14
  119.1 5.2 %collective-permute-start.43 = (bf16[32,1024]{1,0:T(8,128)(2,1)S(1)}, bf16[32,1024]{1,0:T(8,128)(2,1)S(1)}, u32[]{:S(2)}, u32[]{:S(2)}) collective-permute-start(bf16[32,1024]{1,0:T(8,128)(2,1)S(1)} %fusion.30), channel_id=1, source_target_pairs={{0,16},{4,20},{8,24},{12,28},{16,0},{20,4},{24,8},{28,12},{1,17},{... | collective-permute-start | bytes 196616 | tf_op jit(solution)/shard_map/ppermute | solution.py:14
  120.3 6.3 %collective-permute-start.44 = (bf16[32,1024]{1,0:T(8,128)(2,1)S(1)}, bf16[32,1024]{1,0:T(8,128)(2,1)S(1)}, u32[]{:S(2)}, u32[]{:S(2)}) collective-permute-start(bf16[32,1024]{1,0:T(8,128)(2,1)S(1)} %fusion.30), channel_id=1, source_target_pairs={{0,24},{4,28},{8,16},{12,20},{16,8},{20,12},{24,0},{28,4},{1,25},{... | collective-permute-start | bytes 196616 | tf_op jit(solution)/shard_map/ppermute | solution.py:14
  126.7 1.6 %collective-permute-start.45 = (bf16[128,1024]{1,0:T(8,128)(2,1)S(1)}, bf16[128,1024]{1,0:T(8,128)(2,1)S(1)}, u32[]{:S(2)}, u32[]{:S(2)}) collective-permute-start(bf16[128,1024]{1,0:T(8,128)(2,1)S(1)} %pad_maximum_fusion.3), channel_id=1, source_target_pairs={{0,4},{4,0},{8,12},{12,8},{16,20},{20,16},{24,28},{28,24},{1,5},{5... | collective-permute-start | bytes 786440 | tf_op jit(solution)/shard_map/ppermute | solution.py:14
  (19 other events, 185.7 us)

commit v5 on v4

--- a/solution.py
+++ b/solution.py
@@ -538,14 +538,14 @@
     arrived = [swap(parts[2 * flip + 1], "expert", flip) for flip in range(1, owners)]
     arrived[0], *tied = lax.optimization_barrier((arrived[0], *later, *now))
     done = finish_states(list(tied[: len(later)]), list(tied[len(later) :]))
-    *arrived, ssm_new, conv_new = lax.optimization_barrier((*arrived, *done))
+    *arrived, ssm_new = lax.optimization_barrier((*arrived, done[0]))
     far_sum = parts[1].astype(F32) + sum(part.astype(F32) for part in arrived)
     far_rows = far_sum.astype(BF16).reshape(planes - near_planes, chunk, width)
     from_far = [
         swap(far_rows[k], "dp", 2 * (near_planes + k)).astype(F32) for k in range(planes - near_planes)
     ]
     arrived = [parts[0]] + [swap(parts[2 * flip], "expert", flip) for flip in range(1, owners)]
-    tied = lax.optimization_barrier((*arrived, *from_far))
+    *tied, conv_new = lax.optimization_barrier((*arrived, *from_far, done[1]))
     arrived, from_far = tied[:owners], tied[owners:]
     near_sum = sum(part.astype(F32) for part in arrived).reshape(near_planes, chunk, width)
     mix_rows = scatter_pairs(list(near_sum), "dp", 2) + sum(from_far)

time: 130 us -> 129 us (level)
  no operation moved by 1% of the time
where the time goes in v5:
time: 129 us; the launch traced here: 128 us
  starting transfers between devices  46.4 us (36%)
  waiting for transfers between devices  36 us (28%)
  Pallas kernels  24.3 us (19%)
  other arithmetic  10.5 us (8%)
  local copies, waits for them, and re-layouts  6.41 us (5%)
  matrix products  3.31 us (3%)
  between operations  1.51 us (1%)
    ppermute x46, starting transfers between devices, swap(): return lax.ppermute(values, axis, [(i, i ^ flip) for i in range(size)])  46.4 us
    ppermute x46, waiting for transfers between devices, swap(): return lax.ppermute(values, axis, [(i, i ^ flip) for i in range(size)])  36 us
    pallas_call x2, Pallas kernels, expert_kernel(): pl.pallas_call(kernel, out_shape=out_shape, in_specs=in_specs, out_specs=...  15.4 us
    pallas_call x1, Pallas kernels, place_rows(): pl.pallas_call(kernel, out_shape=jax.ShapeDtypeStruct((row_count,) + row_...  3.5 us
    pallas_call x1, Pallas kernels, pack_rows(): pl.pallas_call(kernel, out_shape=[jax.ShapeDtypeStruct((count + (0 if tai...  2.85 us
  transfers between devices with their start and end apart: 46, of which 20 were waited for; matrix products, arithmetic and copies ran while one was open for 12% of the time, Pallas kernels for 17%

profile of v5, /device:TPU:0, one launch (start us, length us, event | category | flops | bytes accessed | tf_op | source)
XLA Modules:
  0.0 128.5 jit_solution(14036206508829550424)
XLA Ops:
  0.7 3.0 %collective-permute-start = (bf16[64,512]{1,0:T(8,128)(2,1)}, bf16[64,512]{1,0:T(8,128)(2,1)S(1)}, u32[]{:S(2)}, u32[]{:S(2)}) collective-permute-start(bf16[64,512]{1,0:T(8,128)(2,1)} %param.23), channel_id=1, source_target_pairs={{0,1},{1,0},{2,3},{3,2},{4,5},{5,4},{6,7},{7,6},{8,9},{9,8},{10,11... | collective-permute-start | bytes 196616 | tf_op jit(solution)/shard_map/ppermute | solution.py:14
  3.7 1.5 %collective-permute-start.1 = (bf16[64,512]{1,0:T(8,128)(2,1)}, bf16[64,512]{1,0:T(8,128)(2,1)S(1)}, u32[]{:S(2)}, u32[]{:S(2)}) collective-permute-start(bf16[64,512]{1,0:T(8,128)(2,1)} %param.23), channel_id=1, source_target_pairs={{0,2},{1,3},{2,0},{3,1},{4,6},{5,7},{6,4},{7,5},{8,10},{9,11},{10,... | collective-permute-start | bytes 196616 | tf_op jit(solution)/shard_map/ppermute | solution.py:14
  5.2 0.9 pad_maximum_fusion.5
  7.0 0.9 slice_bitcast_fusion
  9.6 1.0 multiply_reduce_fusion.1
  10.6 1.4 %collective-permute-done.2 = bf16[128,512]{1,0:T(8,128)(2,1)S(1)} collective-permute-done((bf16[128,512]{1,0:T(8,128)(2,1)S(1)}, bf16[128,512]{1,0:T(8,128)(2,1)S(1)}, u32[]{:S(2)}, u32[]{:S(2)}) %collective-permute-start.2) | collective-permute-done | bytes 131104 | tf_op jit(solution)/shard_map/ppermute | solution.py:14
  12.1 1.1 multiply_convert_fusion
  13.7 1.1 collective-permute-done.3
  14.8 1.6 %collective-permute-start.4 = (bf16[64,288]{1,0:T(8,128)(2,1)S(1)}, bf16[64,288]{1,0:T(8,128)(2,1)S(1)}, u32[]{:S(2)}, u32[]{:S(2)}) collective-permute-start(bf16[64,288]{1,0:T(8,128)(2,1)S(1)} %convert_element_type.127), channel_id=1, source_target_pairs={{0,8},{4,12},{8,0},{12,4},{16,24},{20,28},{24,16},{28,20},{1,9},{5... | collective-permute-start | bytes 110600 | tf_op jit(solution)/shard_map/ppermute | solution.py:14
  16.5 2.6 %collective-permute-start.5 = (bf16[64,288]{1,0:T(8,128)(2,1)S(1)}, bf16[64,288]{1,0:T(8,128)(2,1)S(1)}, u32[]{:S(2)}, u32[]{:S(2)}) collective-permute-start(bf16[64,288]{1,0:T(8,128)(2,1)S(1)} %convert_element_type.127), channel_id=1, source_target_pairs={{0,16},{4,20},{8,24},{12,28},{16,0},{20,4},{24,8},{28,12},{1,17},{... | collective-permute-start | bytes 110600 | tf_op jit(solution)/shard_map/ppermute | solution.py:14
  19.8 1.5 %collective-permute-start.8 = (bf16[64,512]{1,0:T(8,128)(2,1)S(1)}, bf16[64,512]{1,0:T(8,128)(2,1)S(1)}, u32[]{:S(2)}, u32[]{:S(2)}) collective-permute-start(bf16[64,512]{1,0:T(8,128)(2,1)S(1)} %copy-done.14), channel_id=1, source_target_pairs={{0,2},{1,3},{2,0},{3,1},{4,6},{5,7},{6,4},{7,5},{8,10},{9,11},{10,... | collective-permute-start | bytes 196616 | tf_op jit(solution)/shard_map/ppermute | solution.py:14
  25.5 0.9 multiply_reduce_fusion
  27.4 1.4 %collective-permute-start.11 = (bf16[64,512]{1,0:T(8,128)(2,1)S(1)}, bf16[64,512]{1,0:T(8,128)(2,1)S(1)}, u32[]{:S(2)}, u32[]{:S(2)}) collective-permute-start(bf16[64,512]{1,0:T(8,128)(2,1)S(1)} %fusion.27), channel_id=1, source_target_pairs={{0,3},{1,2},{2,1},{3,0},{4,7},{5,6},{6,5},{7,4},{8,11},{9,10},{10,... | collective-permute-start | bytes 196616 | tf_op jit(solution)/shard_map/ppermute | solution.py:14
  28.8 1.5 %collective-permute-start.9 = (bf16[64,512]{1,0:T(8,128)(2,1)S(1)}, bf16[64,512]{1,0:T(8,128)(2,1)S(1)}, u32[]{:S(2)}, u32[]{:S(2)}) collective-permute-start(bf16[64,512]{1,0:T(8,128)(2,1)S(1)} %fusion.27), channel_id=1, source_target_pairs={{0,1},{1,0},{2,3},{3,2},{4,5},{5,4},{6,7},{7,6},{8,9},{9,8},{10,11... | collective-permute-start | bytes 196616 | tf_op jit(solution)/shard_map/ppermute | solution.py:14
  30.3 1.6 %add_convert_fusion.states_ref.refs_0_ = bf16[64,16,512]{2,1,0:T(8,128)(2,1)} fusion(bf16[64,16,512]{2,1,0:T(8,128)(2,1)S(1)} %copy-done.2, f32[64,16]{1,0:T(8,128)S(1)} %get-tuple-element.80, f32[64,512]{1,0:T(8,128)S(1)} %convert_multiply_fusion, f32[16,512]{1,0:T(8,128)S(1)} %exponential_negate_fusion, f32[64,512]{1,0:T(8,128)S(1)} %get-tuple-element.77), kind=kLoop, calls=%fused_computation | loop fusion | flops 3145728 | bytes 2396160 | tf_op jit(solution)/shard_map/convert_element_type | solution.py:444
  31.9 2.9 %pack_rows.1 = (bf16[36,16,512]{2,1,0:T(8,128)(2,1)}, bf16[36,16,512]{2,1,0:T(8,128)(2,1)}, bf16[36,16,512]{2,1,0:T(8,128)(2,1)}) custom-call(s32[128]{0:T(128)} %select_reduce_fusion.1.rows_ref, bf16[64,16,512]{2,1,0:T(8,128)(2,1)} %add_convert_fusion.states_ref.refs_0_, bf16[4,16,512]{2,1,0:T(8,128)(2,1)} %squeeze.33.refs_0_, ...), custom_call_target="tpu_custom_call" | custom-call | tf_op jit(solution)/shard_map/pack_rows/pallas_call | solution.py:86
  36.2 1.5 %collective-permute-start.20 = (bf16[36,16,512]{2,1,0:T(8,128)(2,1)}, bf16[36,16,512]{2,1,0:T(8,128)(2,1)S(1)}, u32[]{:S(2)}, u32[]{:S(2)}) collective-permute-start(bf16[36,16,512]{2,1,0:T(8,128)(2,1)} %get-tuple-element.88), channel_id=1, source_target_pairs={{0,2},{1,3},{2,0},{3,1},{4,6},{5,7},{6,4},{7,5},{8,10},{9,11},{10,... | collective-permute-start | bytes 1769480 | tf_op jit(solution)/shard_map/ppermute | solution.py:14
  38.7 3.5 %collective-permute-start.14 = (bf16[32,1024]{1,0:T(8,128)(2,1)S(1)}, bf16[32,1024]{1,0:T(8,128)(2,1)S(1)}, u32[]{:S(2)}, u32[]{:S(2)}) collective-permute-start(bf16[32,1024]{1,0:T(8,128)(2,1)S(1)} %get-tuple-element.157), channel_id=1, source_target_pairs={{0,16},{4,20},{8,24},{12,28},{16,0},{20,4},{24,8},{28,12},{1,17},{... | collective-permute-start | bytes 196616 | tf_op jit(solution)/shard_map/ppermute | solution.py:14
  42.5 4.3 %collective-permute-done.14 = bf16[32,1024]{1,0:T(8,128)(2,1)S(1)} collective-permute-done((bf16[32,1024]{1,0:T(8,128)(2,1)S(1)}, bf16[32,1024]{1,0:T(8,128)(2,1)S(1)}, u32[]{:S(2)}, u32[]{:S(2)}) %collective-permute-start.14) | collective-permute-done | bytes 65568 | tf_op jit(solution)/shard_map/ppermute | solution.py:14
  46.8 1.5 %collective-permute-done.15 = bf16[32,1024]{1,0:T(8,128)(2,1)S(1)} collective-permute-done((bf16[32,1024]{1,0:T(8,128)(2,1)S(1)}, bf16[32,1024]{1,0:T(8,128)(2,1)S(1)}, u32[]{:S(2)}, u32[]{:S(2)}) %collective-permute-start.15) | collective-permute-done | bytes 65568 | tf_op jit(solution)/shard_map/ppermute | solution.py:14
  48.3 0.9 fusion.34
  49.2 2.3 %collective-permute-start.17 = (bf16[32,1024]{1,0:T(8,128)(2,1)S(1)}, bf16[32,1024]{1,0:T(8,128)(2,1)S(1)}, u32[]{:S(2)}, u32[]{:S(2)}) collective-permute-start(bf16[32,1024]{1,0:T(8,128)(2,1)S(1)} %fusion.34), channel_id=1, source_target_pairs={{0,16},{4,20},{8,24},{12,28},{16,0},{20,4},{24,8},{28,12},{1,17},{... | collective-permute-start | bytes 196616 | tf_op jit(solution)/shard_map/ppermute | solution.py:14
  51.5 2.1 %collective-permute-start.18 = (bf16[32,1024]{1,0:T(8,128)(2,1)S(1)}, bf16[32,1024]{1,0:T(8,128)(2,1)S(1)}, u32[]{:S(2)}, u32[]{:S(2)}) collective-permute-start(bf16[32,1024]{1,0:T(8,128)(2,1)S(1)} %fusion.34), channel_id=1, source_target_pairs={{0,24},{4,28},{8,16},{12,20},{16,8},{20,12},{24,0},{28,4},{1,25},{... | collective-permute-start | bytes 196616 | tf_op jit(solution)/shard_map/ppermute | solution.py:14
  53.8 2.3 %collective-permute-done.17 = bf16[32,1024]{1,0:T(8,128)(2,1)S(1)} collective-permute-done((bf16[32,1024]{1,0:T(8,128)(2,1)S(1)}, bf16[32,1024]{1,0:T(8,128)(2,1)S(1)}, u32[]{:S(2)}, u32[]{:S(2)}) %collective-permute-start.17) | collective-permute-done | bytes 65568 | tf_op jit(solution)/shard_map/ppermute | solution.py:14
  56.1 1.5 %collective-permute-done.18 = bf16[32,1024]{1,0:T(8,128)(2,1)S(1)} collective-permute-done((bf16[32,1024]{1,0:T(8,128)(2,1)S(1)}, bf16[32,1024]{1,0:T(8,128)(2,1)S(1)}, u32[]{:S(2)}, u32[]{:S(2)}) %collective-permute-start.18) | collective-permute-done | bytes 65568 | tf_op jit(solution)/shard_map/ppermute | solution.py:14
  57.6 0.9 copy-done.4
  59.0 1.5 %collective-permute-start.22 = (bf16[128,1024]{1,0:T(8,128)(2,1)S(1)}, bf16[128,1024]{1,0:T(8,128)(2,1)S(1)}, u32[]{:S(2)}, u32[]{:S(2)}) collective-permute-start(bf16[128,1024]{1,0:T(8,128)(2,1)S(1)} %pad_maximum_fusion.1.refs_0_), channel_id=1, source_target_pairs={{0,2},{1,3},{2,0},{3,1},{4,6},{5,7},{6,4},{7,5},{8,10},{9,11},{10,... | collective-permute-start | bytes 786440 | tf_op jit(solution)/shard_map/ppermute | solution.py:14
  60.6 1.4 %collective-permute-start.23 = (bf16[128,1024]{1,0:T(8,128)(2,1)S(1)}, bf16[128,1024]{1,0:T(8,128)(2,1)S(1)}, u32[]{:S(2)}, u32[]{:S(2)}) collective-permute-start(bf16[128,1024]{1,0:T(8,128)(2,1)S(1)} %pad_maximum_fusion.1.refs_0_), channel_id=1, source_target_pairs={{0,3},{1,2},{2,1},{3,0},{4,7},{5,6},{6,5},{7,4},{8,11},{9,10},{10,... | collective-permute-start | bytes 786440 | tf_op jit(solution)/shard_map/ppermute | solution.py:14
  62.2 3.9 %expert_sums.1 = (f32[256,896]{1,0:T(8,128)S(1)}, f32[256,896]{1,0:T(8,128)S(1)}, f32[256,1]{1,0:T(8,128)S(1)}) custom-call(s32[4]{0:T(128)S(1)} %iota_xor_fusion.ids_ref, bf16[128,1024]{1,0:T(8,128)(2,1)S(1)} %pad_maximum_fusion.1.refs_0_, bf16[128,1024]{1,0:T(8,128)(2,1)S(1)} %collective-permute-done.24.refs_1_, f32[4,1,1024]{2,1,0:T(1,128)S(1)} %bitcast.36, ...), custom_call_target="tpu_custom_call" | custom-call | tf_op jit(solution)/shard_map/expert_sums/pallas_call | solution.py:274
  66.1 1.5 %collective-permute-done.21.refs_0_ = bf16[128,1024]{1,0:T(8,128)(2,1)S(1)} collective-permute-done((bf16[128,1024]{1,0:T(8,128)(2,1)S(1)}, bf16[128,1024]{1,0:T(8,128)(2,1)S(1)}, u32[]{:S(2)}, u32[]{:S(2)}) %collective-permute-start.21) | collective-permute-done | bytes 262176 | tf_op jit(solution)/shard_map/ppermute | solution.py:14
  67.6 5.5 %collective-permute-done.22.refs_2_ = bf16[128,1024]{1,0:T(8,128)(2,1)S(1)} collective-permute-done((bf16[128,1024]{1,0:T(8,128)(2,1)S(1)}, bf16[128,1024]{1,0:T(8,128)(2,1)S(1)}, u32[]{:S(2)}, u32[]{:S(2)}) %collective-permute-start.22) | collective-permute-done | bytes 262176 | tf_op jit(solution)/shard_map/ppermute | solution.py:14
  73.6 1.5 %collective-permute-start.32 = (bf16[36,16,512]{2,1,0:T(8,128)(2,1)}, bf16[36,16,512]{2,1,0:T(8,128)(2,1)S(1)}, u32[]{:S(2)}, u32[]{:S(2)}) collective-permute-start(bf16[36,16,512]{2,1,0:T(8,128)(2,1)} %get-tuple-element.110), channel_id=1, source_target_pairs={{0,3},{1,2},{2,1},{3,0},{4,7},{5,6},{6,5},{7,4},{8,11},{9,10},{10,... | collective-permute-start | bytes 1769480 | tf_op jit(solution)/shard_map/ppermute | solution.py:14
  75.4 11.5 %expert_outputs.1 = (bf16[128,1024]{1,0:T(8,128)(2,1)}, bf16[128,1024]{1,0:T(8,128)(2,1)}, bf16[128,1024]{1,0:T(8,128)(2,1)}, bf16[128,1024]{1,0:T(8,128)(2,1)},...) custom-call(s32[4]{0:T(128)S(1)} %iota_xor_fusion.ids_ref, ...), custom_call_target="tpu_custom_call" | custom-call | tf_op jit(solution)/shard_map/expert_outputs/pallas_call | solution.py:274
  90.5 2.6 %add_pairs.1 = (bf16[64,1024]{1,0:T(8,128)(2,1)}, bf16[64,1024]{1,0:T(8,128)(2,1)}, bf16[64,1024]{1,0:T(8,128)(2,1)}, bf16[64,1024]{1,0:T(8,128)(2,1)}, bf16[64,...) custom-call(bf16[128,1024]{1,0:T(8,128)(2,1)} %get-tuple-element.102.refs_0_, ...), custom_call_target="tpu_custom_call" | custom-call | tf_op jit(solution)/shard_map/add_pairs/pallas_call | solution.py:315
  93.1 1.6 %collective-permute-start.33 = (bf16[64,1024]{1,0:T(8,128)(2,1)}, bf16[64,1024]{1,0:T(8,128)(2,1)S(1)}, u32[]{:S(2)}, u32[]{:S(2)}) collective-permute-start(bf16[64,1024]{1,0:T(8,128)(2,1)} %get-tuple-element.115), channel_id=1, source_target_pairs={{0,1},{1,0},{2,3},{3,2},{4,5},{5,4},{6,7},{7,6},{8,9},{9,8},{10,11... | collective-permute-start | bytes 393224 | tf_op jit(solution)/shard_map/ppermute | solution.py:14
  95.2 1.4 %collective-permute-start.35 = (bf16[64,1024]{1,0:T(8,128)(2,1)}, bf16[64,1024]{1,0:T(8,128)(2,1)S(1)}, u32[]{:S(2)}, u32[]{:S(2)}) collective-permute-start(bf16[64,1024]{1,0:T(8,128)(2,1)} %get-tuple-element.121), channel_id=1, source_target_pairs={{0,3},{1,2},{2,1},{3,0},{4,7},{5,6},{6,5},{7,4},{8,11},{9,10},{10,... | collective-permute-start | bytes 393224 | tf_op jit(solution)/shard_map/ppermute | solution.py:14
  97.4 1.5 %collective-permute-start.36 = (bf16[64,1024]{1,0:T(8,128)(2,1)}, bf16[64,1024]{1,0:T(8,128)(2,1)S(1)}, u32[]{:S(2)}, u32[]{:S(2)}) collective-permute-start(bf16[64,1024]{1,0:T(8,128)(2,1)} %get-tuple-element.127), channel_id=1, source_target_pairs={{0,1},{1,0},{2,3},{3,2},{4,5},{5,4},{6,7},{7,6},{8,9},{9,8},{10,11... | collective-permute-start | bytes 393224 | tf_op jit(solution)/shard_map/ppermute | solution.py:14
  99.4 1.4 %collective-permute-start.38 = (bf16[64,1024]{1,0:T(8,128)(2,1)}, bf16[64,1024]{1,0:T(8,128)(2,1)S(1)}, u32[]{:S(2)}, u32[]{:S(2)}) collective-permute-start(bf16[64,1024]{1,0:T(8,128)(2,1)} %get-tuple-element.129), channel_id=1, source_target_pairs={{0,3},{1,2},{2,1},{3,0},{4,7},{5,6},{6,5},{7,4},{8,11},{9,10},{10,... | collective-permute-start | bytes 393224 | tf_op jit(solution)/shard_map/ppermute | solution.py:14
  101.0 3.5 %place_rows.1 = bf16[64,16,512]{2,1,0:T(8,128)(2,1)} custom-call(s32[64]{0:T(128)} %get-tuple-element.142.rows_ref, bf16[64,16,512]{2,1,0:T(8,128)(2,1)} %add_convert_fusion.states_ref.refs_0_, bf16[36,16,512]{2,1,0:T(8,128)(2,1)} %copy-done.3, bf16[36,16,512]{2,1,0:T(8,128)(2,1)} %copy-done.4, bf16[36,16,512]{2,1,0:T(8,128)(2,1)} %copy-done.5), custom_call_target="tpu_custom_call" | custom-call | tf_op jit(solution)/shard_map/place_rows/pallas_call | solution.py:121
  104.9 1.4 %collective-permute-start.39 = (bf16[32,1024]{1,0:T(8,128)(2,1)S(1)}, bf16[32,1024]{1,0:T(8,128)(2,1)S(1)}, u32[]{:S(2)}, u32[]{:S(2)}) collective-permute-start(bf16[32,1024]{1,0:T(8,128)(2,1)S(1)} %get-tuple-element.162), channel_id=1, source_target_pairs={{0,16},{4,20},{8,24},{12,28},{16,0},{20,4},{24,8},{28,12},{1,17},{... | collective-permute-start | bytes 196616 | tf_op jit(solution)/shard_map/ppermute | solution.py:14
  106.4 0.9 collective-permute-start.40
  108.0 2.9 %collective-permute-done.39 = bf16[32,1024]{1,0:T(8,128)(2,1)S(1)} collective-permute-done((bf16[32,1024]{1,0:T(8,128)(2,1)S(1)}, bf16[32,1024]{1,0:T(8,128)(2,1)S(1)}, u32[]{:S(2)}, u32[]{:S(2)}) %collective-permute-start.39) | collective-permute-done | bytes 65568 | tf_op jit(solution)/shard_map/ppermute | solution.py:14
  110.9 1.6 %collective-permute-done.40 = bf16[32,1024]{1,0:T(8,128)(2,1)S(1)} collective-permute-done((bf16[32,1024]{1,0:T(8,128)(2,1)S(1)}, bf16[32,1024]{1,0:T(8,128)(2,1)S(1)}, u32[]{:S(2)}, u32[]{:S(2)}) %collective-permute-start.40) | collective-permute-done | bytes 65568 | tf_op jit(solution)/shard_map/ppermute | solution.py:14
  112.7 5.5 %collective-permute-done.41 = bf16[32,1024]{1,0:T(8,128)(2,1)S(1)} collective-permute-done((bf16[32,1024]{1,0:T(8,128)(2,1)S(1)}, bf16[32,1024]{1,0:T(8,128)(2,1)S(1)}, u32[]{:S(2)}, u32[]{:S(2)}) %collective-permute-start.41) | collective-permute-done | bytes 65568 | tf_op jit(solution)/shard_map/ppermute | solution.py:14
  118.3 1.2 collective-permute-start.43
  119.5 3.2 %collective-permute-start.44 = (bf16[32,1024]{1,0:T(8,128)(2,1)S(1)}, bf16[32,1024]{1,0:T(8,128)(2,1)S(1)}, u32[]{:S(2)}, u32[]{:S(2)}) collective-permute-start(bf16[32,1024]{1,0:T(8,128)(2,1)S(1)} %fusion.30), channel_id=1, source_target_pairs={{0,24},{4,28},{8,16},{12,20},{16,8},{20,12},{24,0},{28,4},{1,25},{... | collective-permute-start | bytes 196616 | tf_op jit(solution)/shard_map/ppermute | solution.py:14
  123.5 2.2 %collective-permute-done.44 = bf16[32,1024]{1,0:T(8,128)(2,1)S(1)} collective-permute-done((bf16[32,1024]{1,0:T(8,128)(2,1)S(1)}, bf16[32,1024]{1,0:T(8,128)(2,1)S(1)}, u32[]{:S(2)}, u32[]{:S(2)}) %collective-permute-start.44) | collective-permute-done | bytes 65568 | tf_op jit(solution)/shard_map/ppermute | solution.py:14
  126.0 1.5 %collective-permute-done.45 = bf16[128,1024]{1,0:T(8,128)(2,1)S(1)} collective-permute-done((bf16[128,1024]{1,0:T(8,128)(2,1)S(1)}, bf16[128,1024]{1,0:T(8,128)(2,1)S(1)}, u32[]{:S(2)}, u32[]{:S(2)}) %collective-permute-start.45) | collective-permute-done | bytes 262176 | tf_op jit(solution)/shard_map/ppermute | solution.py:14
  (181 shorter events, 22.0 us)
Async XLA Ops:
  0.6 34.5 %copy-start = (bf16[512,1024]{1,0:T(8,128)(2,1)S(1)}, bf16[512,1024]{1,0:T(8,128)(2,1)}, u32[]{:S(2)}) copy-start(bf16[512,1024]{1,0:T(8,128)(2,1)} %param.32) | copy-start | bytes 3145732
  0.7 11.4 %collective-permute-start = (bf16[64,512]{1,0:T(8,128)(2,1)}, bf16[64,512]{1,0:T(8,128)(2,1)S(1)}, u32[]{:S(2)}, u32[]{:S(2)}) collective-permute-start(bf16[64,512]{1,0:T(8,128)(2,1)} %param.23), channel_id=1, source_target_pairs={{0,1},{1,0},{2,3},{3,2},{4,5},{5,4},{6,7},{7,6},{8,9},{9,8},{10,11... | collective-permute-start | bytes 196616 | tf_op jit(solution)/shard_map/ppermute | solution.py:14
  3.7 8.4 %collective-permute-start.1 = (bf16[64,512]{1,0:T(8,128)(2,1)}, bf16[64,512]{1,0:T(8,128)(2,1)S(1)}, u32[]{:S(2)}, u32[]{:S(2)}) collective-permute-start(bf16[64,512]{1,0:T(8,128)(2,1)} %param.23), channel_id=1, source_target_pairs={{0,2},{1,3},{2,0},{3,1},{4,6},{5,7},{6,4},{7,5},{8,10},{9,11},{10,... | collective-permute-start | bytes 196616 | tf_op jit(solution)/shard_map/ppermute | solution.py:14
  6.1 5.9 %collective-permute-start.2 = (bf16[128,512]{1,0:T(8,128)(2,1)S(1)}, bf16[128,512]{1,0:T(8,128)(2,1)S(1)}, u32[]{:S(2)}, u32[]{:S(2)}) collective-permute-start(bf16[128,512]{1,0:T(8,128)(2,1)S(1)} %pad_maximum_fusion.5), channel_id=1, source_target_pairs={{0,3},{1,2},{2,1},{3,0},{4,7},{5,6},{6,5},{7,4},{8,11},{9,10},{10,... | collective-permute-start | bytes 393224 | tf_op jit(solution)/shard_map/ppermute | solution.py:14
  13.4 1.4 %collective-permute-start.3 = (f32[64,288]{1,0:T(8,128)S(1)}, f32[64,288]{1,0:T(8,128)S(1)}, u32[]{:S(2)}, u32[]{:S(2)}) collective-permute-start(f32[64,288]{1,0:T(8,128)S(1)} %fusion.67), channel_id=1, source_target_pairs={{0,4},{4,0},{8,12},{12,8},{16,20},{20,16},{24,28},{28,24},{1,5},{5... | collective-permute-start | bytes 221192 | tf_op jit(solution)/shard_map/ppermute | solution.py:14
  14.8 10.1 %collective-permute-start.4 = (bf16[64,288]{1,0:T(8,128)(2,1)S(1)}, bf16[64,288]{1,0:T(8,128)(2,1)S(1)}, u32[]{:S(2)}, u32[]{:S(2)}) collective-permute-start(bf16[64,288]{1,0:T(8,128)(2,1)S(1)} %convert_element_type.127), channel_id=1, source_target_pairs={{0,8},{4,12},{8,0},{12,4},{16,24},{20,28},{24,16},{28,20},{1,9},{5... | collective-permute-start | bytes 110600 | tf_op jit(solution)/shard_map/ppermute | solution.py:14
  16.5 8.5 %collective-permute-start.5 = (bf16[64,288]{1,0:T(8,128)(2,1)S(1)}, bf16[64,288]{1,0:T(8,128)(2,1)S(1)}, u32[]{:S(2)}, u32[]{:S(2)}) collective-permute-start(bf16[64,288]{1,0:T(8,128)(2,1)S(1)} %convert_element_type.127), channel_id=1, source_target_pairs={{0,16},{4,20},{8,24},{12,28},{16,0},{20,4},{24,8},{28,12},{1,17},{... | collective-permute-start | bytes 110600 | tf_op jit(solution)/shard_map/ppermute | solution.py:14
  19.1 5.9 %collective-permute-start.6 = (bf16[64,288]{1,0:T(8,128)(2,1)S(1)}, bf16[64,288]{1,0:T(8,128)(2,1)S(1)}, u32[]{:S(2)}, u32[]{:S(2)}) collective-permute-start(bf16[64,288]{1,0:T(8,128)(2,1)S(1)} %convert_element_type.127), channel_id=1, source_target_pairs={{0,24},{4,28},{8,16},{12,20},{16,8},{20,12},{24,0},{28,4},{1,25},{... | collective-permute-start | bytes 110600 | tf_op jit(solution)/shard_map/ppermute | solution.py:14
  19.3 7.2 %collective-permute-start.7 = (bf16[64,512]{1,0:T(8,128)(2,1)S(1)}, bf16[64,512]{1,0:T(8,128)(2,1)S(1)}, u32[]{:S(2)}, u32[]{:S(2)}) collective-permute-start(bf16[64,512]{1,0:T(8,128)(2,1)S(1)} %copy-done.14), channel_id=1, source_target_pairs={{0,1},{1,0},{2,3},{3,2},{4,5},{5,4},{6,7},{7,6},{8,9},{9,8},{10,11... | collective-permute-start | bytes 196616 | tf_op jit(solution)/shard_map/ppermute | solution.py:14
  19.8 6.6 %collective-permute-start.8 = (bf16[64,512]{1,0:T(8,128)(2,1)S(1)}, bf16[64,512]{1,0:T(8,128)(2,1)S(1)}, u32[]{:S(2)}, u32[]{:S(2)}) collective-permute-start(bf16[64,512]{1,0:T(8,128)(2,1)S(1)} %copy-done.14), channel_id=1, source_target_pairs={{0,2},{1,3},{2,0},{3,1},{4,6},{5,7},{6,4},{7,5},{8,10},{9,11},{10,... | collective-permute-start | bytes 196616 | tf_op jit(solution)/shard_map/ppermute | solution.py:14
  26.7 8.0 %collective-permute-start.10 = (bf16[64,512]{1,0:T(8,128)(2,1)S(1)}, bf16[64,512]{1,0:T(8,128)(2,1)S(1)}, u32[]{:S(2)}, u32[]{:S(2)}) collective-permute-start(bf16[64,512]{1,0:T(8,128)(2,1)S(1)} %fusion.27), channel_id=1, source_target_pairs={{0,2},{1,3},{2,0},{3,1},{4,6},{5,7},{6,4},{7,5},{8,10},{9,11},{10,... | collective-permute-start | bytes 196616 | tf_op jit(solution)/shard_map/ppermute | solution.py:14
  27.4 7.4 %collective-permute-start.11 = (bf16[64,512]{1,0:T(8,128)(2,1)S(1)}, bf16[64,512]{1,0:T(8,128)(2,1)S(1)}, u32[]{:S(2)}, u32[]{:S(2)}) collective-permute-start(bf16[64,512]{1,0:T(8,128)(2,1)S(1)} %fusion.27), channel_id=1, source_target_pairs={{0,3},{1,2},{2,1},{3,0},{4,7},{5,6},{6,5},{7,4},{8,11},{9,10},{10,... | collective-permute-start | bytes 196616 | tf_op jit(solution)/shard_map/ppermute | solution.py:14
  28.8 6.0 %collective-permute-start.9 = (bf16[64,512]{1,0:T(8,128)(2,1)S(1)}, bf16[64,512]{1,0:T(8,128)(2,1)S(1)}, u32[]{:S(2)}, u32[]{:S(2)}) collective-permute-start(bf16[64,512]{1,0:T(8,128)(2,1)S(1)} %fusion.27), channel_id=1, source_target_pairs={{0,1},{1,0},{2,3},{3,2},{4,5},{5,4},{6,7},{7,6},{8,9},{9,8},{10,11... | collective-permute-start | bytes 196616 | tf_op jit(solution)/shard_map/ppermute | solution.py:14
  35.5 2.2 %collective-permute-start.12 = (bf16[128,1024]{1,0:T(8,128)(2,1)S(1)}, bf16[128,1024]{1,0:T(8,128)(2,1)S(1)}, u32[]{:S(2)}, u32[]{:S(2)}) collective-permute-start(bf16[128,1024]{1,0:T(8,128)(2,1)S(1)} %convolution_convert_fusion), channel_id=1, source_target_pairs={{0,4},{4,0},{8,12},{12,8},{16,20},{20,16},{24,28},{28,24},{1,5},{5... | collective-permute-start | bytes 786440 | tf_op jit(solution)/shard_map/ppermute | solution.py:14
  35.6 22.0 %collective-permute-start.19 = (bf16[36,16,512]{2,1,0:T(8,128)(2,1)}, bf16[36,16,512]{2,1,0:T(8,128)(2,1)S(1)}, u32[]{:S(2)}, u32[]{:S(2)}) collective-permute-start(bf16[36,16,512]{2,1,0:T(8,128)(2,1)} %get-tuple-element.87), channel_id=1, source_target_pairs={{0,1},{1,0},{2,3},{3,2},{4,5},{5,4},{6,7},{7,6},{8,9},{9,8},{10,11... | collective-permute-start | bytes 1769480 | tf_op jit(solution)/shard_map/ppermute | solution.py:14
  36.2 21.5 %collective-permute-start.20 = (bf16[36,16,512]{2,1,0:T(8,128)(2,1)}, bf16[36,16,512]{2,1,0:T(8,128)(2,1)S(1)}, u32[]{:S(2)}, u32[]{:S(2)}) collective-permute-start(bf16[36,16,512]{2,1,0:T(8,128)(2,1)} %get-tuple-element.88), channel_id=1, source_target_pairs={{0,2},{1,3},{2,0},{3,1},{4,6},{5,7},{6,4},{7,5},{8,10},{9,11},{10,... | collective-permute-start | bytes 1769480 | tf_op jit(solution)/shard_map/ppermute | solution.py:14
  38.0 4.5 %collective-permute-start.13 = (bf16[32,1024]{1,0:T(8,128)(2,1)S(1)}, bf16[32,1024]{1,0:T(8,128)(2,1)S(1)}, u32[]{:S(2)}, u32[]{:S(2)}) collective-permute-start(bf16[32,1024]{1,0:T(8,128)(2,1)S(1)} %get-tuple-element.155), channel_id=1, source_target_pairs={{0,8},{4,12},{8,0},{12,4},{16,24},{20,28},{24,16},{28,20},{1,9},{5... | collective-permute-start | bytes 196616 | tf_op jit(solution)/shard_map/ppermute | solution.py:14
  38.7 8.1 %collective-permute-start.14 = (bf16[32,1024]{1,0:T(8,128)(2,1)S(1)}, bf16[32,1024]{1,0:T(8,128)(2,1)S(1)}, u32[]{:S(2)}, u32[]{:S(2)}) collective-permute-start(bf16[32,1024]{1,0:T(8,128)(2,1)S(1)} %get-tuple-element.157), channel_id=1, source_target_pairs={{0,16},{4,20},{8,24},{12,28},{16,0},{20,4},{24,8},{28,12},{1,17},{... | collective-permute-start | bytes 196616 | tf_op jit(solution)/shard_map/ppermute | solution.py:14
  42.2 6.1 %collective-permute-start.15 = (bf16[32,1024]{1,0:T(8,128)(2,1)S(1)}, bf16[32,1024]{1,0:T(8,128)(2,1)S(1)}, u32[]{:S(2)}, u32[]{:S(2)}) collective-permute-start(bf16[32,1024]{1,0:T(8,128)(2,1)S(1)} %get-tuple-element.156), channel_id=1, source_target_pairs={{0,24},{4,28},{8,16},{12,20},{16,8},{20,12},{24,0},{28,4},{1,25},{... | collective-permute-start | bytes 196616 | tf_op jit(solution)/shard_map/ppermute | solution.py:14
  49.2 4.6 %collective-permute-start.16 = (bf16[32,1024]{1,0:T(8,128)(2,1)S(1)}, bf16[32,1024]{1,0:T(8,128)(2,1)S(1)}, u32[]{:S(2)}, u32[]{:S(2)}) collective-permute-start(bf16[32,1024]{1,0:T(8,128)(2,1)S(1)} %fusion.34), channel_id=1, source_target_pairs={{0,8},{4,12},{8,0},{12,4},{16,24},{20,28},{24,16},{28,20},{1,9},{5... | collective-permute-start | bytes 196616 | tf_op jit(solution)/shard_map/ppermute | solution.py:14
  49.2 6.8 %collective-permute-start.17 = (bf16[32,1024]{1,0:T(8,128)(2,1)S(1)}, bf16[32,1024]{1,0:T(8,128)(2,1)S(1)}, u32[]{:S(2)}, u32[]{:S(2)}) collective-permute-start(bf16[32,1024]{1,0:T(8,128)(2,1)S(1)} %fusion.34), channel_id=1, source_target_pairs={{0,16},{4,20},{8,24},{12,28},{16,0},{20,4},{24,8},{28,12},{1,17},{... | collective-permute-start | bytes 196616 | tf_op jit(solution)/shard_map/ppermute | solution.py:14
  51.5 6.1 %collective-permute-start.18 = (bf16[32,1024]{1,0:T(8,128)(2,1)S(1)}, bf16[32,1024]{1,0:T(8,128)(2,1)S(1)}, u32[]{:S(2)}, u32[]{:S(2)}) collective-permute-start(bf16[32,1024]{1,0:T(8,128)(2,1)S(1)} %fusion.34), channel_id=1, source_target_pairs={{0,24},{4,28},{8,16},{12,20},{16,8},{20,12},{24,0},{28,4},{1,25},{... | collective-permute-start | bytes 196616 | tf_op jit(solution)/shard_map/ppermute | solution.py:14
  57.6 43.3 %copy-start.3 = (bf16[36,16,512]{2,1,0:T(8,128)(2,1)}, bf16[36,16,512]{2,1,0:T(8,128)(2,1)S(1)}, u32[]{:S(2)}) copy-start(bf16[36,16,512]{2,1,0:T(8,128)(2,1)S(1)} %collective-permute-done.19.refs_1_) | copy-start | bytes 1769476
  58.5 3.6 %collective-permute-start.24 = (bf16[128,1024]{1,0:T(8,128)(2,1)S(1)}, bf16[128,1024]{1,0:T(8,128)(2,1)S(1)}, u32[]{:S(2)}, u32[]{:S(2)}) collective-permute-start(bf16[128,1024]{1,0:T(8,128)(2,1)S(1)} %pad_maximum_fusion.1.refs_0_), channel_id=1, source_target_pairs={{0,4},{4,0},{8,12},{12,8},{16,20},{20,16},{24,28},{28,24},{1,5},{5... | collective-permute-start | bytes 786440 | tf_op jit(solution)/shard_map/ppermute | solution.py:14
  58.5 9.1 %collective-permute-start.21 = (bf16[128,1024]{1,0:T(8,128)(2,1)S(1)}, bf16[128,1024]{1,0:T(8,128)(2,1)S(1)}, u32[]{:S(2)}, u32[]{:S(2)}) collective-permute-start(bf16[128,1024]{1,0:T(8,128)(2,1)S(1)} %pad_maximum_fusion.1.refs_0_), channel_id=1, source_target_pairs={{0,1},{1,0},{2,3},{3,2},{4,5},{5,4},{6,7},{7,6},{8,9},{9,8},{10,11... | collective-permute-start | bytes 786440 | tf_op jit(solution)/shard_map/ppermute | solution.py:14
  59.0 14.1 %collective-permute-start.22 = (bf16[128,1024]{1,0:T(8,128)(2,1)S(1)}, bf16[128,1024]{1,0:T(8,128)(2,1)S(1)}, u32[]{:S(2)}, u32[]{:S(2)}) collective-permute-start(bf16[128,1024]{1,0:T(8,128)(2,1)S(1)} %pad_maximum_fusion.1.refs_0_), channel_id=1, source_target_pairs={{0,2},{1,3},{2,0},{3,1},{4,6},{5,7},{6,4},{7,5},{8,10},{9,11},{10,... | collective-permute-start | bytes 786440 | tf_op jit(solution)/shard_map/ppermute | solution.py:14
  60.6 12.5 %collective-permute-start.23 = (bf16[128,1024]{1,0:T(8,128)(2,1)S(1)}, bf16[128,1024]{1,0:T(8,128)(2,1)S(1)}, u32[]{:S(2)}, u32[]{:S(2)}) collective-permute-start(bf16[128,1024]{1,0:T(8,128)(2,1)S(1)} %pad_maximum_fusion.1.refs_0_), channel_id=1, source_target_pairs={{0,3},{1,2},{2,1},{3,0},{4,7},{5,6},{6,5},{7,4},{8,11},{9,10},{10,... | collective-permute-start | bytes 786440 | tf_op jit(solution)/shard_map/ppermute | solution.py:14
  73.1 2.0 %collective-permute-start.25 = (bf16[128,1024]{1,0:T(8,128)(2,1)S(1)}, bf16[128,1024]{1,0:T(8,128)(2,1)S(1)}, u32[]{:S(2)}, u32[]{:S(2)}) collective-permute-start(bf16[128,1024]{1,0:T(8,128)(2,1)S(1)} %collective-permute-done.21.refs_0_), channel_id=1, source_target_pairs={{0,4},{4,0},{8,12},{12,8},{16,20},{20,16},{24,28},{28,24},{1,5},{5... | collective-permute-start | bytes 786440 | tf_op jit(solution)/shard_map/ppermute | solution.py:14
  73.1 2.0 %collective-permute-start.26 = (bf16[128,1024]{1,0:T(8,128)(2,1)S(1)}, bf16[128,1024]{1,0:T(8,128)(2,1)S(1)}, u32[]{:S(2)}, u32[]{:S(2)}) collective-permute-start(bf16[128,1024]{1,0:T(8,128)(2,1)S(1)} %collective-permute-done.22.refs_2_), channel_id=1, source_target_pairs={{0,4},{4,0},{8,12},{12,8},{16,20},{20,16},{24,28},{28,24},{1,5},{5... | collective-permute-start | bytes 786440 | tf_op jit(solution)/shard_map/ppermute | solution.py:14
  73.6 1.8 %collective-permute-start.27 = (bf16[128,1024]{1,0:T(8,128)(2,1)S(1)}, bf16[128,1024]{1,0:T(8,128)(2,1)S(1)}, u32[]{:S(2)}, u32[]{:S(2)}) collective-permute-start(bf16[128,1024]{1,0:T(8,128)(2,1)S(1)} %collective-permute-done.23.refs_4_), channel_id=1, source_target_pairs={{0,4},{4,0},{8,12},{12,8},{16,20},{20,16},{24,28},{28,24},{1,5},{5... | collective-permute-start | bytes 786440 | tf_op jit(solution)/shard_map/ppermute | solution.py:14
  73.6 16.8 %collective-permute-start.32 = (bf16[36,16,512]{2,1,0:T(8,128)(2,1)}, bf16[36,16,512]{2,1,0:T(8,128)(2,1)S(1)}, u32[]{:S(2)}, u32[]{:S(2)}) collective-permute-start(bf16[36,16,512]{2,1,0:T(8,128)(2,1)} %get-tuple-element.110), channel_id=1, source_target_pairs={{0,3},{1,2},{2,1},{3,0},{4,7},{5,6},{6,5},{7,4},{8,11},{9,10},{10,... | collective-permute-start | bytes 1769480 | tf_op jit(solution)/shard_map/ppermute | solution.py:14
  86.9 1.8 %collective-permute-start.28 = (bf16[128,1024]{1,0:T(8,128)(2,1)}, bf16[128,1024]{1,0:T(8,128)(2,1)S(1)}, u32[]{:S(2)}, u32[]{:S(2)}) collective-permute-start(bf16[128,1024]{1,0:T(8,128)(2,1)} %get-tuple-element.106), channel_id=1, source_target_pairs={{0,4},{4,0},{8,12},{12,8},{16,20},{20,16},{24,28},{28,24},{1,5},{5... | collective-permute-start | bytes 786440 | tf_op jit(solution)/shard_map/ppermute | solution.py:14
  87.1 2.0 %collective-permute-start.29 = (bf16[128,1024]{1,0:T(8,128)(2,1)}, bf16[128,1024]{1,0:T(8,128)(2,1)S(1)}, u32[]{:S(2)}, u32[]{:S(2)}) collective-permute-start(bf16[128,1024]{1,0:T(8,128)(2,1)} %get-tuple-element.107), channel_id=1, source_target_pairs={{0,4},{4,0},{8,12},{12,8},{16,20},{20,16},{24,28},{28,24},{1,5},{5... | collective-permute-start | bytes 786440 | tf_op jit(solution)/shard_map/ppermute | solution.py:14
  87.5 2.4 %collective-permute-start.30 = (bf16[128,1024]{1,0:T(8,128)(2,1)}, bf16[128,1024]{1,0:T(8,128)(2,1)S(1)}, u32[]{:S(2)}, u32[]{:S(2)}) collective-permute-start(bf16[128,1024]{1,0:T(8,128)(2,1)} %get-tuple-element.108), channel_id=1, source_target_pairs={{0,4},{4,0},{8,12},{12,8},{16,20},{20,16},{24,28},{28,24},{1,5},{5... | collective-permute-start | bytes 786440 | tf_op jit(solution)/shard_map/ppermute | solution.py:14
  87.6 2.4 %collective-permute-start.31 = (bf16[128,1024]{1,0:T(8,128)(2,1)}, bf16[128,1024]{1,0:T(8,128)(2,1)}, u32[]{:S(2)}, u32[]{:S(2)}) collective-permute-start(bf16[128,1024]{1,0:T(8,128)(2,1)} %get-tuple-element.109), channel_id=1, source_target_pairs={{0,4},{4,0},{8,12},{12,8},{16,20},{20,16},{24,28},{28,24},{1,5},{5... | collective-permute-start | bytes 786440 | tf_op jit(solution)/shard_map/ppermute | solution.py:14
  93.1 6.3 %collective-permute-start.33 = (bf16[64,1024]{1,0:T(8,128)(2,1)}, bf16[64,1024]{1,0:T(8,128)(2,1)S(1)}, u32[]{:S(2)}, u32[]{:S(2)}) collective-permute-start(bf16[64,1024]{1,0:T(8,128)(2,1)} %get-tuple-element.115), channel_id=1, source_target_pairs={{0,1},{1,0},{2,3},{3,2},{4,5},{5,4},{6,7},{7,6},{8,9},{9,8},{10,11... | collective-permute-start | bytes 393224 | tf_op jit(solution)/shard_map/ppermute | solution.py:14
  94.7 9.9 %collective-permute-start.34 = (bf16[64,1024]{1,0:T(8,128)(2,1)}, bf16[64,1024]{1,0:T(8,128)(2,1)S(1)}, u32[]{:S(2)}, u32[]{:S(2)}) collective-permute-start(bf16[64,1024]{1,0:T(8,128)(2,1)} %get-tuple-element.120), channel_id=1, source_target_pairs={{0,2},{1,3},{2,0},{3,1},{4,6},{5,7},{6,4},{7,5},{8,10},{9,11},{10,... | collective-permute-start | bytes 393224 | tf_op jit(solution)/shard_map/ppermute | solution.py:14
  95.2 9.3 %collective-permute-start.35 = (bf16[64,1024]{1,0:T(8,128)(2,1)}, bf16[64,1024]{1,0:T(8,128)(2,1)S(1)}, u32[]{:S(2)}, u32[]{:S(2)}) collective-permute-start(bf16[64,1024]{1,0:T(8,128)(2,1)} %get-tuple-element.121), channel_id=1, source_target_pairs={{0,3},{1,2},{2,1},{3,0},{4,7},{5,6},{6,5},{7,4},{8,11},{9,10},{10,... | collective-permute-start | bytes 393224 | tf_op jit(solution)/shard_map/ppermute | solution.py:14
  97.4 15.1 %collective-permute-start.36 = (bf16[64,1024]{1,0:T(8,128)(2,1)}, bf16[64,1024]{1,0:T(8,128)(2,1)S(1)}, u32[]{:S(2)}, u32[]{:S(2)}) collective-permute-start(bf16[64,1024]{1,0:T(8,128)(2,1)} %get-tuple-element.127), channel_id=1, source_target_pairs={{0,1},{1,0},{2,3},{3,2},{4,5},{5,4},{6,7},{7,6},{8,9},{9,8},{10,11... | collective-permute-start | bytes 393224 | tf_op jit(solution)/shard_map/ppermute | solution.py:14
  98.9 13.6 %collective-permute-start.37 = (bf16[64,1024]{1,0:T(8,128)(2,1)}, bf16[64,1024]{1,0:T(8,128)(2,1)S(1)}, u32[]{:S(2)}, u32[]{:S(2)}) collective-permute-start(bf16[64,1024]{1,0:T(8,128)(2,1)} %get-tuple-element.128), channel_id=1, source_target_pairs={{0,2},{1,3},{2,0},{3,1},{4,6},{5,7},{6,4},{7,5},{8,10},{9,11},{10,... | collective-permute-start | bytes 393224 | tf_op jit(solution)/shard_map/ppermute | solution.py:14
  99.4 13.0 %collective-permute-start.38 = (bf16[64,1024]{1,0:T(8,128)(2,1)}, bf16[64,1024]{1,0:T(8,128)(2,1)S(1)}, u32[]{:S(2)}, u32[]{:S(2)}) collective-permute-start(bf16[64,1024]{1,0:T(8,128)(2,1)} %get-tuple-element.129), channel_id=1, source_target_pairs={{0,3},{1,2},{2,1},{3,0},{4,7},{5,6},{6,5},{7,4},{8,11},{9,10},{10,... | collective-permute-start | bytes 393224 | tf_op jit(solution)/shard_map/ppermute | solution.py:14
  104.9 5.9 %collective-permute-start.39 = (bf16[32,1024]{1,0:T(8,128)(2,1)S(1)}, bf16[32,1024]{1,0:T(8,128)(2,1)S(1)}, u32[]{:S(2)}, u32[]{:S(2)}) collective-permute-start(bf16[32,1024]{1,0:T(8,128)(2,1)S(1)} %get-tuple-element.162), channel_id=1, source_target_pairs={{0,16},{4,20},{8,24},{12,28},{16,0},{20,4},{24,8},{28,12},{1,17},{... | collective-permute-start | bytes 196616 | tf_op jit(solution)/shard_map/ppermute | solution.py:14
  106.4 6.1 %collective-permute-start.40 = (bf16[32,1024]{1,0:T(8,128)(2,1)S(1)}, bf16[32,1024]{1,0:T(8,128)(2,1)S(1)}, u32[]{:S(2)}, u32[]{:S(2)}) collective-permute-start(bf16[32,1024]{1,0:T(8,128)(2,1)S(1)} %get-tuple-element.161), channel_id=1, source_target_pairs={{0,24},{4,28},{8,16},{12,20},{16,8},{20,12},{24,0},{28,4},{1,25},{... | collective-permute-start | bytes 196616 | tf_op jit(solution)/shard_map/ppermute | solution.py:14
  112.6 5.6 %collective-permute-start.41 = (bf16[32,1024]{1,0:T(8,128)(2,1)S(1)}, bf16[32,1024]{1,0:T(8,128)(2,1)S(1)}, u32[]{:S(2)}, u32[]{:S(2)}) collective-permute-start(bf16[32,1024]{1,0:T(8,128)(2,1)S(1)} %unstack.53), channel_id=1, source_target_pairs={{0,8},{4,12},{8,0},{12,4},{16,24},{20,28},{24,16},{28,20},{1,9},{5... | collective-permute-start | bytes 196616 | tf_op jit(solution)/shard_map/ppermute | solution.py:14
  118.2 4.5 %collective-permute-start.42 = (bf16[32,1024]{1,0:T(8,128)(2,1)S(1)}, bf16[32,1024]{1,0:T(8,128)(2,1)S(1)}, u32[]{:S(2)}, u32[]{:S(2)}) collective-permute-start(bf16[32,1024]{1,0:T(8,128)(2,1)S(1)} %fusion.30), channel_id=1, source_target_pairs={{0,8},{4,12},{8,0},{12,4},{16,24},{20,28},{24,16},{28,20},{1,9},{5... | collective-permute-start | bytes 196616 | tf_op jit(solution)/shard_map/ppermute | solution.py:14
  118.3 5.2 %collective-permute-start.43 = (bf16[32,1024]{1,0:T(8,128)(2,1)S(1)}, bf16[32,1024]{1,0:T(8,128)(2,1)S(1)}, u32[]{:S(2)}, u32[]{:S(2)}) collective-permute-start(bf16[32,1024]{1,0:T(8,128)(2,1)S(1)} %fusion.30), channel_id=1, source_target_pairs={{0,16},{4,20},{8,24},{12,28},{16,0},{20,4},{24,8},{28,12},{1,17},{... | collective-permute-start | bytes 196616 | tf_op jit(solution)/shard_map/ppermute | solution.py:14
  119.5 6.3 %collective-permute-start.44 = (bf16[32,1024]{1,0:T(8,128)(2,1)S(1)}, bf16[32,1024]{1,0:T(8,128)(2,1)S(1)}, u32[]{:S(2)}, u32[]{:S(2)}) collective-permute-start(bf16[32,1024]{1,0:T(8,128)(2,1)S(1)} %fusion.30), channel_id=1, source_target_pairs={{0,24},{4,28},{8,16},{12,20},{16,8},{20,12},{24,0},{28,4},{1,25},{... | collective-permute-start | bytes 196616 | tf_op jit(solution)/shard_map/ppermute | solution.py:14
  125.9 1.6 %collective-permute-start.45 = (bf16[128,1024]{1,0:T(8,128)(2,1)S(1)}, bf16[128,1024]{1,0:T(8,128)(2,1)S(1)}, u32[]{:S(2)}, u32[]{:S(2)}) collective-permute-start(bf16[128,1024]{1,0:T(8,128)(2,1)S(1)} %pad_maximum_fusion.3), channel_id=1, source_target_pairs={{0,4},{4,0},{8,12},{12,8},{16,20},{20,16},{24,28},{28,24},{1,5},{5... | collective-permute-start | bytes 786440 | tf_op jit(solution)/shard_map/ppermute | solution.py:14
  (19 other events, 179.7 us)
